TPU v7x, 32 devices: a whole 2x2x4 slice. The times are simulated.
32 devices in a mesh: user: 2 (over x), item: 16 (over z, y, core).
Axes of the slice: x: 2, y: 2, z: 4, core: 2. Of those that a mesh axis runs over, the one named last changes fastest.
Arguments:
- play_counts: int32 [16, 62, 96, 512], P('item', 'user'), may hold values from 0 to 4096
- tile_owner: int32 [16, 62], P('item', 'user'), may hold values from 0 to 1, as said below
- tile_cell: int32 [16, 62], P('item', 'user'), may hold values from 0 to 31, as said below
- tile_rows: int32 [16, 62], P('item', 'user'), may hold values from 48 to 96
- tile_cols: int32 [16, 62], P('item', 'user'), may hold values from 256 to 512
- item_factors: bfloat16 [32768, 256], P('item')
Outputs:
- folded: float32 [1536, 256], P('user', 'item')
Inputs may be any that keep to these rules, and one draw needn't show every extreme that they name: `tile_owner`: for each item shard, an ingest position sends at most 16 tiles to one owner, and some owner gets exactly 16 of them. `tile_cell`: among the tiles of one item shard bound for one owner, no two share a cell.
All inputs are finite; a program needn't handle non-finite values.
Results may differ from a plain program's by a relative error of at most 0.0039.
Values may be sent and summed in bfloat16 or wider, within the bound.
No kernel may reach another device: no remote copies, remote signals or barrier semaphores. Data moves between devices by JAX's collectives and lax.ppermute only.
A program may use at most 64 MiB of HBM per device.

v0:
```python
import jax
import jax.numpy as jnp
from jax import lax
from jax.sharding import PartitionSpec as P

GROUPS = 8
CBLK = 4
ITERS = 4


EPS = 1.0
GUARD = 1e-06


def tile_weights(counts, rows, cols):
    rank_rows = lax.broadcasted_iota(jnp.int32, counts.shape, counts.ndim - 2)
    rank_cols = lax.broadcasted_iota(jnp.int32, counts.shape, counts.ndim - 1)
    inside = (rank_rows < rows[..., None, None]) & (rank_cols < cols[..., None, None])
    values = jnp.log1p(counts.astype(jnp.float32) / EPS)
    return jnp.where(inside, values, jnp.float32(0.0)).astype(jnp.bfloat16)


def shards(play_counts, tile_owner, tile_cell, tile_rows, tile_cols, item_factors):
    counts = play_counts[0]
    owners = tile_owner[0]
    cells = tile_cell[0]
    tiles_dev, tile_height, tile_width = counts.shape
    n_user = lax.axis_size("user")
    n_item = lax.axis_size("item")
    cells_all = GROUPS * CBLK
    capacity = cells_all // n_user
    weights = tile_weights(counts, tile_rows[0], tile_cols[0]).reshape(
        tiles_dev, tile_height * tile_width
    )
    onehot = (owners[:, None] == jnp.arange(n_user, dtype=jnp.int32)[None, :]).astype(jnp.int32)
    ranking = jnp.sum((jnp.cumsum(onehot, axis=0) - onehot) * onehot, axis=1)
    slots = owners * capacity + ranking
    select = slots[None, :] == jnp.arange(n_user * capacity, dtype=jnp.int32)[:, None]
    outgoing = jnp.dot(
        select.astype(jnp.bfloat16), weights, preferred_element_type=jnp.float32
    ).astype(jnp.bfloat16)
    labels = jnp.sum(jnp.where(select, (cells + 1)[None, :], 0), axis=1).astype(jnp.bfloat16)
    arrived, arrived_labels = (
        lax.all_to_all(
            outgoing.reshape(n_user, capacity, -1), "user", split_axis=0, concat_axis=0, tiled=True
        ),
        lax.all_to_all(
            labels.reshape(n_user, capacity), "user", split_axis=0, concat_axis=0, tiled=True
        ),
    )
    arrived = arrived.reshape(n_user * capacity, -1)
    arrived_labels = arrived_labels.reshape(-1)
    place = (
        arrived_labels[None, :]
        == (jnp.arange(cells_all, dtype=jnp.int32) + 1).astype(jnp.bfloat16)[:, None]
    ).astype(jnp.bfloat16)
    grid = jnp.dot(place, arrived, preferred_element_type=jnp.float32).astype(jnp.bfloat16)
    plays = (
        grid.reshape(GROUPS, CBLK, tile_height, tile_width)
        .transpose(0, 2, 1, 3)
        .reshape(GROUPS * tile_height, CBLK * tile_width)
    )
    confidence = 1.0 + plays.astype(jnp.float32)
    observed = plays > 0
    weighted = jnp.where(observed, confidence, jnp.float32(0.0)).astype(jnp.bfloat16)
    seen = lax.psum(jnp.sum(observed.astype(jnp.float32), axis=1), "item")
    reg = seen / float(item_factors.shape[0] * n_item)
    rank = item_factors.shape[1]
    share_rows = rank // n_item

    def summed(matrix):
        return lax.psum(jnp.dot(matrix, item_factors, preferred_element_type=jnp.float32), "item")

    rhs = summed(weighted)
    folded = jnp.zeros_like(rhs)
    residual = rhs
    direction = rhs
    norm_now = jnp.sum(residual * residual, axis=1)
    for number in range(ITERS):
        projected = lax.dot_general(
            direction.astype(jnp.bfloat16),
            item_factors,
            (((1,), (1,)), ((), ())),
            preferred_element_type=jnp.float32,
        )
        scaled = (confidence * projected).astype(jnp.bfloat16)
        image = summed(scaled) + reg[:, None] * direction
        alpha = norm_now / (jnp.sum(direction * image, axis=1) + GUARD)
        folded = folded + alpha[:, None] * direction
        residual = residual - alpha[:, None] * image
        fresh = jnp.sum(residual * residual, axis=1)
        direction = residual + (fresh / (norm_now + GUARD))[:, None] * direction
        norm_now = fresh
    return lax.dynamic_slice_in_dim(folded, lax.axis_index("item") * share_rows, share_rows, 1)


def solution(mesh):
    placed = (
        P("item", "user", None, None),
        P("item", "user"),
        P("item", "user"),
        P("item", "user"),
        P("item", "user"),
        P("item", None),
    )
    return jax.shard_map(
        shards, mesh=mesh, in_specs=placed, out_specs=P("user", "item"), check_vma=False
    )
```

profile of v0, /device:TPU:0, one launch (start us, length us, event | category | flops | bytes accessed | tf_op | source)
XLA Modules:
  0.0 592.6 jit_solution(11047977744021487436)
XLA Ops:
  6.5 0.8 fusion.22
  7.4 0.1 reduce_window_sum.11
  7.4 0.8 select_reduce_fusion.1
  8.2 0.7 fusion.27
  8.9 0.1 select_reduce_fusion
  9.0 0.7 convert_element_type.99
  9.7 4.2 all-to-all-start
  13.9 4.8 log-plus-one_bitcast_fusion
  18.7 0.4 pad
  19.2 0.0 copy-start.7
  19.2 0.0 copy-start.8
  19.2 1.8 copy.25
  21.0 0.1 copy.23
  21.1 0.1 copy.24
  21.1 3.0 convolution_convert_fusion.1
  24.2 0.0 all-to-all-done
  24.2 5.2 all-to-all-start.1
  29.4 0.2 all-reduce.6.cloned.1.call-start
  29.6 0.1 eq.53
  29.7 36.3 %all-to-all-done.1 = bf16[2,16,49152]{2,1,0:T(8,128)(2,1)} async-done(((bf16[2,16,49152]{2,1,0:T(8,128)(2,1)}), bf16[2,16,49152]{2,1,0:T(8,128)(2,1)}, u32[]{:S(2)}, u32[]{:S(2)}) %all-to-all-start.1) | async-done | bytes 3145760 | tf_op jit(solution)/shard_map/all_to_all | solution.py:44
  66.0 2.9 convert_add_fusion
  68.9 3.6 copy.28
  72.6 4.0 copy.21
  76.6 3.2 copy.29
  79.9 0.8 broadcast_compare_fusion
  80.7 1.0 copy.26
  81.7 2.0 copy.20
  83.7 0.9 copy.27
  84.6 2.0 fusion
  86.6 0.0 all-reduce.6.cloned.1.call-update
  86.6 0.0 all-reduce.8.cloned.1.call-start
  86.6 92.7 %all-reduce.6.cloned.1.call-done = f32[768,256]{1,0:T(8,128)} async-done(((f32[768,256]{1,0:T(8,128)}), f32[768,256]{1,0:T(8,128)}) %all-reduce.6.cloned.1.call-update) | async-done | bytes 786448 | tf_op jit(solution)/shard_map/psum | solution.py:72
  179.3 6.0 %fusion.7 = f32[768,256]{1,0:T(8,128)} fusion(bf16[2048,256]{1,0:T(8,128)(2,1)S(1)} %copy-done, f32[768,2048]{1,0:T(8,128)} %bitcast.49, f32[768,256]{1,0:T(8,128)} %all-reduce.6.cloned.1.call-done), kind=kOutput, calls=%fused_computation.19 | convolution fusion | flops 1613955072 | bytes 8912896 | tf_op jit(solution)/shard_map/dot_general | solution.py:72
  185.3 0.0 all-reduce.8.cloned.1.call-update
  185.3 0.0 all-reduce.10.cloned.1.call-start
  185.4 0.7 convert_reduce_fusion
  186.1 0.1 reduce_sum.108
  186.2 30.5 %psum.44 = f32[768]{0:T(1024)S(1)} all-reduce(f32[768]{0:T(1024)S(1)} %reduce_sum.108), channel_id=1, replica_groups=mesh['user'=2,'item'=16] {'item'}, use_global_device_ids=true, to_apply=%region_7.8 | all-reduce | flops 768 | bytes 6144 | tf_op jit(solution)/shard_map/psum | solution.py:66
  216.7 59.8 %all-reduce.8.cloned.1.call-done = f32[768,256]{1,0:T(8,128)} async-done(((f32[768,256]{1,0:T(8,128)}), f32[768,256]{1,0:T(8,128)}) %all-reduce.8.cloned.1.call-update) | async-done | bytes 786448 | tf_op jit(solution)/shard_map/psum | solution.py:72
  276.5 0.0 copy-done.2
  276.5 1.6 multiply_reduce_fusion.6
  278.1 1.5 multiply_reduce_fusion.5
  279.6 0.4 multiply_add_fusion.4
  280.0 5.6 fusion.8
  285.6 0.0 all-reduce.10.cloned.1.call-update
  285.6 0.3 all-reduce.12.cloned.1.call-start
  285.9 90.9 %all-reduce.10.cloned.1.call-done = f32[768,256]{1,0:T(8,128)} async-done(((f32[768,256]{1,0:T(8,128)}), f32[768,256]{1,0:T(8,128)}) %all-reduce.10.cloned.1.call-update) | async-done | bytes 786448 | tf_op jit(solution)/shard_map/psum | solution.py:72
  376.8 1.4 multiply_reduce_fusion.4
  378.3 1.6 multiply_reduce_fusion.3
  379.9 0.9 copy-done.4
  380.8 0.2 multiply_add_fusion.2
  381.0 5.7 fusion.9
  386.6 0.0 all-reduce.12.cloned.1.call-update
  386.7 0.0 all-reduce.14.cloned.1.call-start
  386.7 91.1 %all-reduce.12.cloned.1.call-done = f32[768,256]{1,0:T(8,128)} async-done(((f32[768,256]{1,0:T(8,128)}), f32[768,256]{1,0:T(8,128)}) %all-reduce.12.cloned.1.call-update) | async-done | bytes 786448 | tf_op jit(solution)/shard_map/psum | solution.py:72
  477.8 1.5 multiply_reduce_fusion.2
  479.4 1.8 multiply_reduce_fusion.1
  481.2 1.3 multiply_add_fusion
  482.5 5.9 fusion.10
  488.3 0.0 all-reduce.14.cloned.1.call-update
  488.4 91.2 %all-reduce.14.cloned.1.call-done = f32[768,256]{1,0:T(8,128)} async-done(((f32[768,256]{1,0:T(8,128)}), f32[768,256]{1,0:T(8,128)}) %all-reduce.14.cloned.1.call-update) | async-done | bytes 786448 | tf_op jit(solution)/shard_map/psum | solution.py:72
  579.6 1.7 multiply_reduce_fusion
  581.2 2.6 fusion.11
  583.9 1.8 copy.22
  (27 shorter events, 0.1 us)
Async XLA Ops:
  6.5 78.1 %copy-start = (bf16[2048,256]{1,0:T(8,128)(2,1)S(1)}, bf16[2048,256]{1,0:T(8,128)(2,1)}, u32[]{:S(2)}) copy-start(bf16[2048,256]{1,0:T(8,128)(2,1)} %param.11) | copy-start | bytes 3145732
  9.7 14.5 %all-to-all-start = ((bf16[2,1,16]{2,1,0:T(2,128)(2,1)}), bf16[2,1,16]{2,1,0:T(2,128)(2,1)S(1)}, u32[]{:S(2)}, u32[]{:S(2)}) async-start(bf16[2,1,16]{2,1,0:T(2,128)(2,1)} %convert_element_type.99), calls=%async_computation | async-start | bytes 2048 | tf_op jit(solution)/shard_map/all_to_all | solution.py:47
  19.2 1.9 copy-start.7
  19.2 1.9 copy-start.8
  24.2 41.8 %all-to-all-start.1 = ((bf16[2,16,49152]{2,1,0:T(8,128)(2,1)}), bf16[2,16,49152]{2,1,0:T(8,128)(2,1)}, u32[]{:S(2)}, u32[]{:S(2)}) async-start(bf16[2,16,49152]{2,1,0:T(8,128)(2,1)} %bitcast.61), calls=%async_computation.1 | async-start | bytes 6291456 | tf_op jit(solution)/shard_map/all_to_all | solution.py:44
  29.4 149.9 %all-reduce.6.cloned.1.call-start = ((), (), s32[]{:S(2)}) async-start(), calls=%async_computation.2 | async-start | bytes 1572864 | tf_op jit(solution)/shard_map/psum | solution.py:72
  79.9 4.7 copy-start.1
  86.6 189.9 %all-reduce.8.cloned.1.call-start = ((), (), s32[]{:S(2)}) async-start(), calls=%async_computation.3 | async-start | bytes 1572864 | tf_op jit(solution)/shard_map/psum | solution.py:72
  179.3 97.1 %copy-start.2 = (f32[768,256]{1,0:T(8,128)S(1)}, f32[768,256]{1,0:T(8,128)}, u32[]{:S(2)}) copy-start(f32[768,256]{1,0:T(8,128)} %all-reduce.6.cloned.1.call-done) | copy-start | bytes 2359300
  185.3 191.5 %all-reduce.10.cloned.1.call-start = ((), (), s32[]{:S(2)}) async-start(), calls=%async_computation.4 | async-start | bytes 1572864 | tf_op jit(solution)/shard_map/psum | solution.py:72
  276.5 3.2 copy-start.3
  285.6 192.2 %all-reduce.12.cloned.1.call-start = ((), (), s32[]{:S(2)}) async-start(), calls=%async_computation.5 | async-start | bytes 1572864 | tf_op jit(solution)/shard_map/psum | solution.py:72
  379.9 0.9 copy-start.4
  386.7 192.9 %all-reduce.14.cloned.1.call-start = ((), (), s32[]{:S(2)}) async-start(), calls=%async_computation.6 | async-start | bytes 1572864 | tf_op jit(solution)/shard_map/psum | solution.py:72
  477.8 3.4 copy-start.5
  477.8 3.4 copy-start.6
Sparse Core Ops, SparseCore 0:
  86.7 92.5 all-reduce.5
  185.5 90.9 all-reduce.7
  285.8 91.0 all-reduce.9
  386.8 91.0 all-reduce.11
  488.5 91.0 all-reduce.13
where the time goes:
time: 598 us; the launch traced here: 593 us
  waiting for transfers between devices  462 us (77%)
  matrix products  31 us (5%)
  blocking collectives  30.5 us (5%)
  other arithmetic  24.5 us (4%)
  local copies, waits for them, and re-layouts  20.6 us (3%)
  between operations  13.9 us (2%)
  starting transfers between devices  10 us (2%)
    psum x5, waiting for transfers between devices, summed(): lax.psum(jnp.dot(matrix, item_factors, preferred_element_type=jnp.float32...  426 us
    all_to_all x1, waiting for transfers between devices, shards(): lax.all_to_all(outgoing.reshape(n_user, capacity, -1), 'user', split_axis...  36.3 us
    psum x1, blocking collectives, shards(): seen = lax.psum(jnp.sum(observed.astype(jnp.float32), axis=1), 'item')  30.5 us
    dot_general x5, matrix products, summed(): jnp.dot(matrix, item_factors, preferred_element_type=jnp.float32)  25.1 us
    unnamed x28, local copies, waits for them, and re-layouts  12 us
  transfers between devices with their start and end apart: 7, of which 6 were waited for; matrix products, arithmetic and copies ran while one was open for 2% of the time, Pallas kernels for 0%

commit v1 on v0

v1 whole, which is shorter than its diff:
```python
import functools

import jax
import jax.numpy as jnp
from jax import lax
from jax.experimental import pallas as pl
from jax.experimental.pallas import tpu as pltpu
from jax.sharding import PartitionSpec as P

GROUPS = 8
CBLK = 4
ITERS = 4

EPS = 1.0
GUARD = 1e-06

HALVES = 2
HG = GROUPS // HALVES

BF16 = jnp.bfloat16
F32 = jnp.float32
VMEM = pl.BlockSpec(memory_space=pltpu.VMEM)
SMEM = pl.BlockSpec(memory_space=pltpu.SMEM)
ANY = pl.BlockSpec(memory_space=pl.ANY)


def log_tile(counts, rows, cols):
    rank_rows = lax.broadcasted_iota(jnp.int32, counts.shape, 0)
    rank_cols = lax.broadcasted_iota(jnp.int32, counts.shape, 1)
    inside = (rank_rows < rows) & (rank_cols < cols)
    values = jnp.log(1.0 + counts.astype(F32) / EPS)
    return jnp.where(inside, values, 0.0).astype(BF16)


def start_tiles(n_user, cap, own, at, owner, cell, counts, label, slots, fill, buf, sems):
    total = label.shape[0]
    for s in range(total):
        label[s] = -1
        slots[s] = -1
    for s in range(n_user):
        fill[s] = 0

    def visit(t, carry):
        shift = lax.rem(owner[t] - at[0] + n_user, n_user)

        @pl.when((shift == 0) if own else (shift != 0))
        def _():
            base = 0 if own else shift - 1
            k = fill[base]
            slot = base * cap + k
            fill[base] = k + 1
            slots[slot] = t
            label[slot] = cell[t]
            pltpu.make_async_copy(counts.at[t], buf.at[slot], sems.at[slot]).start()

        return carry

    lax.fori_loop(0, counts.shape[0], visit, 0)


def pack_kernel(n_user, cap, at, owner, cell, rows, cols, counts, tiles, label, slots, fill, buf, sems):
    start_tiles(n_user, cap, False, at, owner, cell, counts, label, slots, fill, buf, sems)

    def work(s, carry):
        t = slots[s]

        @pl.when(t >= 0)
        def _():
            pltpu.make_async_copy(counts.at[t], buf.at[s], sems.at[s]).wait()
            tiles[s] = log_tile(buf[s], rows[t], cols[t])

        return carry

    lax.fori_loop(0, tiles.shape[0], work, 0)


def rhs_kernel(
    n_user, cap, at, owner, cell, rows, cols, out_label, counts, out_tiles, factors,
    keep, send, tiles, label, slots, fill, buf, obuf, dense, sems, osem,
):
    start_tiles(n_user, cap, True, at, owner, cell, counts, label, slots, fill, buf, sems)
    moved = pltpu.make_async_copy(out_tiles, obuf, osem)
    moved.start()
    height, width = counts.shape[1], counts.shape[2]
    half = HG * height
    dense[...] = jnp.zeros_like(dense)

    def put(tile, shift, where):
        group, block = where // CBLK, where % CBLK
        side = jnp.where(group // HG == at[1], 0, 1)
        row = side * (n_user * half) + shift * half + (group % HG) * height
        value = tile.astype(F32)
        weighted = jnp.where(value > 0, 1.0 + value, 0.0).astype(BF16)
        dense[pl.ds(pl.multiple_of(row, 16), height), pl.ds(pl.multiple_of(block * width, 128), width)] = weighted

    moved.wait()

    def work_out(s, carry):
        @pl.when(out_label[s] >= 0)
        def _():
            put(obuf[s], s // cap + 1, out_label[s])

        return carry

    lax.fori_loop(0, out_label.shape[0], work_out, 0)

    def work_own(s, carry):
        t = slots[s]

        @pl.when(t >= 0)
        def _():
            pltpu.make_async_copy(counts.at[t], buf.at[s], sems.at[s]).wait()
            tile = log_tile(buf[s], rows[t], cols[t])
            tiles[s] = tile
            put(tile, 0, label[s])

        return carry

    lax.fori_loop(0, cap, work_own, 0)

    def dots(s, carry):
        row = pl.multiple_of(s * half, 16)
        send[pl.ds(row, half), :] = jnp.dot(
            dense[pl.ds(pl.multiple_of((n_user + s) * half, 16), half), :], factors[...], preferred_element_type=F32
        )
        keep[pl.ds(row, half), :] = jnp.dot(dense[pl.ds(row, half), :], factors[...], preferred_element_type=F32)
        return carry

    lax.fori_loop(0, n_user, dots, 0)


def scaled_block(direction, factors, plays):
    projected = lax.dot_general(direction, factors, (((1,), (1,)), ((), ())), preferred_element_type=F32)
    confidence = 1.0 + plays
    return projected, (confidence * projected).astype(BF16)


def lanes(x):
    return sum(x[:, k * 128 : (k + 1) * 128] for k in range(x.shape[1] // 128))


def first_kernel(
    cap, n_items, table, direction, own, far, pair_own, pair_far, factors,
    image, plays, reg, fbuf, seen, acc, sems, fsems,
):
    blocks, half, width = plays.shape
    height = half // HG

    def each(j, act_copy, act_none):
        for g in range(HG):
            code = table[(j // CBLK) * (HG * CBLK) + g * CBLK + j % CBLK]
            near, other = (own, far) if j < CBLK else (pair_own, pair_far)
            target = plays.at[j, g * height : (g + 1) * height, :]
            sem = sems.at[j * HG + g]

            @pl.when((code >= 0) & (code < cap))
            def _(code=code, near=near, target=target, sem=sem):
                act_copy(pltpu.make_async_copy(near.at[code], target, sem))

            @pl.when(code >= cap)
            def _(code=code, other=other, target=target, sem=sem):
                act_copy(pltpu.make_async_copy(other.at[code - cap], target, sem))

            if act_none:

                @pl.when(code < 0)
                def _(target=target):
                    target[...] = jnp.zeros(target.shape, target.dtype)

    def fcopy(j):
        rows = pl.ds(j * width, width)
        return pltpu.make_async_copy(factors.at[rows], fbuf.at[rows], fsems.at[j])

    for j in range(blocks):
        fcopy(j).start()
        each(j, lambda c: c.start(), True)
    for j in range(blocks):
        fcopy(j).wait()
        each(j, lambda c: c.wait(), False)
        block = fbuf[j * width : (j + 1) * width, :]
        value = plays[j].astype(F32)
        _, scaled = scaled_block(direction[...], block, value)
        part = jnp.dot(scaled, block, preferred_element_type=F32)
        count = lanes(jnp.where(value > 0, 1.0, 0.0))
        if j == 0:
            acc[...] = part
            seen[...] = count
        else:
            acc[...] += part
            seen[...] += count
    share = jnp.sum(seen[...], axis=1, keepdims=True) / n_items
    reg[...] = jnp.broadcast_to(share, reg.shape)
    image[...] = (acc[...] + share * direction[...].astype(F32)).astype(BF16)


def load_blocks(plays, factors, pbuf, fbuf, sems, fsems):
    blocks, _, width = pbuf.shape

    def pcopy(j):
        return pltpu.make_async_copy(plays.at[j], pbuf.at[j], sems.at[j])

    def fcopy(j):
        rows = pl.ds(j * width, width)
        return pltpu.make_async_copy(factors.at[rows], fbuf.at[rows], fsems.at[j])

    for j in range(blocks):
        fcopy(j).start()
        pcopy(j).start()

    def get(j):
        fcopy(j).wait()
        pcopy(j).wait()
        return pbuf[j].astype(F32), fbuf[j * width : (j + 1) * width, :]

    return get


def mid_kernel(direction, reg, plays, factors, image, pbuf, fbuf, acc, sems, fsems):
    get = load_blocks(plays, factors, pbuf, fbuf, sems, fsems)
    for j in range(pbuf.shape[0]):
        value, block = get(j)
        _, scaled = scaled_block(direction[...], block, value)
        part = jnp.dot(scaled, block, preferred_element_type=F32)
        if j == 0:
            acc[...] = part
        else:
            acc[...] += part
    image[...] = (acc[...] + reg[:, :1] * direction[...].astype(F32)).astype(BF16)


def last_kernel(direction, reg, base, plays, factors, payload, pbuf, fbuf, acc, sems, fsems):
    get = load_blocks(plays, factors, pbuf, fbuf, sems, fsems)
    for j in range(pbuf.shape[0]):
        value, block = get(j)
        projected, scaled = scaled_block(direction[...], block, value)
        part = lanes(scaled.astype(F32) * projected)
        if j == 0:
            acc[...] = part
        else:
            acc[...] += part
    wide = direction[...].astype(F32)
    along = acc[...] + reg[:, :1] * lanes(wide * wide)
    along = jnp.broadcast_to(jnp.sum(along, axis=1, keepdims=True), acc.shape)
    groups = acc.shape[0] // 8
    first = 128 - payload_lanes(base.shape[0], groups)
    lane = lax.broadcasted_iota(jnp.int32, (8, 128), 1)
    for tile in range(2):
        laid = jnp.zeros((8, 128), F32)
        for g in range(groups):
            if (g >= 128 - first) == tile:
                laid = jnp.where(lane == first + g - tile * (128 - first), along[g * 8 : (g + 1) * 8, :], laid)
        for i in range(base.shape[0]):
            payload[i, tile * 8 : (tile + 1) * 8, :] = base[i, tile * 8 : (tile + 1) * 8, :] + laid


def payload_lanes(n_item, groups):
    return 128 - (groups // (n_item // HALVES)) * (256 // n_item)


def base_kernel(folded, direction, residual, base):
    n_item = base.shape[0]
    rows, rank = folded.shape
    share = rank // n_item
    pieces = rows // 8
    base[...] = jnp.zeros_like(base)
    norm = jnp.sum(residual[...] * residual[...], axis=1, keepdims=True)
    for s in range(pieces):
        at = slice(s * 8, (s + 1) * 8)
        for i in range(n_item):
            base[i, 0:8, s * share : (s + 1) * share] = folded[at, i * share : (i + 1) * share]
            base[i, 8:16, s * share : (s + 1) * share] = direction[at, i * share : (i + 1) * share]
        for i in range(n_item):
            base[i, 8:16, 112 + s : 113 + s] = norm[at, :]


def final_kernel(got, out):
    n_item = got.shape[0]
    n_chunk = n_item // HALVES
    share = out.shape[1]
    half = out.shape[0] // HALVES
    pieces = half // n_chunk // 8
    first = pieces * share
    for h in range(HALVES):
        sums = [sum(got[k * HALVES + h, t * 8 : (t + 1) * 8, :] for k in range(n_chunk)) for t in range(2)]
        for k in range(n_chunk):
            src = k * HALVES + h
            for s in range(pieces):
                g = k * pieces + s
                lane = first + g % (128 - first)
                along = sums[g // (128 - first)][:, lane : lane + 1]
                alpha = got[src, 8:16, 112 + s : 113 + s] / (along + GUARD)
                row = h * half + g * 8
                at = slice(s * share, (s + 1) * share)
                out[row : row + 8, :] = got[src, 0:8, at] + alpha * got[src, 8:16, at]


def vector_kernel(got, direction, residual, folded, direction_out, residual_out, folded_out, spread):
    image = sum(got[k].astype(F32) for k in range(got.shape[0]))
    d, r = direction[...], residual[...]
    norm = jnp.sum(r * r, axis=1, keepdims=True)
    alpha = norm / (jnp.sum(d * image, axis=1, keepdims=True) + GUARD)
    folded_out[...] = folded[...] + alpha * d
    r = r - alpha * image
    fresh = jnp.sum(r * r, axis=1, keepdims=True)
    d = r + fresh / (norm + GUARD) * d
    residual_out[...] = r
    direction_out[...] = d
    low = d.astype(BF16)
    for k in range(spread.shape[0]):
        spread[k] = low


def shards(play_counts, tile_owner, tile_cell, tile_rows, tile_cols, item_factors):
    counts = play_counts[0]
    tiles_dev, height, width = counts.shape
    n_user = lax.axis_size("user")
    n_item = lax.axis_size("item")
    shard_items, rank = item_factors.shape
    cap = GROUPS * CBLK // n_user
    n_out = (n_user - 1) * cap
    n_chunk = n_item // HALVES
    half = HG * height
    chunk = half // n_chunk
    n_items = float(shard_items * n_item)
    blocks = HALVES * CBLK

    user = lax.axis_index("user")
    core = lax.rem(lax.axis_index("item"), HALVES)
    at = jnp.stack([user, core]).astype(jnp.int32)
    pair = [(i, i ^ 1) for i in range(n_item)]
    groups = [[h + HALVES * k for k in range(n_chunk)] for h in range(HALVES)]

    def call(kernel, ins, outs, scratch, flops=0, nbytes=0):
        return pl.pallas_call(
            kernel,
            out_shape=[o[0] for o in outs],
            in_specs=ins,
            out_specs=[o[1] for o in outs],
            scratch_shapes=scratch,
            compiler_params=pltpu.CompilerParams(vmem_limit_bytes=56 * 2**20),
            cost_estimate=pl.CostEstimate(flops=flops, bytes_accessed=nbytes, transcendentals=0),
        )

    def shape(dims, dtype):
        return jax.ShapeDtypeStruct(dims, dtype)

    def over_users(x, shift):
        return lax.ppermute(x, "user", [(u, (u + shift) % n_user) for u in range(n_user)])

    def exchange(x):
        return lax.all_to_all(x, "item", 0, 0, axis_index_groups=groups, tiled=True)

    route = (at, tile_owner[0], tile_cell[0], tile_rows[0], tile_cols[0])
    dma = pltpu.SemaphoreType.DMA
    out_tiles, out_label = call(
        functools.partial(pack_kernel, n_user, cap),
        [SMEM] * 5 + [ANY],
        [(shape((n_out, height, width), BF16), VMEM), (shape((n_out,), jnp.int32), SMEM)],
        [
            pltpu.SMEM((n_out,), jnp.int32),
            pltpu.SMEM((n_user,), jnp.int32),
            pltpu.VMEM((n_out, height, width), jnp.int32),
            dma((n_out,)),
        ],
        nbytes=n_out * height * width * 6,
    )(*route, counts)
    far, far_label = [], []
    for s in range(1, n_user):
        far.append(over_users(out_tiles[(s - 1) * cap : s * cap], s))
        far_label.append(over_users(out_label[(s - 1) * cap : s * cap], s))
    far = jnp.concatenate(far) if n_user > 2 else far[0]
    far_label = jnp.concatenate(far_label) if n_user > 2 else far_label[0]

    keep, send, own, own_label = call(
        functools.partial(rhs_kernel, n_user, cap),
        [SMEM] * 6 + [ANY, ANY, VMEM],
        [
            (shape((n_user * half, rank), F32), VMEM),
            (shape((n_user * half, rank), F32), VMEM),
            (shape((cap, height, width), BF16), VMEM),
            (shape((cap,), jnp.int32), SMEM),
        ],
        [
            pltpu.SMEM((cap,), jnp.int32),
            pltpu.SMEM((n_user,), jnp.int32),
            pltpu.VMEM((cap, height, width), jnp.int32),
            pltpu.VMEM((n_out, height, width), BF16),
            pltpu.VMEM((HALVES * n_user * half, shard_items), BF16),
            dma((cap,)),
            dma(()),
        ],
        flops=2 * HALVES * n_user * half * shard_items * rank,
        nbytes=2 * tiles_dev * height * width * 4,
    )(*route, out_label, counts, out_tiles, item_factors)

    partial_rhs = (keep + lax.ppermute(send, "item", pair)).astype(BF16)
    partial_rhs = partial_rhs.reshape(n_user, n_chunk, chunk, rank).transpose(1, 0, 2, 3)
    summed = exchange(partial_rhs.reshape(n_chunk, n_user * chunk, rank))
    summed = jnp.sum(summed.astype(F32), axis=0).reshape(n_user, chunk, rank)
    rhs = summed[0]
    for s in range(1, n_user):
        rhs = rhs + over_users(summed[s], s)
    folded = jnp.zeros_like(rhs)
    residual = rhs
    direction = rhs
    spread = jnp.broadcast_to(rhs.astype(BF16)[None], (n_chunk, chunk, rank))

    factors = jnp.concatenate([item_factors, lax.ppermute(item_factors, "item", pair)])
    labels = jnp.concatenate([own_label, far_label])
    pair_own = lax.ppermute(own, "item", pair)
    pair_far = lax.ppermute(far, "item", pair)
    pair_labels = lax.ppermute(labels, "item", pair)
    cells = core * (HG * CBLK) + jnp.arange(HG * CBLK, dtype=jnp.int32)
    code = jnp.arange(1, n_user * cap + 1, dtype=jnp.int32)
    both = jnp.stack([labels, pair_labels])
    table = jnp.sum(jnp.where(both[:, None, :] == cells[None, :, None], code, 0), axis=2) - 1
    table = table.reshape(-1)

    block_flops = 4 * half * blocks * width * rank
    block_bytes = blocks * width * (half + rank) * 2
    plays_shape = (blocks, half, width)
    for number in range(ITERS):
        whole = exchange(spread).reshape(half, rank)
        if number == 0:
            image, plays, reg = call(
                functools.partial(first_kernel, cap, n_items),
                [SMEM, VMEM] + [ANY] * 5,
                [
                    (shape((half, rank), BF16), VMEM),
                    (shape(plays_shape, BF16), VMEM),
                    (shape((half, 128), F32), VMEM),
                ],
                [
                    pltpu.VMEM((blocks * width, rank), BF16),
                    pltpu.VMEM((half, 128), F32),
                    pltpu.VMEM((half, rank), F32),
                    dma((blocks * HG,)),
                    dma((blocks,)),
                ],
                flops=block_flops,
                nbytes=2 * block_bytes,
            )(table, whole, own, far, pair_own, pair_far, factors)
        else:
            last = number == ITERS - 1
            scratch = [
                pltpu.VMEM(plays_shape, BF16),
                pltpu.VMEM((blocks * width, rank), BF16),
                pltpu.VMEM((half, 128 if last else rank), F32),
                dma((blocks,)),
                dma((blocks,)),
            ]
            if last:
                break
            (image,) = call(
                mid_kernel,
                [VMEM, VMEM, ANY, ANY],
                [(shape((half, rank), BF16), VMEM)],
                scratch,
                flops=block_flops,
                nbytes=block_bytes,
            )(whole, reg, plays, factors)
        got = exchange(image.reshape(n_chunk, chunk, rank))
        direction, residual, folded, spread = call(
            vector_kernel,
            [VMEM] * 4,
            [(shape((chunk, rank), F32), VMEM)] * 3 + [(shape((n_chunk, chunk, rank), BF16), VMEM)],
            [],
        )(got, direction, residual, folded)

    (base,) = call(
        base_kernel,
        [VMEM] * 3,
        [(shape((n_item, 16, 128), F32), VMEM)],
        [],
    )(folded, direction, residual)
    (payload,) = call(
        last_kernel,
        [VMEM] * 3 + [ANY] * 2,
        [(shape((n_item, 16, 128), F32), VMEM)],
        scratch,
        flops=block_flops // 2,
        nbytes=block_bytes,
    )(whole, reg, base, plays, factors)
    got = lax.all_to_all(payload, "item", 0, 0, tiled=True)
    (out,) = call(
        final_kernel,
        [VMEM],
        [(shape((HALVES * half, rank // n_item), F32), VMEM)],
        [],
    )(got)
    return out


def solution(mesh):
    placed = (
        P("item", "user", None, None),
        P("item", "user"),
        P("item", "user"),
        P("item", "user"),
        P("item", "user"),
        P("item", None),
    )
    return jax.shard_map(
        shards, mesh=mesh, in_specs=placed, out_specs=P("user", "item"), check_vma=False
    )
```

time: 598 us -> 186 us (0.31)
  waiting for transfers between devices: 462 us -> 31.5 us
  Pallas kernels: 0 us -> 49.3 us
  blocking collectives: 30.5 us -> 71.1 us
  matrix products: 31 us -> 0 us
  other arithmetic: 24.5 us -> 4.28 us
  between operations: 13.9 us -> 0.19 us
  local copies, waits for them, and re-layouts: 20.6 us -> 7.2 us
  starting transfers between devices: 10 us -> 21.4 us
    psum x5 -> x0, waiting for transfers between devices: 426 us -> none  [summed(): lax.psum(jnp.dot(matrix, item_factors, preferred_element_type=jnp.float32...]
    all_to_all x0 -> x6, blocking collectives: none -> 71.1 us  [the longest x5 59 us: exchange(): return lax.all_to_all(x, 'item', 0, 0, axis_index_groups=groups, tiled=True)]
    pallas_call x0 -> x11, Pallas kernels: none -> 49.3 us  [the longest x2 12.4 us: shards(): call(mid_kernel, [VMEM, VMEM, ANY, ANY], [(shape((half, rank), BF16), VME...]
    dot_general x7 -> x0, matrix products: 31 us -> none  [the longest x5 25.1 us: summed(): jnp.dot(matrix, item_factors, preferred_element_type=jnp.float32)]
    psum x1 -> x0, blocking collectives: 30.5 us -> none  [shards(): seen = lax.psum(jnp.sum(observed.astype(jnp.float32), axis=1), 'item')]
    all_to_all x2 -> x3, waiting for transfers between devices: 36.3 us -> 11.8 us  [exchange(): return lax.all_to_all(x, 'item', 0, 0, axis_index_groups=groups, tiled=True)]
    ppermute x0 -> x8, waiting for transfers between devices: none -> 19.7 us  [the longest x3 16.6 us: over_users(): lax.ppermute(x, 'user', [(u, (u + shift) % n_user) for u in range(n_user)])]
    reduce_sum x10 -> x2, other arithmetic: 12.8 us -> 0.24 us  [the longest x1 0.18 us: shards(): jnp.sum(jnp.where(both[:, None, :] == cells[None, :, None], code, 0), axi...]
  transfers between devices with their start and end apart: 7 -> 11, of which waited for: 6 -> 6; matrix products, arithmetic and copies ran while one was open for 2% -> 4% of each run, Pallas kernels for 0% -> 6%
where the time goes in v1:
time: 186 us; the launch traced here: 185 us
  blocking collectives  71.1 us (38%)
  Pallas kernels  49.3 us (27%)
  waiting for transfers between devices  31.5 us (17%)
  starting transfers between devices  21.4 us (12%)
  local copies, waits for them, and re-layouts  7.2 us (4%)
  other arithmetic  4.28 us (2%)
    all_to_all x5, blocking collectives, exchange(): return lax.all_to_all(x, 'item', 0, 0, axis_index_groups=groups, tiled=True)  59 us
    ppermute x3, waiting for transfers between devices, over_users(): lax.ppermute(x, 'user', [(u, (u + shift) % n_user) for u in range(n_user)])  16.6 us
    all_to_all x3, starting transfers between devices, exchange(): return lax.all_to_all(x, 'item', 0, 0, axis_index_groups=groups, tiled=True)  15.3 us
    pallas_call x2, Pallas kernels, shards(): call(mid_kernel, [VMEM, VMEM, ANY, ANY], [(shape((half, rank), BF16), VME...  12.4 us
    all_to_all x1, blocking collectives, shards(): got = lax.all_to_all(payload, 'item', 0, 0, tiled=True)  12.1 us
    all_to_all x3, waiting for transfers between devices, exchange(): return lax.all_to_all(x, 'item', 0, 0, axis_index_groups=groups, tiled=True)  11.8 us
    pallas_call x1, Pallas kernels, shards(): call(functools.partial(rhs_kernel, n_user, cap), [SMEM] * 6 + [ANY, ANY,...  9.87 us
    pallas_call x1, Pallas kernels, shards(): call(functools.partial(first_kernel, cap, n_items), [SMEM, VMEM] + [ANY]...  7.11 us
  transfers between devices with their start and end apart: 11, of which 6 were waited for; matrix products, arithmetic and copies ran while one was open for 4% of the time, Pallas kernels for 6%

profile of v1, /device:TPU:0, one launch (start us, length us, event | category | flops | bytes accessed | tf_op | source)
XLA Modules:
  0.0 184.8 jit_solution(4178764512131797914)
XLA Ops:
  0.0 0.7 pad_add_fusion.1.at
  0.7 4.1 %shard_map.64 = (bf16[16,96,512]{2,1,0:T(8,128)(2,1)}, s32[16]{0:T(128)}) custom-call(s32[2]{0:T(128)} %pad_add_fusion.1.at, s32[31]{0:T(128)} %bitcast.31, s32[31]{0:T(128)} %bitcast.33, s32[31]{0:T(128)} %bitcast.35, s32[31]{0:T(128)} %bitcast.37, s32[31,96,512]{2,1,0:T(8,128)} %bitcast.21), custom_call_target="tpu_custom_call" | custom-call | bytes 4718592 | tf_op jit(solution)/shard_map/pallas_call | solution.py:355
  4.8 3.0 %collective-permute-start.4 = (bf16[16,96,512]{2,1,0:T(8,128)(2,1)}, bf16[16,96,512]{2,1,0:T(8,128)(2,1)}, u32[]{:S(2)}, u32[]{:S(2)}) collective-permute-start(bf16[16,96,512]{2,1,0:T(8,128)(2,1)} %get-tuple-element.27.out_tiles), channel_id=1, source_target_pairs={{0,16},{16,0},{1,17},{17,1},{2,18},{18,2},{3,19},{19,3},{4,20},{20... | collective-permute-start | bytes 4718600 | tf_op jit(solution)/shard_map/ppermute | solution.py:348
  7.8 0.0 copy-start.4
  7.8 0.0 copy-start.1
  7.8 9.9 %shard_map.65 = (f32[768,256]{1,0:T(8,128)}, f32[768,256]{1,0:T(8,128)}, bf16[16,96,512]{2,1,0:T(8,128)(2,1)}, s32[16]{0:T(128)}) custom-call(s32[2]{0:T(128)} %pad_add_fusion.1.at, s32[31]{0:T(128)} %bitcast.32, s32[31]{0:T(128)} %bitcast.34, s32[31]{0:T(128)} %bitcast.36, s32[31]{0:T(128)} %bitcast.38, s32[16]{0:T(128)} %get-tuple-element.26.out_label, ...), custom_call_target="tpu_custom_call" | custom-call | flops 1610612736 | bytes 12189696 | tf_op jit(solution)/shard_map/pallas_call | solution.py:374
  17.7 0.1 collective-permute-start.2
  17.8 0.0 copy-done.4
  17.8 0.1 collective-permute-start
  17.9 0.0 copy-done.1
  17.9 0.5 collective-permute-start.7
  18.4 0.1 collective-permute-start.5
  18.5 1.8 collective-permute-done.2
  20.3 1.2 add_convert_fusion
  21.5 0.0 copy-start.5
  21.5 0.8 copy.10
  22.3 5.8 %all-to-all-start = ((bf16[8,96,256]{2,1,0:T(8,128)(2,1)}), bf16[8,96,256]{2,1,0:T(8,128)(2,1)S(1)}, u32[]{:S(2)}, u32[]{:S(2)}) async-start(bf16[8,96,256]{2,1,0:T(8,128)(2,1)} %bitcast.11), calls=%async_computation | async-start | bytes 786432 | tf_op jit(solution)/shard_map/all_to_all | solution.py:351
  28.1 14.4 %collective-permute-done.4.far = bf16[16,96,512]{2,1,0:T(8,128)(2,1)} collective-permute-done((bf16[16,96,512]{2,1,0:T(8,128)(2,1)}, bf16[16,96,512]{2,1,0:T(8,128)(2,1)}, u32[]{:S(2)}, u32[]{:S(2)}) %collective-permute-start.4) | collective-permute-done | bytes 1572896 | tf_op jit(solution)/shard_map/ppermute | solution.py:348
  42.6 0.0 collective-permute-start.6
  42.6 0.1 constant_dynamic-update-slice_fusion.1
  42.7 0.0 collective-permute-done
  42.7 0.0 copy-done.5
  42.7 0.8 pad_add_fusion.2
  43.5 0.5 collective-permute-start.1
  44.0 0.8 fusion.1
  44.7 1.2 collective-permute-done.1
  46.0 0.0 all-to-all-done
  46.0 0.1 convert_reduce_fusion
  46.0 1.8 collective-permute-start.3
  47.9 0.2 select_reduce_fusion
  48.0 2.2 %collective-permute-done.3 = f32[48,256]{1,0:T(8,128)S(1)} collective-permute-done((f32[48,256]{1,0:T(8,128)S(1)}, f32[48,256]{1,0:T(8,128)S(1)}, u32[]{:S(2)}, u32[]{:S(2)}) %collective-permute-start.3) | collective-permute-done | bytes 49184 | tf_op jit(solution)/shard_map/ppermute | solution.py:348
  50.2 0.6 fusion
  50.8 0.7 broadcast_in_dim.21
  51.5 6.0 %all-to-all-start.1 = ((bf16[8,48,256]{2,1,0:T(8,128)(2,1)}), bf16[8,48,256]{2,1,0:T(8,128)(2,1)S(1)}, u32[]{:S(2)}, u32[]{:S(2)}) async-start(bf16[8,48,256]{2,1,0:T(8,128)(2,1)} %broadcast_in_dim.21), calls=%async_computation.1 | async-start | bytes 393216 | tf_op jit(solution)/shard_map/all_to_all | solution.py:351
  57.6 0.6 sub.7.table
  58.2 0.0 collective-permute-done.7
  58.2 1.3 constant_dynamic-update-slice_fusion.factors
  59.5 0.0 copy-start
  59.5 0.0 collective-permute-done.5.pair_own
  59.5 5.9 %all-to-all-done.1 = bf16[8,48,256]{2,1,0:T(8,128)(2,1)S(1)} async-done(((bf16[8,48,256]{2,1,0:T(8,128)(2,1)}), bf16[8,48,256]{2,1,0:T(8,128)(2,1)S(1)}, u32[]{:S(2)}, u32[]{:S(2)}) %all-to-all-start.1) | async-done | bytes 196640 | tf_op jit(solution)/shard_map/all_to_all | solution.py:351
  65.4 0.0 copy-start.3
  65.4 0.0 collective-permute-done.6.pair_far
  65.4 0.0 copy-done
  65.4 0.7 copy-done.3
  66.0 7.1 %shard_map.66 = (bf16[384,256]{1,0:T(8,128)(2,1)}, bf16[8,384,512]{2,1,0:T(8,128)(2,1)}, f32[384,128]{1,0:T(8,128)}) custom-call(s32[32]{0:T(128)} %sub.7.table, bf16[384,256]{1,0:T(8,128)(2,1)} %bitcast.25, bf16[16,96,512]{2,1,0:T(8,128)(2,1)} %get-tuple-element.31.own, bf16[16,96,512]{2,1,0:T(8,128)(2,1)} %collective-permute-done.4.far, ...), custom_call_target="tpu_custom_call" | custom-call | flops 1610612736 | bytes 10485760 | tf_op jit(solution)/shard_map/pallas_call | solution.py:425
  73.2 11.8 %all_to_all.45.got = bf16[8,48,256]{2,1,0:T(8,128)(2,1)} all-to-all(bf16[8,48,256]{2,1,0:T(8,128)(2,1)} %bitcast.26), channel_id=1, replica_groups={{0,2,4,6,8,10,12,14},{1,3,5,7,9,11,13,15},{16,18,20,22,24,26,28,30},{17..., dimensions={0} | all-to-all | bytes 393216 | tf_op jit(solution)/shard_map/all_to_all | solution.py:351
  85.0 0.6 broadcast_in_dim.22.folded
  85.6 1.9 %shard_map.67 = (f32[48,256]{1,0:T(8,128)}, f32[48,256]{1,0:T(8,128)}, f32[48,256]{1,0:T(8,128)}, bf16[8,48,256]{2,1,0:T(8,128)(2,1)}) custom-call(bf16[8,48,256]{2,1,0:T(8,128)(2,1)} %all_to_all.45.got, f32[48,256]{1,0:T(8,128)} %get-tuple-element.48.direction.residual, f32[48,256]{1,0:T(8,128)} %get-tuple-element.48.direction.residual, ...), custom_call_target="tpu_custom_call" | custom-call | tf_op jit(solution)/shard_map/pallas_call | solution.py:463
  87.5 11.8 %all_to_all.46 = bf16[8,48,256]{2,1,0:T(8,128)(2,1)} all-to-all(bf16[8,48,256]{2,1,0:T(8,128)(2,1)} %get-tuple-element.33), channel_id=1, replica_groups={{0,2,4,6,8,10,12,14},{1,3,5,7,9,11,13,15},{16,18,20,22,24,26,28,30},{17..., dimensions={0} | all-to-all | bytes 393216 | tf_op jit(solution)/shard_map/all_to_all | solution.py:351
  99.2 6.2 %shard_map.68 = bf16[384,256]{1,0:T(8,128)(2,1)} custom-call(bf16[384,256]{1,0:T(8,128)(2,1)} %bitcast.27, f32[384,128]{1,0:T(8,128)} %get-tuple-element.34.reg, bf16[8,384,512]{2,1,0:T(8,128)(2,1)} %get-tuple-element.35.plays, bf16[4096,256]{1,0:T(8,128)(2,1)} %copy-done), custom_call_target="tpu_custom_call" | custom-call | flops 1610612736 | bytes 5242880 | tf_op jit(solution)/shard_map/pallas_call | solution.py:454
  105.4 11.8 %all_to_all.47.got = bf16[8,48,256]{2,1,0:T(8,128)(2,1)} all-to-all(bf16[8,48,256]{2,1,0:T(8,128)(2,1)} %bitcast.28), channel_id=1, replica_groups={{0,2,4,6,8,10,12,14},{1,3,5,7,9,11,13,15},{16,18,20,22,24,26,28,30},{17..., dimensions={0} | all-to-all | bytes 393216 | tf_op jit(solution)/shard_map/all_to_all | solution.py:351
  117.2 1.9 %shard_map.69 = (f32[48,256]{1,0:T(8,128)}, f32[48,256]{1,0:T(8,128)}, f32[48,256]{1,0:T(8,128)}, bf16[8,48,256]{2,1,0:T(8,128)(2,1)}) custom-call(bf16[8,48,256]{2,1,0:T(8,128)(2,1)} %all_to_all.47.got, f32[48,256]{1,0:T(8,128)} %get-tuple-element.36.direction, f32[48,256]{1,0:T(8,128)} %get-tuple-element.37.residual, f32[48,256]{1,0:T(8,128)} %get-tuple-element.38.folded), custom_call_target="tpu_custom_call" | custom-call | tf_op jit(solution)/shard_map/pallas_call | solution.py:463
  119.1 11.8 %all_to_all.48 = bf16[8,48,256]{2,1,0:T(8,128)(2,1)} all-to-all(bf16[8,48,256]{2,1,0:T(8,128)(2,1)} %get-tuple-element.39), channel_id=1, replica_groups={{0,2,4,6,8,10,12,14},{1,3,5,7,9,11,13,15},{16,18,20,22,24,26,28,30},{17..., dimensions={0} | all-to-all | bytes 393216 | tf_op jit(solution)/shard_map/all_to_all | solution.py:351
  130.9 6.2 %shard_map.70 = bf16[384,256]{1,0:T(8,128)(2,1)} custom-call(bf16[384,256]{1,0:T(8,128)(2,1)} %bitcast.29, f32[384,128]{1,0:T(8,128)} %get-tuple-element.34.reg, bf16[8,384,512]{2,1,0:T(8,128)(2,1)} %get-tuple-element.35.plays, bf16[4096,256]{1,0:T(8,128)(2,1)} %copy-done), custom_call_target="tpu_custom_call" | custom-call | flops 1610612736 | bytes 5242880 | tf_op jit(solution)/shard_map/pallas_call | solution.py:454
  137.1 11.8 %all_to_all.49.got = bf16[8,48,256]{2,1,0:T(8,128)(2,1)} all-to-all(bf16[8,48,256]{2,1,0:T(8,128)(2,1)} %bitcast.30), channel_id=1, replica_groups={{0,2,4,6,8,10,12,14},{1,3,5,7,9,11,13,15},{16,18,20,22,24,26,28,30},{17..., dimensions={0} | all-to-all | bytes 393216 | tf_op jit(solution)/shard_map/all_to_all | solution.py:351
  148.9 1.9 %shard_map.71 = (f32[48,256]{1,0:T(8,128)}, f32[48,256]{1,0:T(8,128)}, f32[48,256]{1,0:T(8,128)}, bf16[8,48,256]{2,1,0:T(8,128)(2,1)}) custom-call(bf16[8,48,256]{2,1,0:T(8,128)(2,1)} %all_to_all.49.got, f32[48,256]{1,0:T(8,128)} %get-tuple-element.40.direction, f32[48,256]{1,0:T(8,128)} %get-tuple-element.41.residual, f32[48,256]{1,0:T(8,128)} %get-tuple-element.42.folded), custom_call_target="tpu_custom_call" | custom-call | tf_op jit(solution)/shard_map/pallas_call | solution.py:463
  150.8 3.4 %all-to-all-start.7 = ((bf16[8,48,256]{2,1,0:T(8,128)(2,1)}), bf16[8,48,256]{2,1,0:T(8,128)(2,1)S(1)}, u32[]{:S(2)}, u32[]{:S(2)}) async-start(bf16[8,48,256]{2,1,0:T(8,128)(2,1)} %get-tuple-element.43), calls=%async_computation.7 | async-start | bytes 393216 | tf_op jit(solution)/shard_map/all_to_all | solution.py:351
  154.2 1.8 shard_map.72.base
  155.9 6.0 %all-to-all-done.7 = bf16[8,48,256]{2,1,0:T(8,128)(2,1)S(1)} async-done(((bf16[8,48,256]{2,1,0:T(8,128)(2,1)}), bf16[8,48,256]{2,1,0:T(8,128)(2,1)S(1)}, u32[]{:S(2)}, u32[]{:S(2)}) %all-to-all-start.7) | async-done | bytes 196640 | tf_op jit(solution)/shard_map/all_to_all | solution.py:351
  161.9 0.7 copy-done.2
  162.6 5.9 %shard_map.73 = f32[16,16,128]{2,1,0:T(8,128)} custom-call(bf16[384,256]{1,0:T(8,128)(2,1)} %bitcast.24, f32[384,128]{1,0:T(8,128)} %get-tuple-element.34.reg, f32[16,16,128]{2,1,0:T(8,128)} %shard_map.72.base, bf16[8,384,512]{2,1,0:T(8,128)(2,1)} %get-tuple-element.35.plays, bf16[4096,256]{1,0:T(8,128)(2,1)} %copy-done), custom_call_target="tpu_custom_call" | custom-call | flops 805306368 | bytes 5242880 | tf_op jit(solution)/shard_map/pallas_call | solution.py:476
  168.5 12.1 %all_to_all.50.got = f32[16,16,128]{2,1,0:T(8,128)} all-to-all(f32[16,16,128]{2,1,0:T(8,128)} %shard_map.73), channel_id=1, replica_groups=mesh['user'=2,'item'=16] {'item'}, dimensions={0} | all-to-all | bytes 262144 | tf_op jit(solution)/shard_map/all_to_all | solution.py:484
  180.6 2.5 %shard_map.74 = f32[768,16]{1,0:T(8,128)} custom-call(f32[16,16,128]{2,1,0:T(8,128)} %all_to_all.50.got), custom_call_target="tpu_custom_call" | custom-call | tf_op jit(solution)/shard_map/pallas_call | solution.py:485
  183.0 1.8 copy.11
  (6 shorter events, 0.0 us)
Async XLA Ops:
  4.8 37.8 %collective-permute-start.4 = (bf16[16,96,512]{2,1,0:T(8,128)(2,1)}, bf16[16,96,512]{2,1,0:T(8,128)(2,1)}, u32[]{:S(2)}, u32[]{:S(2)}) collective-permute-start(bf16[16,96,512]{2,1,0:T(8,128)(2,1)} %get-tuple-element.27.out_tiles), channel_id=1, source_target_pairs={{0,16},{16,0},{1,17},{17,1},{2,18},{18,2},{3,19},{19,3},{4,20},{20... | collective-permute-start | bytes 4718600 | tf_op jit(solution)/shard_map/ppermute | solution.py:348
  7.8 10.0 %copy-start.4 = (s32[16]{0:T(128)S(1)}, s32[16]{0:T(128)}, u32[]{:S(2)}) copy-start(s32[16]{0:T(128)} %get-tuple-element.26.out_label) | copy-start | bytes 196
  7.8 10.1 %copy-start.1 = (bf16[2048,256]{1,0:T(8,128)(2,1)S(1)}, bf16[2048,256]{1,0:T(8,128)(2,1)}, u32[]{:S(2)}) copy-start(bf16[2048,256]{1,0:T(8,128)(2,1)} %factors.1) | copy-start | bytes 3145732
  17.7 2.6 %collective-permute-start.2 = (f32[768,256]{1,0:T(8,128)}, f32[768,256]{1,0:T(8,128)S(1)}, u32[]{:S(2)}, u32[]{:S(2)}) collective-permute-start(f32[768,256]{1,0:T(8,128)} %get-tuple-element.30), channel_id=1, source_target_pairs={{0,1},{1,0},{2,3},{3,2},{4,5},{5,4},{6,7},{7,6},{8,9},{9,8},{10,11... | collective-permute-start | bytes 2359304 | tf_op jit(solution)/shard_map/ppermute | solution.py:396
  17.8 24.9 %collective-permute-start = (s32[16]{0:T(128)S(1)}, s32[16]{0:T(128)}, u32[]{:S(2)}, u32[]{:S(2)}) collective-permute-start(s32[16]{0:T(128)S(1)} %copy-done.4), channel_id=1, source_target_pairs={{0,16},{16,0},{1,17},{17,1},{2,18},{18,2},{3,19},{19,3},{4,20},{20... | collective-permute-start | bytes 200 | tf_op jit(solution)/shard_map/ppermute | solution.py:348
  17.9 40.3 %collective-permute-start.7 = (bf16[2048,256]{1,0:T(8,128)(2,1)S(1)}, bf16[2048,256]{1,0:T(8,128)(2,1)}, u32[]{:S(2)}, u32[]{:S(2)}) collective-permute-start(bf16[2048,256]{1,0:T(8,128)(2,1)S(1)} %copy-done.1), channel_id=1, source_target_pairs={{0,1},{1,0},{2,3},{3,2},{4,5},{5,4},{6,7},{7,6},{8,9},{9,8},{10,11... | collective-permute-start | bytes 3145736 | tf_op jit(solution)/shard_map/ppermute | solution.py:408
  18.4 41.1 %collective-permute-start.5 = (bf16[16,96,512]{2,1,0:T(8,128)(2,1)}, bf16[16,96,512]{2,1,0:T(8,128)(2,1)}, u32[]{:S(2)}, u32[]{:S(2)}) collective-permute-start(bf16[16,96,512]{2,1,0:T(8,128)(2,1)} %get-tuple-element.31.own), channel_id=1, source_target_pairs={{0,1},{1,0},{2,3},{3,2},{4,5},{5,4},{6,7},{7,6},{8,9},{9,8},{10,11... | collective-permute-start | bytes 4718600 | tf_op jit(solution)/shard_map/ppermute | solution.py:410
  21.5 21.2 %copy-start.5 = (s32[16]{0:T(128)S(1)}, s32[16]{0:T(128)}, u32[]{:S(2)}) copy-start(s32[16]{0:T(128)} %get-tuple-element.28) | copy-start | bytes 196
  22.3 23.7 %all-to-all-start = ((bf16[8,96,256]{2,1,0:T(8,128)(2,1)}), bf16[8,96,256]{2,1,0:T(8,128)(2,1)S(1)}, u32[]{:S(2)}, u32[]{:S(2)}) async-start(bf16[8,96,256]{2,1,0:T(8,128)(2,1)} %bitcast.11), calls=%async_computation | async-start | bytes 786432 | tf_op jit(solution)/shard_map/all_to_all | solution.py:351
  42.6 22.8 %collective-permute-start.6 = (bf16[16,96,512]{2,1,0:T(8,128)(2,1)}, bf16[16,96,512]{2,1,0:T(8,128)(2,1)}, u32[]{:S(2)}, u32[]{:S(2)}) collective-permute-start(bf16[16,96,512]{2,1,0:T(8,128)(2,1)} %collective-permute-done.4.far), channel_id=1, source_target_pairs={{0,1},{1,0},{2,3},{3,2},{4,5},{5,4},{6,7},{7,6},{8,9},{9,8},{10,11... | collective-permute-start | bytes 4718600 | tf_op jit(solution)/shard_map/ppermute | solution.py:411
  43.5 2.5 %collective-permute-start.1 = (s32[32]{0:T(128)S(1)}, s32[32]{0:T(128)S(1)}, u32[]{:S(2)}, u32[]{:S(2)}) collective-permute-start(s32[32]{0:T(128)S(1)} %pad_add_fusion.2), channel_id=1, source_target_pairs={{0,1},{1,0},{2,3},{3,2},{4,5},{5,4},{6,7},{7,6},{8,9},{9,8},{10,11... | collective-permute-start | bytes 392 | tf_op jit(solution)/shard_map/ppermute | solution.py:412
  46.0 4.2 %collective-permute-start.3 = (f32[48,256]{1,0:T(8,128)S(1)}, f32[48,256]{1,0:T(8,128)S(1)}, u32[]{:S(2)}, u32[]{:S(2)}) collective-permute-start(f32[48,256]{1,0:T(8,128)S(1)} %slice.11), channel_id=1, source_target_pairs={{0,16},{16,0},{1,17},{17,1},{2,18},{18,2},{3,19},{19,3},{4,20},{20... | collective-permute-start | bytes 147464 | tf_op jit(solution)/shard_map/ppermute | solution.py:348
  51.5 13.8 %all-to-all-start.1 = ((bf16[8,48,256]{2,1,0:T(8,128)(2,1)}), bf16[8,48,256]{2,1,0:T(8,128)(2,1)S(1)}, u32[]{:S(2)}, u32[]{:S(2)}) async-start(bf16[8,48,256]{2,1,0:T(8,128)(2,1)} %broadcast_in_dim.21), calls=%async_computation.1 | async-start | bytes 393216 | tf_op jit(solution)/shard_map/all_to_all | solution.py:351
  59.5 5.9 %copy-start = (bf16[4096,256]{1,0:T(8,128)(2,1)}, bf16[4096,256]{1,0:T(8,128)(2,1)S(1)}, u32[]{:S(2)}) copy-start(bf16[4096,256]{1,0:T(8,128)(2,1)S(1)} %constant_dynamic-update-slice_fusion.factors) | copy-start | bytes 6291460
  65.4 0.7 copy-start.3
  150.8 11.1 %all-to-all-start.7 = ((bf16[8,48,256]{2,1,0:T(8,128)(2,1)}), bf16[8,48,256]{2,1,0:T(8,128)(2,1)S(1)}, u32[]{:S(2)}, u32[]{:S(2)}) async-start(bf16[8,48,256]{2,1,0:T(8,128)(2,1)} %get-tuple-element.43), calls=%async_computation.7 | async-start | bytes 393216 | tf_op jit(solution)/shard_map/all_to_all | solution.py:351
  161.9 0.7 copy-start.2

commit v2 on v1

v2 whole, which is shorter than its diff:
```python
import functools

import jax
import jax.numpy as jnp
from jax import lax
from jax.experimental import pallas as pl
from jax.experimental.pallas import tpu as pltpu
from jax.sharding import PartitionSpec as P

GROUPS = 8
CBLK = 4
ITERS = 4

EPS = 1.0
GUARD = 1e-06

HALVES = 2
HG = GROUPS // HALVES

BF16 = jnp.bfloat16
F32 = jnp.float32
VMEM = pl.BlockSpec(memory_space=pltpu.VMEM)
SMEM = pl.BlockSpec(memory_space=pltpu.SMEM)
HBM = pl.BlockSpec(memory_space=pltpu.HBM)


def log_tile(counts, rows, cols):
    rank_rows = lax.broadcasted_iota(jnp.int32, counts.shape, 0)
    rank_cols = lax.broadcasted_iota(jnp.int32, counts.shape, 1)
    inside = (rank_rows < rows) & (rank_cols < cols)
    values = jnp.log(1.0 + counts.astype(F32) / EPS)
    return jnp.where(inside, values, 0.0).astype(BF16)


def start_tiles(n_user, cap, own, owner, cell, counts, label, slots, fill, buf, sems):
    total = label.shape[0]
    for s in range(total):
        label[s] = -1
        slots[s] = -1
    for s in range(n_user):
        fill[s] = 0
    me = lax.axis_index("user")

    def visit(t, carry):
        shift = lax.rem(owner[t] - me + n_user, n_user)

        @pl.when((shift == 0) if own else (shift != 0))
        def _():
            base = 0 if own else shift - 1
            k = fill[base]
            slot = base * cap + k
            fill[base] = k + 1
            slots[slot] = t
            label[slot] = cell[t]
            pltpu.make_async_copy(counts.at[t], buf.at[slot], sems.at[slot]).start()

        return carry

    lax.fori_loop(0, counts.shape[0], visit, 0)


def label_rows(label, base, count):
    lane = lax.broadcasted_iota(jnp.int32, (16, 128), 1)
    block = jnp.zeros((16, 128), F32)
    for k in range(count):
        block = jnp.where(lane == k, label[base + k].astype(F32), block)
    return block.astype(BF16)


def pack_kernel(n_user, cap, sizes, owner, cell, rows, cols, counts, *refs):
    parts, (label, slots, fill, buf, logs, cells, sems, out_sems, cell_sems) = refs[: len(sizes)], refs[len(sizes) :]
    start_tiles(n_user, cap, False, owner, cell, counts, label, slots, fill, buf, sems)
    height = counts.shape[1]

    def cells_copy(shift):
        tail = pl.ds(sizes[0] * height, 16)
        return pltpu.make_async_copy(cells.at[shift], parts[0].at[shift, tail, :], cell_sems.at[shift])

    cells[...] = jnp.zeros_like(cells)
    for shift in range(n_user - 1):
        cells[shift, :, 0:128] = label_rows(label, shift * cap, cap)
        cells_copy(shift).start()

    def each(s, act):
        k, shift = lax.rem(s, cap), s // cap
        low = 0
        for part, size in zip(parts, sizes):

            @pl.when((slots[s] >= 0) & (k >= low) & (k < low + size))
            def _(part=part, low=low):
                row = pl.multiple_of((k - low) * height, 16)
                act(pltpu.make_async_copy(logs.at[s], part.at[shift, pl.ds(row, height), :], out_sems.at[s]))

            low += size

    def work(s, carry):
        t = slots[s]

        @pl.when(t >= 0)
        def _():
            pltpu.make_async_copy(counts.at[t], buf.at[s], sems.at[s]).wait()
            logs[s] = log_tile(buf[s], rows[t], cols[t])

        each(s, lambda copy: copy.start())
        return carry

    def finish(s, carry):
        each(s, lambda copy: copy.wait())
        return carry

    lax.fori_loop(0, label.shape[0], work, 0)
    lax.fori_loop(0, label.shape[0], finish, 0)
    for shift in range(n_user - 1):
        cells_copy(shift).wait()


def this_half():
    return lax.rem(lax.axis_index("item"), HALVES)


def rhs_kernel(n_user, cap, sizes, owner, cell, rows, cols, out_label, counts, *refs):
    n = len(sizes)
    parts, (factors, keep, send, tiles, label), bufs = refs[:n], refs[n : n + 5], refs[n + 5 : n + 5 + n]
    slots, fill, buf, logs, dense, sems, out_sems, part_sems = refs[n + 5 + n :]
    start_tiles(n_user, cap, True, owner, cell, counts, label, slots, fill, buf, sems)
    height, width = counts.shape[1], counts.shape[2]
    half = HG * height
    core = this_half()
    moves = [
        pltpu.make_async_copy(part.at[:, pl.ds(0, size * height), :], target, part_sems.at[i])
        for i, (part, target, size) in enumerate(zip(parts, bufs, sizes))
    ]
    for move in moves:
        move.start()
    dense[...] = jnp.zeros_like(dense)

    def put(tile, shift, where):
        group, block = where // CBLK, where % CBLK
        side = jnp.where(group // HG == core, 0, 1)
        row = side * (n_user * half) + shift * half + (group % HG) * height
        one, none = jnp.ones((), BF16), jnp.zeros((), BF16)
        weighted = jnp.where(tile > none, tile + one, none)
        dense[pl.ds(pl.multiple_of(row, 16), height), pl.ds(pl.multiple_of(block * width, 128), width)] = weighted

    low = 0
    for move, source, size in zip(moves, bufs, sizes):
        move.wait()

        def put_sent(s, carry, source=source, size=size, low=low):
            shift, k = s // size, lax.rem(s, size)
            where = out_label[shift * cap + low + k]

            @pl.when(where >= 0)
            def _():
                put(source[shift, pl.ds(pl.multiple_of(k * height, 16), height), :], shift + 1, where)

            return carry

        lax.fori_loop(0, (n_user - 1) * size, put_sent, 0)
        low += size

    def own_copy(s):
        at = pl.ds(pl.multiple_of(s * height, 16), height)
        return pltpu.make_async_copy(logs.at[at], tiles.at[at], out_sems.at[s])

    tail = pl.ds(cap * height, 16)
    tail_copy = pltpu.make_async_copy(logs.at[tail], tiles.at[tail], out_sems.at[cap])
    logs[cap * height :, :] = jnp.zeros((16, width), BF16)
    logs[cap * height :, 0:128] = label_rows(label, 0, cap)
    tail_copy.start()

    def work_own(s, carry):
        t = slots[s]

        @pl.when(t >= 0)
        def _():
            pltpu.make_async_copy(counts.at[t], buf.at[s], sems.at[s]).wait()
            tile = log_tile(buf[s], rows[t], cols[t])
            logs[pl.ds(pl.multiple_of(s * height, 16), height), :] = tile
            own_copy(s).start()
            put(tile, 0, label[s])

        return carry

    def finish_own(s, carry):
        @pl.when(slots[s] >= 0)
        def _():
            own_copy(s).wait()

        return carry

    lax.fori_loop(0, cap, work_own, 0)
    n_chunk = keep.shape[0]
    chunk = half // n_chunk
    for side, target in ((1, send), (0, keep)):

        def dots(s, carry, side=side, target=target):
            row = pl.multiple_of((side * n_user + s) * half, 16)
            part = jnp.dot(dense[pl.ds(row, half), :], factors[...], preferred_element_type=F32)
            at = pl.ds(pl.multiple_of(s * chunk, 8), chunk)
            for k in range(n_chunk):
                target[k, at, :] = part[k * chunk : (k + 1) * chunk, :].astype(target.dtype)
            return carry

        lax.fori_loop(0, n_user, dots, 0)
    lax.fori_loop(0, cap, finish_own, 0)
    tail_copy.wait()


def place_tiles(act, source, label_of, count, plays, first_block, sems, base):
    height = plays.shape[1] // HG
    core = this_half()

    def visit(k, carry):
        where = label_of(k)

        @pl.when((where >= core * (HG * CBLK)) & (where < (core + 1) * (HG * CBLK)))
        def _():
            local = where - core * (HG * CBLK)
            target = plays.at[
                first_block + lax.rem(local, CBLK), pl.ds(pl.multiple_of(local // CBLK * height, 16), height), :
            ]
            tile = source.at[pl.ds(pl.multiple_of(k * height, 16), height), :]
            act(pltpu.make_async_copy(tile, target, sems.at[base + k]))

        return carry

    lax.fori_loop(0, count, visit, 0)


def place_kernel(cap, sizes, own_label, tiles, pair_tiles, *refs):
    n = len(sizes) - 1
    parts, pair_parts = refs[:n], refs[n : 2 * n]
    factors, pair_factors, plays, stacked, labels, raw, whole, raw_sems, label_sem, sems = refs[2 * n :]
    height = plays.shape[1] // HG
    senders = parts[0].shape[0]
    tails = [pair_tiles.at[pl.ds(cap * height, 16), pl.ds(0, 128)]]
    for first in (parts[0], pair_parts[0]):
        for s in range(senders):
            tails.append(first.at[s, pl.ds(sizes[0] * height, 16), pl.ds(0, 128)])
    reads = [pltpu.make_async_copy(tail, raw.at[i], raw_sems.at[i]) for i, tail in enumerate(tails)]
    for read in reads:
        read.start()
    plays[...] = jnp.zeros_like(plays)

    def both(act):
        place_tiles(act, tiles, lambda k: own_label[k], cap, plays, 0, sems, 0)
        place_tiles(act, pair_tiles, lambda k: labels[0, k], cap, plays, CBLK, sems, cap)
        base = 2 * cap
        for side, group in enumerate((parts, pair_parts)):
            for s in range(senders):
                row = 1 + side * senders + s
                low = 0
                for part, size in zip(group, sizes):
                    label_of = lambda k, row=row, low=low: labels[row, low + k]
                    place_tiles(act, part.at[s], label_of, size, plays, side * CBLK, sems, base)
                    low += size
                    base += size

    for i, read in enumerate(reads):
        read.wait()
        whole[i : i + 1, :] = raw[i].astype(F32)[0:1, :].astype(jnp.int32)
    to_scalars = pltpu.make_async_copy(whole, labels, label_sem)
    to_scalars.start()
    items = factors.shape[0]
    stacked[:items, :] = factors[...]
    stacked[items:, :] = pair_factors[...]
    to_scalars.wait()
    both(lambda copy: copy.start())
    both(lambda copy: copy.wait())


def start_kernel(*refs):
    *parts, direction, spread = refs
    rhs = sum(p[...] for p in parts)
    direction[...] = rhs
    low = rhs.astype(BF16)
    for k in range(spread.shape[0]):
        spread[k] = low


def scaled_block(direction, factors, plays):
    projected = lax.dot_general(direction, factors, (((1,), (1,)), ((), ())), preferred_element_type=F32)
    confidence = 1.0 + plays
    return projected, (confidence * projected).astype(BF16)


def lanes(x):
    return sum(x[:, k * 128 : (k + 1) * 128] for k in range(x.shape[1] // 128))


def first_kernel(
    n_items, offset, labels, direction, placed, late, pair_late, factors, image, plays, reg, seen, acc, buf, sems
):
    senders, height = late.shape[0], plays.shape[1] // HG
    size = late.shape[1] // height
    moves = [pltpu.make_async_copy(part, buf.at[i], sems.at[i]) for i, part in enumerate((late, pair_late))]
    for move in moves:
        move.start()
    plays[...] = placed[...]
    core = this_half()
    for side, move in enumerate(moves):
        move.wait()

        def visit(i, carry, side=side):
            s, k = i // size, lax.rem(i, size)
            where = labels[1 + side * senders + s, offset + k]

            @pl.when((where >= core * (HG * CBLK)) & (where < (core + 1) * (HG * CBLK)))
            def _():
                local = where - core * (HG * CBLK)
                row = pl.ds(pl.multiple_of(local // CBLK * height, 16), height)
                tile = buf[side, s, pl.ds(pl.multiple_of(k * height, 16), height), :]
                plays[side * CBLK + lax.rem(local, CBLK), row, :] = tile

            return carry

        lax.fori_loop(0, senders * size, visit, 0)
    blocks, _, width = plays.shape
    for j in range(blocks):
        block = factors[j * width : (j + 1) * width, :]
        value = plays[j].astype(F32)
        _, scaled = scaled_block(direction[...], block, value)
        part = jnp.dot(scaled, block, preferred_element_type=F32)
        count = lanes(jnp.where(value > 0, 1.0, 0.0))
        if j == 0:
            acc[...] = part
            seen[...] = count
        else:
            acc[...] += part
            seen[...] += count
    share = jnp.sum(seen[...], axis=1, keepdims=True) / n_items
    reg[...] = jnp.broadcast_to(share, reg.shape)
    image[...] = (acc[...] + share * direction[...].astype(F32)).astype(BF16)


def mid_kernel(direction, reg, plays, factors, image, acc):
    blocks, _, width = plays.shape
    for j in range(blocks):
        block = factors[j * width : (j + 1) * width, :]
        _, scaled = scaled_block(direction[...], block, plays[j].astype(F32))
        part = jnp.dot(scaled, block, preferred_element_type=F32)
        if j == 0:
            acc[...] = part
        else:
            acc[...] += part
    image[...] = (acc[...] + reg[:, :1] * direction[...].astype(F32)).astype(BF16)


def last_kernel(direction, reg, base, plays, factors, payload, acc, laid):
    blocks, _, width = plays.shape
    for j in range(blocks):
        block = factors[j * width : (j + 1) * width, :]
        projected, scaled = scaled_block(direction[...], block, plays[j].astype(F32))
        part = lanes(scaled.astype(F32) * projected)
        if j == 0:
            acc[...] = part
        else:
            acc[...] += part
    wide = direction[...].astype(F32)
    along = acc[...] + reg[:, :1] * lanes(wide * wide)
    along = jnp.broadcast_to(jnp.sum(along, axis=1, keepdims=True), acc.shape)
    laid[...] = jnp.zeros_like(laid)
    n_item = base.shape[0]
    first, free = free_lanes(acc.shape[0] * HALVES // n_item)
    put_row(laid, 0, as_row(along), first, free)
    for i in range(n_item):
        payload[i] = base[i] + laid[...]


def free_lanes(chunk):
    return 2 * chunk, 128 - 2 * chunk


def as_row(column):
    n = column.shape[0]
    return jnp.concatenate([column[k : min(k + 128, n), :].T[0:1, :] for k in range(0, n, 128)], axis=1)


def put_row(target, row, values, first, free):
    n = values.shape[1]
    for k in range(0, n, free):
        m = min(free, n - k)
        target[row + k // free : row + k // free + 1, first : first + m] = values[:, k : k + m]


def get_row(source, row, n, first, free):
    pieces = [source[row + k // free : row + k // free + 1, first : first + min(free, n - k)] for k in range(0, n, free)]
    return jnp.concatenate(pieces, axis=1)


def lay_base(folded, direction, residual, base):
    n_item, share, _ = base.shape
    chunk = folded.shape[0]
    first, free = free_lanes(chunk)
    base[...] = jnp.zeros_like(base)
    norm = jnp.sum(residual * residual, axis=1, keepdims=True)
    norm = as_row(jnp.broadcast_to(norm, (chunk, 128)))
    sides = (folded.T, direction.T)
    row = n_item // HALVES * chunk // free
    for i in range(n_item):
        for k in range(2):
            base[i, :, k * chunk : (k + 1) * chunk] = sides[k][i * share : (i + 1) * share, :]
        put_row(base.at[i], row, norm, first, free)


def final_kernel(got, out):
    n_item = got.shape[0]
    n_chunk = n_item // HALVES
    half = out.shape[1] // HALVES
    chunk = half // n_chunk
    first, free = free_lanes(chunk)
    for h in range(HALVES):
        sources = [got[k * HALVES + h] for k in range(n_chunk)]
        along = get_row(sum(sources), 0, half, first, free)
        norm = jnp.concatenate([get_row(x, half // free, chunk, first, free) for x in sources], axis=1)
        alpha = norm / (along + GUARD)
        for k, x in enumerate(sources):
            at = slice(k * chunk, (k + 1) * chunk)
            out[:, h * half + k * chunk : h * half + (k + 1) * chunk] = x[:, :chunk] + alpha[:, at] * x[:, chunk : 2 * chunk]


def vector_kernel(number, got, direction, residual, folded, spread, *outs):
    image = sum(got[k].astype(F32) for k in range(got.shape[0]))
    d, r = direction[...], residual[...]
    norm = jnp.sum(r * r, axis=1, keepdims=True)
    alpha = norm / (jnp.sum(d * image, axis=1, keepdims=True) + GUARD)
    step = alpha * d
    total = folded[...] + step if number else step
    r = r - alpha * image
    fresh = jnp.sum(r * r, axis=1, keepdims=True)
    d = r + fresh / (norm + GUARD) * d
    low = d.astype(BF16)
    for k in range(spread.shape[0]):
        spread[k] = low
    if len(outs) == 1:
        lay_base(total, d, r, outs[0])
    else:
        outs[0][...], outs[1][...], outs[2][...] = d, r, total


def shards(play_counts, tile_owner, tile_cell, tile_rows, tile_cols, item_factors):
    counts = play_counts[0]
    tiles_dev, height, width = counts.shape
    n_user = lax.axis_size("user")
    n_item = lax.axis_size("item")
    shard_items, rank = item_factors.shape
    cap = GROUPS * CBLK // n_user
    n_out = (n_user - 1) * cap
    n_chunk = n_item // HALVES
    half = HG * height
    chunk = half // n_chunk
    n_items = float(shard_items * n_item)
    blocks = HALVES * CBLK
    pair = [(i, i ^ 1) for i in range(n_item)]
    groups = [[h + HALVES * k for k in range(n_chunk)] for h in range(HALVES)]

    def shape(dims, dtype):
        return jax.ShapeDtypeStruct(dims, dtype)

    def call(kernel, ins, outs, scratch, grant, flops=0, nbytes=0, aliases=None):
        return pl.pallas_call(
            kernel,
            out_shape=[o[0] for o in outs],
            in_specs=ins,
            out_specs=[o[1] for o in outs],
            scratch_shapes=scratch,
            input_output_aliases=aliases or {},
            compiler_params=pltpu.CompilerParams(vmem_limit_bytes=grant * 2**20),
            cost_estimate=pl.CostEstimate(flops=flops, bytes_accessed=nbytes, transcendentals=0),
        )

    def over_users(x, shift):
        return lax.ppermute(x, "user", [(u, (u + shift) % n_user) for u in range(n_user)])

    def from_users(x):
        got = [over_users(x[s - 1 : s], s) for s in range(1, n_user)]
        return jnp.concatenate(got) if n_user > 2 else got[0]

    def to_pair(x):
        return lax.ppermute(x, "item", pair)

    def exchange(x):
        return lax.all_to_all(x, "item", 0, 0, axis_index_groups=groups, tiled=True)

    route = (tile_owner[0], tile_cell[0], tile_rows[0], tile_cols[0])
    dma = pltpu.SemaphoreType.DMA
    sizes = [cap - cap // 4, cap // 4]
    part_shapes = [(n_user - 1, size * height, width) for size in sizes]
    sent_shapes = [(n_user - 1, size * height + (0 if i else 16), width) for i, size in enumerate(sizes)]
    *parts, out_label = call(
        functools.partial(pack_kernel, n_user, cap, sizes),
        [SMEM] * 4 + [HBM],
        [(shape(sent, BF16), HBM) for sent in sent_shapes] + [(shape((n_out,), jnp.int32), SMEM)],
        [
            pltpu.SMEM((n_out,), jnp.int32),
            pltpu.SMEM((n_user,), jnp.int32),
            pltpu.VMEM((n_out, height, width), jnp.int32),
            pltpu.VMEM((n_out, height, width), BF16),
            pltpu.VMEM((n_user - 1, 16, width), BF16),
            dma((n_out,)),
            dma((n_out,)),
            dma((n_user - 1,)),
        ],
        56,
        nbytes=n_out * height * width * 6,
    )(*route, counts)
    far = [from_users(part) for part in parts[:-1]]
    pair_factors = to_pair(item_factors)

    state = (n_chunk, n_user * chunk, rank)
    keep, send, own, own_label = call(
        functools.partial(rhs_kernel, n_user, cap, sizes),
        [SMEM] * 5 + [HBM] * (1 + len(sizes)) + [VMEM],
        [
            (pltpu.VMEM(state, F32), VMEM),
            (pltpu.VMEM(state, BF16), VMEM),
            (shape((cap * height + 16, width), BF16), HBM),
            (shape((cap,), jnp.int32), SMEM),
        ],
        [pltpu.VMEM(part, BF16) for part in part_shapes]
        + [
            pltpu.SMEM((cap,), jnp.int32),
            pltpu.SMEM((n_user,), jnp.int32),
            pltpu.VMEM((cap, height, width), jnp.int32),
            pltpu.VMEM((cap * height + 16, width), BF16),
            pltpu.VMEM((HALVES * n_user * half, shard_items), BF16),
            dma((cap,)),
            dma((cap + 1,)),
            dma((len(sizes),)),
        ],
        56,
        flops=2 * HALVES * n_user * half * shard_items * rank,
        nbytes=2 * tiles_dev * height * width * 4,
    )(*route, out_label, counts, *parts, item_factors)

    summed = exchange((keep + to_pair(send).astype(F32)).astype(BF16))
    pair_own = to_pair(own)
    summed = jnp.sum(summed.astype(F32), axis=0).reshape(n_user, chunk, rank)
    terms = [summed[0]] + [over_users(summed[s], s) for s in range(1, n_user)]
    direction, spread = call(
        start_kernel,
        [VMEM] * n_user,
        [(shape((chunk, rank), F32), VMEM), (shape((n_chunk, chunk, rank), BF16), VMEM)],
        [],
        4,
    )(*terms)
    residual = folded = direction
    last_part, spread = lax.optimization_barrier((parts[-1], spread))
    late = from_users(last_part)
    pair_parts = [to_pair(part) for part in far]
    plays_shape = (blocks, half, width)
    n_labels = 2 * (n_user - 1) + 1
    label_shape = (-(-n_labels // 8) * 8, 128)
    placed, factors, labels = call(
        functools.partial(place_kernel, cap, sizes),
        [SMEM] + [HBM] * (2 + 2 * len(far)) + [VMEM] * 2,
        [
            (pltpu.VMEM(plays_shape, BF16), VMEM),
            (pltpu.VMEM((HALVES * shard_items, rank), BF16), VMEM),
            (shape(label_shape, jnp.int32), SMEM),
        ],
        [
            pltpu.VMEM((n_labels, 16, 128), BF16),
            pltpu.VMEM(label_shape, jnp.int32),
            dma((n_labels,)),
            dma(()),
            dma((2 * n_user * cap,)),
        ],
        50,
        nbytes=2 * blocks * half * width,
    )(own_label, own, pair_own, *far, *pair_parts, item_factors, pair_factors)

    block_flops = 4 * half * blocks * width * rank
    block_bytes = blocks * width * (half + rank) * 2
    share = rank // n_item
    payload_shape = shape((n_item, share, 128), F32)
    image_out = (shape((half, rank), BF16), VMEM)
    for number in range(ITERS):
        whole = exchange(spread).reshape(half, rank)
        if number == ITERS - 1:
            break
        if number == 0:
            late, whole, labels = lax.optimization_barrier((late, whole, labels))
            pair_late = to_pair(late)
            image, plays, reg = call(
                functools.partial(first_kernel, n_items, cap - sizes[-1]),
                [SMEM] + [VMEM] * 2 + [HBM] * 2 + [VMEM],
                [image_out, (pltpu.VMEM(plays_shape, BF16), VMEM), (shape((half, 128), F32), VMEM)],
                [
                    pltpu.VMEM((half, 128), F32),
                    pltpu.VMEM((half, rank), F32),
                    pltpu.VMEM((2, *part_shapes[-1]), BF16),
                    dma((2,)),
                ],
                20,
                flops=block_flops,
                nbytes=2 * block_bytes,
            )(labels, whole, placed, late, pair_late, factors)
        else:
            (image,) = call(
                mid_kernel,
                [VMEM] * 4,
                [image_out],
                [pltpu.VMEM((half, rank), F32)],
                12,
                flops=block_flops,
                nbytes=block_bytes,
            )(whole, reg, plays, factors)
        got = exchange(image.reshape(n_chunk, chunk, rank))
        ends = number == ITERS - 2
        outs = [(payload_shape, VMEM)] if ends else [(shape((chunk, rank), F32), VMEM)] * 3
        spread, *outs = call(
            functools.partial(vector_kernel, number),
            [VMEM] * 4,
            [(shape((n_chunk, chunk, rank), BF16), VMEM)] + outs,
            [],
            4,
        )(got, direction, residual, folded)
        if ends:
            (base,) = outs
        else:
            direction, residual, folded = outs

    (payload,) = call(
        last_kernel,
        [VMEM] * 5,
        [(payload_shape, VMEM)],
        [pltpu.VMEM((half, 128), F32), pltpu.VMEM((share, 128), F32)],
        12,
        flops=block_flops // 2,
        nbytes=block_bytes,
    )(whole, reg, base, plays, factors)
    got = lax.all_to_all(payload, "item", 0, 0, tiled=True)
    (out,) = call(final_kernel, [VMEM], [(shape((share, HALVES * half), F32), VMEM)], [], 4)(got)
    return out.T


def solution(mesh):
    placed = (
        P("item", "user", None, None),
        P("item", "user"),
        P("item", "user"),
        P("item", "user"),
        P("item", "user"),
        P("item", None),
    )
    return jax.shard_map(
        shards, mesh=mesh, in_specs=placed, out_specs=P("user", "item"), check_vma=False
    )
```

time: 186 us -> 148 us (0.80)
  Pallas kernels: 49.3 us -> 31.3 us
  waiting for transfers between devices: 31.5 us -> 17.9 us
  blocking collectives: 71.1 us -> 77 us
  starting transfers between devices: 21.4 us -> 16 us
  other arithmetic: 4.28 us -> 0.88 us
  local copies, waits for them, and re-layouts: 7.2 us -> 4.23 us
    pallas_call x11 -> x12, Pallas kernels: 49.3 us -> 31.3 us  [the longest x1 8.83 us: shards(): call(functools.partial(rhs_kernel, n_user, cap, sizes), [SMEM] * 5 + [HBM...]
    all_to_all x3 -> x2, waiting for transfers between devices: 11.8 us -> 2.11 us  [exchange(): return lax.all_to_all(x, 'item', 0, 0, axis_index_groups=groups, tiled=True)]
    all_to_all x5 -> x6, blocking collectives: 59 us -> 66.4 us  [exchange(): return lax.all_to_all(x, 'item', 0, 0, axis_index_groups=groups, tiled=True)]
    all_to_all x3 -> x2, starting transfers between devices: 15.3 us -> 10.7 us  [exchange(): return lax.all_to_all(x, 'item', 0, 0, axis_index_groups=groups, tiled=True)]
    ppermute x3, waiting for transfers between devices: 16.6 us -> 12.9 us  [over_users(): lax.ppermute(x, 'user', [(u, (u + shift) % n_user) for u in range(n_user)])]
    unnamed x13 -> x10, local copies, waits for them, and re-layouts: 1.43 us -> 4.22 us
  transfers between devices with their start and end apart: 11 -> 10, of which waited for: 6 -> 5; matrix products, arithmetic and copies ran while one was open for 4% -> 1% of each run, Pallas kernels for 6% -> 11%
where the time goes in v2:
time: 148 us; the launch traced here: 147 us
  blocking collectives  77 us (52%)
  Pallas kernels  31.3 us (21%)
  waiting for transfers between devices  17.9 us (12%)
  starting transfers between devices  16 us (11%)
  local copies, waits for them, and re-layouts  4.23 us (3%)
    all_to_all x6, blocking collectives, exchange(): return lax.all_to_all(x, 'item', 0, 0, axis_index_groups=groups, tiled=True)  66.4 us
    ppermute x3, waiting for transfers between devices, over_users(): lax.ppermute(x, 'user', [(u, (u + shift) % n_user) for u in range(n_user)])  12.9 us
    all_to_all x2, starting transfers between devices, exchange(): return lax.all_to_all(x, 'item', 0, 0, axis_index_groups=groups, tiled=True)  10.7 us
    all_to_all x1, blocking collectives, shards(): got = lax.all_to_all(payload, 'item', 0, 0, tiled=True)  10.5 us
    pallas_call x1, Pallas kernels, shards(): call(functools.partial(rhs_kernel, n_user, cap, sizes), [SMEM] * 5 + [HBM...  8.83 us
    pallas_call x1, Pallas kernels, shards(): call(functools.partial(place_kernel, cap, sizes), [SMEM] + [HBM] * (2 + 2...  6.32 us
    pallas_call x1, Pallas kernels, shards(): call(functools.partial(pack_kernel, n_user, cap, sizes), [SMEM] * 4 + [HB...  4.38 us
    unnamed x10, local copies, waits for them, and re-layouts  4.22 us
  transfers between devices with their start and end apart: 10, of which 5 were waited for; matrix products, arithmetic and copies ran while one was open for 1% of the time, Pallas kernels for 11%

profile of v2, /device:TPU:0, one launch (start us, length us, event | category | flops | bytes accessed | tf_op | source)
XLA Modules:
  0.0 147.4 jit_solution(3388174649869348904)
XLA Ops:
  0.0 4.4 %shard_map.64 = (bf16[1,1168,512]{2,1,0:T(8,128)(2,1)}, bf16[1,384,512]{2,1,0:T(8,128)(2,1)}, s32[16]{0:T(128)}) custom-call(s32[31]{0:T(128)} %bitcast.22, s32[31]{0:T(128)} %bitcast.24, s32[31]{0:T(128)} %bitcast.26, s32[31]{0:T(128)} %bitcast.28, s32[31,96,512]{2,1,0:T(8,128)} %bitcast.20), custom_call_target="tpu_custom_call" | custom-call | bytes 4718592 | tf_op jit(solution)/shard_map/pallas_call | solution.py:491
  4.4 3.0 %collective-permute-start.4 = (bf16[1,1168,512]{2,1,0:T(8,128)(2,1)}, bf16[1,1168,512]{2,1,0:T(8,128)(2,1)}, u32[]{:S(2)}, u32[]{:S(2)}) collective-permute-start(bf16[1,1168,512]{2,1,0:T(8,128)(2,1)} %get-tuple-element.37.refs_0_), channel_id=1, source_target_pairs={{0,16},{16,0},{1,17},{17,1},{2,18},{18,2},{3,19},{19,3},{4,20},{20... | collective-permute-start | bytes 3588104 | tf_op jit(solution)/shard_map/ppermute | solution.py:474
  7.4 8.8 %shard_map.65 = (f32[8,96,256]{2,1,0:T(8,128)S(1)}, bf16[8,96,256]{2,1,0:T(8,128)(2,1)S(1)}, bf16[1552,512]{1,0:T(8,128)(2,1)}, s32[16]{0:T(128)}) custom-call(s32[31]{0:T(128)} %bitcast.23, s32[31]{0:T(128)} %bitcast.25, s32[31]{0:T(128)} %bitcast.27, s32[31]{0:T(128)} %bitcast.29, s32[16]{0:T(128)} %get-tuple-element.36.out_label, ...), custom_call_target="tpu_custom_call" | custom-call | flops 1610612736 | bytes 12189696 | tf_op jit(solution)/shard_map/pallas_call | solution.py:512
  16.2 0.0 copy-start.3
  16.2 0.0 copy-start.4
  16.2 0.1 collective-permute-start
  16.3 0.5 collective-permute-start.3
  16.8 1.2 collective-permute-done
  18.0 0.8 add_convert_fusion
  18.8 5.8 %all-to-all-start = ((bf16[8,96,256]{2,1,0:T(8,128)(2,1)}), bf16[8,96,256]{2,1,0:T(8,128)(2,1)S(1)}, u32[]{:S(2)}, u32[]{:S(2)}) async-start(bf16[8,96,256]{2,1,0:T(8,128)(2,1)} %add_convert_fusion), calls=%async_computation | async-start | bytes 786432 | tf_op jit(solution)/shard_map/all_to_all | solution.py:484
  24.7 9.4 %collective-permute-done.4.refs_0_ = bf16[1,1168,512]{2,1,0:T(8,128)(2,1)} collective-permute-done((bf16[1,1168,512]{2,1,0:T(8,128)(2,1)}, bf16[1,1168,512]{2,1,0:T(8,128)(2,1)}, u32[]{:S(2)}, u32[]{:S(2)}) %collective-permute-start.4) | collective-permute-done | bytes 1196064 | tf_op jit(solution)/shard_map/ppermute | solution.py:474
  34.0 0.0 collective-permute-start.5
  34.0 0.0 copy-done.3
  34.0 0.5 collective-permute-start.6
  34.5 2.1 %all-to-all-done = bf16[8,96,256]{2,1,0:T(8,128)(2,1)S(1)} async-done(((bf16[8,96,256]{2,1,0:T(8,128)(2,1)}), bf16[8,96,256]{2,1,0:T(8,128)(2,1)S(1)}, u32[]{:S(2)}, u32[]{:S(2)}) %all-to-all-start) | async-done | bytes 393248 | tf_op jit(solution)/shard_map/all_to_all | solution.py:484
  36.7 0.1 convert_reduce_fusion
  36.7 0.6 collective-permute-start.1
  37.3 3.5 %collective-permute-done.1.refs_1_ = f32[48,256]{1,0:T(8,128)S(1)} collective-permute-done((f32[48,256]{1,0:T(8,128)S(1)}, f32[48,256]{1,0:T(8,128)S(1)}, u32[]{:S(2)}, u32[]{:S(2)}) %collective-permute-start.1) | collective-permute-done | bytes 49184 | tf_op jit(solution)/shard_map/ppermute | solution.py:474
  40.9 0.7 shard_map.66
  41.6 0.0 copy-done.4
  41.6 0.6 collective-permute-start.2
  42.1 4.9 %all-to-all-start.1 = ((bf16[8,48,256]{2,1,0:T(8,128)(2,1)}), bf16[8,48,256]{2,1,0:T(8,128)(2,1)S(1)}, u32[]{:S(2)}, u32[]{:S(2)}) async-start(bf16[8,48,256]{2,1,0:T(8,128)(2,1)} %get-tuple-element.42), calls=%async_computation.1 | async-start | bytes 393216 | tf_op jit(solution)/shard_map/all_to_all | solution.py:484
  47.0 0.0 collective-permute-done.6.refs_3_
  47.0 0.0 collective-permute-done.3.pair_tiles
  47.0 0.0 collective-permute-done.5.refs_1_
  47.0 6.3 %shard_map.67 = (bf16[8,384,512]{2,1,0:T(8,128)(2,1)S(1)}, bf16[4096,256]{1,0:T(8,128)(2,1)S(1)}, s32[8,128]{1,0:T(8,128)}) custom-call(s32[16]{0:T(128)} %get-tuple-element.43.own_label, bf16[1552,512]{1,0:T(8,128)(2,1)} %get-tuple-element.44.tiles, bf16[1552,512]{1,0:T(8,128)(2,1)} %collective-permute-done.3.pair_tiles, ...), custom_call_target="tpu_custom_call" | custom-call | bytes 3145728 | tf_op jit(solution)/shard_map/pallas_call | solution.py:555
  53.4 0.0 copy-start
  53.4 1.6 %copy-done = bf16[8,384,512]{2,1,0:T(8,128)(2,1)} copy-done((bf16[8,384,512]{2,1,0:T(8,128)(2,1)}, bf16[8,384,512]{2,1,0:T(8,128)(2,1)S(1)}, u32[]{:S(2)}) %copy-start) | copy-done | bytes 3145752
  55.0 0.0 all-to-all-done.1
  55.0 0.0 collective-permute-done.2.late
  55.0 0.0 collective-permute-start.7
  55.0 1.7 %collective-permute-done.7.pair_late = bf16[1,384,512]{2,1,0:T(8,128)(2,1)S(1)} collective-permute-done((bf16[1,384,512]{2,1,0:T(8,128)(2,1)S(1)}, bf16[1,384,512]{2,1,0:T(8,128)(2,1)S(1)}, u32[]{:S(2)}, u32[]{:S(2)}) %collective-permute-start.7) | collective-permute-done | bytes 393248 | tf_op jit(solution)/shard_map/ppermute | solution.py:481
  56.7 0.0 copy-start.1
  56.7 1.9 %copy-done.1 = bf16[8,384,512]{2,1,0:T(8,128)(2,1)S(1)} copy-done((bf16[8,384,512]{2,1,0:T(8,128)(2,1)S(1)}, bf16[8,384,512]{2,1,0:T(8,128)(2,1)}, u32[]{:S(2)}) %copy-start.1) | copy-done | bytes 3145752
  58.6 0.0 copy-start.2
  58.6 0.7 copy-done.2
  59.3 3.6 %shard_map.68 = (bf16[384,256]{1,0:T(8,128)(2,1)S(1)}, bf16[8,384,512]{2,1,0:T(8,128)(2,1)S(1)}, f32[384,128]{1,0:T(8,128)S(1)}) custom-call(s32[8,128]{1,0:T(8,128)S(1)} %copy-done.2, bf16[384,256]{1,0:T(8,128)(2,1)S(1)} %bitcast.14, bf16[8,384,512]{2,1,0:T(8,128)(2,1)S(1)} %copy-done.1, bf16[1,384,512]{2,1,0:T(8,128)(2,1)S(1)} %collective-permute-done.2.late, ...), custom_call_target="tpu_custom_call" | custom-call | flops 1610612736 | bytes 10485760 | tf_op jit(solution)/shard_map/pallas_call | solution.py:586
  62.9 14.0 %all_to_all.45.got = bf16[8,48,256]{2,1,0:T(8,128)(2,1)S(1)} all-to-all(bf16[8,48,256]{2,1,0:T(8,128)(2,1)S(1)} %bitcast.15), channel_id=1, replica_groups={{0,2,4,6,8,10,12,14},{1,3,5,7,9,11,13,15},{16,18,20,22,24,26,28,30},{17..., dimensions={0} | all-to-all | bytes 393216 | tf_op jit(solution)/shard_map/all_to_all | solution.py:484
  76.9 0.2 shard_map.69
  77.1 10.7 %all_to_all.46 = bf16[8,48,256]{2,1,0:T(8,128)(2,1)S(1)} all-to-all(bf16[8,48,256]{2,1,0:T(8,128)(2,1)S(1)} %get-tuple-element.53), channel_id=1, replica_groups={{0,2,4,6,8,10,12,14},{1,3,5,7,9,11,13,15},{16,18,20,22,24,26,28,30},{17..., dimensions={0} | all-to-all | bytes 393216 | tf_op jit(solution)/shard_map/all_to_all | solution.py:484
  87.8 2.0 %shard_map.70 = bf16[384,256]{1,0:T(8,128)(2,1)S(1)} custom-call(bf16[384,256]{1,0:T(8,128)(2,1)S(1)} %bitcast.16, f32[384,128]{1,0:T(8,128)S(1)} %get-tuple-element.54.reg, bf16[8,384,512]{2,1,0:T(8,128)(2,1)S(1)} %get-tuple-element.55.plays, bf16[4096,256]{1,0:T(8,128)(2,1)S(1)} %get-tuple-element.50.factors), custom_call_target="tpu_custom_call" | custom-call | flops 1610612736 | bytes 5242880 | tf_op jit(solution)/shard_map/pallas_call | solution.py:601
  89.8 10.7 %all_to_all.47.got = bf16[8,48,256]{2,1,0:T(8,128)(2,1)S(1)} all-to-all(bf16[8,48,256]{2,1,0:T(8,128)(2,1)S(1)} %bitcast.17), channel_id=1, replica_groups={{0,2,4,6,8,10,12,14},{1,3,5,7,9,11,13,15},{16,18,20,22,24,26,28,30},{17..., dimensions={0} | all-to-all | bytes 393216 | tf_op jit(solution)/shard_map/all_to_all | solution.py:484
  100.5 0.2 shard_map.71
  100.7 10.5 %all_to_all.48 = bf16[8,48,256]{2,1,0:T(8,128)(2,1)S(1)} all-to-all(bf16[8,48,256]{2,1,0:T(8,128)(2,1)S(1)} %get-tuple-element.59), channel_id=1, replica_groups={{0,2,4,6,8,10,12,14},{1,3,5,7,9,11,13,15},{16,18,20,22,24,26,28,30},{17..., dimensions={0} | all-to-all | bytes 393216 | tf_op jit(solution)/shard_map/all_to_all | solution.py:484
  111.2 2.0 %shard_map.72 = bf16[384,256]{1,0:T(8,128)(2,1)S(1)} custom-call(bf16[384,256]{1,0:T(8,128)(2,1)S(1)} %bitcast.18, f32[384,128]{1,0:T(8,128)S(1)} %get-tuple-element.54.reg, bf16[8,384,512]{2,1,0:T(8,128)(2,1)S(1)} %get-tuple-element.55.plays, bf16[4096,256]{1,0:T(8,128)(2,1)S(1)} %get-tuple-element.50.factors), custom_call_target="tpu_custom_call" | custom-call | flops 1610612736 | bytes 5242880 | tf_op jit(solution)/shard_map/pallas_call | solution.py:601
  113.1 10.4 %all_to_all.49.got = bf16[8,48,256]{2,1,0:T(8,128)(2,1)S(1)} all-to-all(bf16[8,48,256]{2,1,0:T(8,128)(2,1)S(1)} %bitcast.19), channel_id=1, replica_groups={{0,2,4,6,8,10,12,14},{1,3,5,7,9,11,13,15},{16,18,20,22,24,26,28,30},{17..., dimensions={0} | all-to-all | bytes 393216 | tf_op jit(solution)/shard_map/all_to_all | solution.py:484
  123.5 0.4 shard_map.73
  123.9 10.2 %all_to_all.50 = bf16[8,48,256]{2,1,0:T(8,128)(2,1)S(1)} all-to-all(bf16[8,48,256]{2,1,0:T(8,128)(2,1)S(1)} %get-tuple-element.63), channel_id=1, replica_groups={{0,2,4,6,8,10,12,14},{1,3,5,7,9,11,13,15},{16,18,20,22,24,26,28,30},{17..., dimensions={0} | all-to-all | bytes 393216 | tf_op jit(solution)/shard_map/all_to_all | solution.py:484
  134.1 1.8 %shard_map.74 = f32[16,16,128]{2,1,0:T(8,128)S(1)} custom-call(bf16[384,256]{1,0:T(8,128)(2,1)S(1)} %bitcast.13, f32[384,128]{1,0:T(8,128)S(1)} %get-tuple-element.54.reg, f32[16,16,128]{2,1,0:T(8,128)S(1)} %get-tuple-element.64.base, bf16[8,384,512]{2,1,0:T(8,128)(2,1)S(1)} %get-tuple-element.55.plays, bf16[4096,256]{1,0:T(8,128)(2,1)S(1)} %get-tuple-element.50.factors), custom_call_target="tpu_custom_call" | custom-call | flops 805306368 | bytes 5242880 | tf_op jit(solution)/shard_map/pallas_call | solution.py:625
  135.9 10.5 %all_to_all.51.got = f32[16,16,128]{2,1,0:T(8,128)S(1)} all-to-all(f32[16,16,128]{2,1,0:T(8,128)S(1)} %shard_map.74), channel_id=1, replica_groups=mesh['user'=2,'item'=16] {'item'}, dimensions={0} | all-to-all | bytes 262144 | tf_op jit(solution)/shard_map/all_to_all | solution.py:634
  146.4 1.0 shard_map.75
  (1 shorter events, 0.0 us)
Async XLA Ops:
  4.4 29.6 %collective-permute-start.4 = (bf16[1,1168,512]{2,1,0:T(8,128)(2,1)}, bf16[1,1168,512]{2,1,0:T(8,128)(2,1)}, u32[]{:S(2)}, u32[]{:S(2)}) collective-permute-start(bf16[1,1168,512]{2,1,0:T(8,128)(2,1)} %get-tuple-element.37.refs_0_), channel_id=1, source_target_pairs={{0,16},{16,0},{1,17},{17,1},{2,18},{18,2},{3,19},{19,3},{4,20},{20... | collective-permute-start | bytes 3588104 | tf_op jit(solution)/shard_map/ppermute | solution.py:474
  16.2 17.8 %copy-start.3 = (bf16[2048,256]{1,0:T(8,128)(2,1)S(1)}, bf16[2048,256]{1,0:T(8,128)(2,1)}, u32[]{:S(2)}) copy-start(bf16[2048,256]{1,0:T(8,128)(2,1)} %refs_2_.3) | copy-start | bytes 3145732
  16.2 25.4 %copy-start.4 = (bf16[1,384,512]{2,1,0:T(8,128)(2,1)S(1)}, bf16[1,384,512]{2,1,0:T(8,128)(2,1)}, u32[]{:S(2)}) copy-start(bf16[1,384,512]{2,1,0:T(8,128)(2,1)} %get-tuple-element.41.refs_1_) | copy-start | bytes 1179652
  16.2 1.8 %collective-permute-start = (bf16[8,96,256]{2,1,0:T(8,128)(2,1)S(1)}, bf16[8,96,256]{2,1,0:T(8,128)(2,1)S(1)}, u32[]{:S(2)}, u32[]{:S(2)}) collective-permute-start(bf16[8,96,256]{2,1,0:T(8,128)(2,1)S(1)} %get-tuple-element.39), channel_id=1, source_target_pairs={{0,1},{1,0},{2,3},{3,2},{4,5},{5,4},{6,7},{7,6},{8,9},{9,8},{10,11... | collective-permute-start | bytes 1179656 | tf_op jit(solution)/shard_map/ppermute | solution.py:481
  16.3 30.7 %collective-permute-start.3 = (bf16[1552,512]{1,0:T(8,128)(2,1)}, bf16[1552,512]{1,0:T(8,128)(2,1)}, u32[]{:S(2)}, u32[]{:S(2)}) collective-permute-start(bf16[1552,512]{1,0:T(8,128)(2,1)} %get-tuple-element.44.tiles), channel_id=1, source_target_pairs={{0,1},{1,0},{2,3},{3,2},{4,5},{5,4},{6,7},{7,6},{8,9},{9,8},{10,11... | collective-permute-start | bytes 4767752 | tf_op jit(solution)/shard_map/ppermute | solution.py:481
  18.8 17.8 %all-to-all-start = ((bf16[8,96,256]{2,1,0:T(8,128)(2,1)}), bf16[8,96,256]{2,1,0:T(8,128)(2,1)S(1)}, u32[]{:S(2)}, u32[]{:S(2)}) async-start(bf16[8,96,256]{2,1,0:T(8,128)(2,1)} %add_convert_fusion), calls=%async_computation | async-start | bytes 786432 | tf_op jit(solution)/shard_map/all_to_all | solution.py:484
  34.0 13.0 %collective-permute-start.5 = (bf16[1,1168,512]{2,1,0:T(8,128)(2,1)}, bf16[1,1168,512]{2,1,0:T(8,128)(2,1)}, u32[]{:S(2)}, u32[]{:S(2)}) collective-permute-start(bf16[1,1168,512]{2,1,0:T(8,128)(2,1)} %collective-permute-done.4.refs_0_), channel_id=1, source_target_pairs={{0,1},{1,0},{2,3},{3,2},{4,5},{5,4},{6,7},{7,6},{8,9},{9,8},{10,11... | collective-permute-start | bytes 3588104 | tf_op jit(solution)/shard_map/ppermute | solution.py:481
  34.0 13.0 %collective-permute-start.6 = (bf16[2048,256]{1,0:T(8,128)(2,1)S(1)}, bf16[2048,256]{1,0:T(8,128)(2,1)}, u32[]{:S(2)}, u32[]{:S(2)}) collective-permute-start(bf16[2048,256]{1,0:T(8,128)(2,1)S(1)} %copy-done.3), channel_id=1, source_target_pairs={{0,1},{1,0},{2,3},{3,2},{4,5},{5,4},{6,7},{7,6},{8,9},{9,8},{10,11... | collective-permute-start | bytes 3145736 | tf_op jit(solution)/shard_map/ppermute | solution.py:481
  36.7 4.2 %collective-permute-start.1 = (f32[48,256]{1,0:T(8,128)S(1)}, f32[48,256]{1,0:T(8,128)S(1)}, u32[]{:S(2)}, u32[]{:S(2)}) collective-permute-start(f32[48,256]{1,0:T(8,128)S(1)} %get-tuple-element.65), channel_id=1, source_target_pairs={{0,16},{16,0},{1,17},{17,1},{2,18},{18,2},{3,19},{19,3},{4,20},{20... | collective-permute-start | bytes 147464 | tf_op jit(solution)/shard_map/ppermute | solution.py:474
  41.6 13.4 %collective-permute-start.2 = (bf16[1,384,512]{2,1,0:T(8,128)(2,1)S(1)}, bf16[1,384,512]{2,1,0:T(8,128)(2,1)S(1)}, u32[]{:S(2)}, u32[]{:S(2)}) collective-permute-start(bf16[1,384,512]{2,1,0:T(8,128)(2,1)S(1)} %copy-done.4), channel_id=1, source_target_pairs={{0,16},{16,0},{1,17},{17,1},{2,18},{18,2},{3,19},{19,3},{4,20},{20... | collective-permute-start | bytes 1179656 | tf_op jit(solution)/shard_map/ppermute | solution.py:474
  42.1 12.9 %all-to-all-start.1 = ((bf16[8,48,256]{2,1,0:T(8,128)(2,1)}), bf16[8,48,256]{2,1,0:T(8,128)(2,1)S(1)}, u32[]{:S(2)}, u32[]{:S(2)}) async-start(bf16[8,48,256]{2,1,0:T(8,128)(2,1)} %get-tuple-element.42), calls=%async_computation.1 | async-start | bytes 393216 | tf_op jit(solution)/shard_map/all_to_all | solution.py:484
  53.4 1.6 %copy-start = (bf16[8,384,512]{2,1,0:T(8,128)(2,1)}, bf16[8,384,512]{2,1,0:T(8,128)(2,1)S(1)}, u32[]{:S(2)}) copy-start(bf16[8,384,512]{2,1,0:T(8,128)(2,1)S(1)} %get-tuple-element.48.placed) | copy-start | bytes 9437188
  55.0 1.7 %collective-permute-start.7 = (bf16[1,384,512]{2,1,0:T(8,128)(2,1)S(1)}, bf16[1,384,512]{2,1,0:T(8,128)(2,1)S(1)}, u32[]{:S(2)}, u32[]{:S(2)}) collective-permute-start(bf16[1,384,512]{2,1,0:T(8,128)(2,1)S(1)} %collective-permute-done.2.late), channel_id=1, source_target_pairs={{0,1},{1,0},{2,3},{3,2},{4,5},{5,4},{6,7},{7,6},{8,9},{9,8},{10,11... | collective-permute-start | bytes 1179656 | tf_op jit(solution)/shard_map/ppermute | solution.py:481
  56.7 1.9 %copy-start.1 = (bf16[8,384,512]{2,1,0:T(8,128)(2,1)S(1)}, bf16[8,384,512]{2,1,0:T(8,128)(2,1)}, u32[]{:S(2)}) copy-start(bf16[8,384,512]{2,1,0:T(8,128)(2,1)} %copy-done) | copy-start | bytes 9437188
  58.6 0.7 copy-start.2

commit v3 on v2

--- a/solution.py
+++ b/solution.py
@@ -25,11 +25,10 @@
 
 
 def log_tile(counts, rows, cols):
-    rank_rows = lax.broadcasted_iota(jnp.int32, counts.shape, 0)
-    rank_cols = lax.broadcasted_iota(jnp.int32, counts.shape, 1)
-    inside = (rank_rows < rows) & (rank_cols < cols)
-    values = jnp.log(1.0 + counts.astype(F32) / EPS)
-    return jnp.where(inside, values, 0.0).astype(BF16)
+    height, width = counts.shape
+    in_rows = (lax.broadcasted_iota(jnp.int32, (height, 1), 0) < rows).astype(F32)
+    in_cols = (lax.broadcasted_iota(jnp.int32, (1, width), 1) < cols).astype(F32)
+    return jnp.log(1.0 + counts.astype(F32) / EPS * in_cols * in_rows).astype(BF16)
 
 
 def start_tiles(n_user, cap, own, owner, cell, counts, label, slots, fill, buf, sems):
@@ -243,8 +242,10 @@
         read.start()
     plays[...] = jnp.zeros_like(plays)
 
-    def both(act):
+    def own(act):
         place_tiles(act, tiles, lambda k: own_label[k], cap, plays, 0, sems, 0)
+
+    def others(act):
         place_tiles(act, pair_tiles, lambda k: labels[0, k], cap, plays, CBLK, sems, cap)
         base = 2 * cap
         for side, group in enumerate((parts, pair_parts)):
@@ -257,6 +258,7 @@
                     low += size
                     base += size
 
+    own(lambda copy: copy.start())
     for i, read in enumerate(reads):
         read.wait()
         whole[i : i + 1, :] = raw[i].astype(F32)[0:1, :].astype(jnp.int32)
@@ -266,8 +268,9 @@
     stacked[:items, :] = factors[...]
     stacked[items:, :] = pair_factors[...]
     to_scalars.wait()
-    both(lambda copy: copy.start())
-    both(lambda copy: copy.wait())
+    others(lambda copy: copy.start())
+    own(lambda copy: copy.wait())
+    others(lambda copy: copy.wait())
 
 
 def start_kernel(*refs):
@@ -537,6 +540,7 @@
     summed = exchange((keep + to_pair(send).astype(F32)).astype(BF16))
     pair_own = to_pair(own)
     summed = jnp.sum(summed.astype(F32), axis=0).reshape(n_user, chunk, rank)
+    last_part, summed = lax.optimization_barrier((parts[-1], summed))
     terms = [summed[0]] + [over_users(summed[s], s) for s in range(1, n_user)]
     direction, spread = call(
         start_kernel,
@@ -546,7 +550,6 @@
         4,
     )(*terms)
     residual = folded = direction
-    last_part, spread = lax.optimization_barrier((parts[-1], spread))
     late = from_users(last_part)
     pair_parts = [to_pair(part) for part in far]
     plays_shape = (blocks, half, width)
@@ -556,7 +559,7 @@
         functools.partial(place_kernel, cap, sizes),
         [SMEM] + [HBM] * (2 + 2 * len(far)) + [VMEM] * 2,
         [
-            (pltpu.VMEM(plays_shape, BF16), VMEM),
+            (shape(plays_shape, BF16), VMEM),
             (pltpu.VMEM((HALVES * shard_items, rank), BF16), VMEM),
             (shape(label_shape, jnp.int32), SMEM),
         ],

time: 148 us -> 147 us (level)
    unnamed x10 -> x8, local copies, waits for them, and re-layouts: 4.22 us -> 3.06 us
where the time goes in v3:
time: 147 us; the launch traced here: 146 us
  blocking collectives  76.9 us (52%)
  Pallas kernels  31.9 us (22%)
  waiting for transfers between devices  17.3 us (12%)
  starting transfers between devices  15.4 us (10%)
  local copies, waits for them, and re-layouts  3.07 us (2%)
    all_to_all x6, blocking collectives, exchange(): return lax.all_to_all(x, 'item', 0, 0, axis_index_groups=groups, tiled=True)  66.4 us
    ppermute x3, waiting for transfers between devices, over_users(): lax.ppermute(x, 'user', [(u, (u + shift) % n_user) for u in range(n_user)])  11.9 us
    all_to_all x1, blocking collectives, shards(): got = lax.all_to_all(payload, 'item', 0, 0, tiled=True)  10.5 us
    all_to_all x2, starting transfers between devices, exchange(): return lax.all_to_all(x, 'item', 0, 0, axis_index_groups=groups, tiled=True)  9.26 us
    pallas_call x1, Pallas kernels, shards(): call(functools.partial(rhs_kernel, n_user, cap, sizes), [SMEM] * 5 + [HBM...  9 us
    pallas_call x1, Pallas kernels, shards(): call(functools.partial(place_kernel, cap, sizes), [SMEM] + [HBM] * (2 + 2...  6.48 us
    ppermute x3, starting transfers between devices, over_users(): lax.ppermute(x, 'user', [(u, (u + shift) % n_user) for u in range(n_user)])  5.02 us
    pallas_call x1, Pallas kernels, shards(): call(functools.partial(pack_kernel, n_user, cap, sizes), [SMEM] * 4 + [HB...  4.4 us
  transfers between devices with their start and end apart: 10, of which 5 were waited for; matrix products, arithmetic and copies ran while one was open for 1% of the time, Pallas kernels for 11%

profile of v3, /device:TPU:0, one launch (start us, length us, event | category | flops | bytes accessed | tf_op | source)
XLA Modules:
  0.0 145.7 jit_solution(3974103711104650154)
XLA Ops:
  0.0 4.4 %shard_map.64 = (bf16[1,1168,512]{2,1,0:T(8,128)(2,1)}, bf16[1,384,512]{2,1,0:T(8,128)(2,1)}, s32[16]{0:T(128)}) custom-call(s32[31]{0:T(128)} %bitcast.28, s32[31]{0:T(128)} %bitcast.30, s32[31]{0:T(128)} %bitcast.32, s32[31]{0:T(128)} %bitcast.34, s32[31,96,512]{2,1,0:T(8,128)} %bitcast.25), custom_call_target="tpu_custom_call" | custom-call | bytes 4718592 | tf_op jit(solution)/shard_map/pallas_call | solution.py:494
  4.4 2.9 %collective-permute-start.4 = (bf16[1,1168,512]{2,1,0:T(8,128)(2,1)}, bf16[1,1168,512]{2,1,0:T(8,128)(2,1)}, u32[]{:S(2)}, u32[]{:S(2)}) collective-permute-start(bf16[1,1168,512]{2,1,0:T(8,128)(2,1)} %get-tuple-element.37.refs_0_), channel_id=1, source_target_pairs={{0,16},{16,0},{1,17},{17,1},{2,18},{18,2},{3,19},{19,3},{4,20},{20... | collective-permute-start | bytes 3588104 | tf_op jit(solution)/shard_map/ppermute | solution.py:477
  7.3 9.0 %shard_map.65 = (f32[8,96,256]{2,1,0:T(8,128)S(1)}, bf16[8,96,256]{2,1,0:T(8,128)(2,1)S(1)}, bf16[1552,512]{1,0:T(8,128)(2,1)}, s32[16]{0:T(128)}) custom-call(s32[31]{0:T(128)} %bitcast.29, s32[31]{0:T(128)} %bitcast.31, s32[31]{0:T(128)} %bitcast.33, s32[31]{0:T(128)} %bitcast.35, s32[16]{0:T(128)} %get-tuple-element.36.out_label, ...), custom_call_target="tpu_custom_call" | custom-call | flops 1610612736 | bytes 12189696 | tf_op jit(solution)/shard_map/pallas_call | solution.py:515
  16.3 0.0 copy-start
  16.4 0.1 collective-permute-start
  16.4 0.5 collective-permute-start.3
  16.9 1.2 collective-permute-done
  18.1 0.0 copy-start.2
  18.2 0.9 add_convert_fusion
  19.0 5.9 %all-to-all-start = ((bf16[8,96,256]{2,1,0:T(8,128)(2,1)}), bf16[8,96,256]{2,1,0:T(8,128)(2,1)S(1)}, u32[]{:S(2)}, u32[]{:S(2)}) async-start(bf16[8,96,256]{2,1,0:T(8,128)(2,1)} %add_convert_fusion), calls=%async_computation | async-start | bytes 786432 | tf_op jit(solution)/shard_map/all_to_all | solution.py:487
  24.9 9.2 %collective-permute-done.4.refs_0_ = bf16[1,1168,512]{2,1,0:T(8,128)(2,1)} collective-permute-done((bf16[1,1168,512]{2,1,0:T(8,128)(2,1)}, bf16[1,1168,512]{2,1,0:T(8,128)(2,1)}, u32[]{:S(2)}, u32[]{:S(2)}) %collective-permute-start.4) | collective-permute-done | bytes 1196064 | tf_op jit(solution)/shard_map/ppermute | solution.py:477
  34.1 0.0 collective-permute-start.5
  34.1 0.0 copy-done
  34.1 0.5 collective-permute-start.6
  34.6 2.3 %all-to-all-done = bf16[8,96,256]{2,1,0:T(8,128)(2,1)S(1)} async-done(((bf16[8,96,256]{2,1,0:T(8,128)(2,1)}), bf16[8,96,256]{2,1,0:T(8,128)(2,1)S(1)}, u32[]{:S(2)}, u32[]{:S(2)}) %all-to-all-start) | async-done | bytes 393248 | tf_op jit(solution)/shard_map/all_to_all | solution.py:487
  36.9 0.1 convert_reduce_fusion
  36.9 0.6 collective-permute-start.2
  37.5 1.5 %collective-permute-start.1 = (bf16[1,384,512]{2,1,0:T(8,128)(2,1)}, bf16[1,384,512]{2,1,0:T(8,128)(2,1)}, u32[]{:S(2)}, u32[]{:S(2)}) collective-permute-start(bf16[1,384,512]{2,1,0:T(8,128)(2,1)} %get-tuple-element.40.refs_1_), channel_id=1, source_target_pairs={{0,16},{16,0},{1,17},{17,1},{2,18},{18,2},{3,19},{19,3},{4,20},{20... | collective-permute-start | bytes 1179656 | tf_op jit(solution)/shard_map/ppermute | solution.py:477
  39.0 2.7 %collective-permute-done.2.refs_1_ = f32[48,256]{1,0:T(8,128)S(1)} collective-permute-done((f32[48,256]{1,0:T(8,128)S(1)}, f32[48,256]{1,0:T(8,128)S(1)}, u32[]{:S(2)}, u32[]{:S(2)}) %collective-permute-start.2) | collective-permute-done | bytes 49184 | tf_op jit(solution)/shard_map/ppermute | solution.py:477
  41.7 0.7 shard_map.66
  42.4 3.4 %all-to-all-start.1 = ((bf16[8,48,256]{2,1,0:T(8,128)(2,1)}), bf16[8,48,256]{2,1,0:T(8,128)(2,1)S(1)}, u32[]{:S(2)}, u32[]{:S(2)}) async-start(bf16[8,48,256]{2,1,0:T(8,128)(2,1)} %get-tuple-element.42), calls=%async_computation.1 | async-start | bytes 393216 | tf_op jit(solution)/shard_map/all_to_all | solution.py:487
  45.8 0.0 collective-permute-done.6.refs_3_
  45.8 0.0 collective-permute-done.3.pair_tiles
  45.8 0.0 copy-start.3
  45.8 0.0 collective-permute-done.5.refs_1_
  45.8 1.2 copy-done.3
  47.0 0.0 copy-done.2
  47.0 6.5 %shard_map.67 = (bf16[8,384,512]{2,1,0:T(8,128)(2,1)}, bf16[4096,256]{1,0:T(8,128)(2,1)S(1)}, s32[8,128]{1,0:T(8,128)S(1)}) custom-call(s32[16]{0:T(128)S(1)} %copy-done.2, bf16[1552,512]{1,0:T(8,128)(2,1)} %get-tuple-element.44.tiles, bf16[1552,512]{1,0:T(8,128)(2,1)} %copy-done.3, bf16[1,1168,512]{2,1,0:T(8,128)(2,1)} %collective-permute-done.4.refs_0_, ...), custom_call_target="tpu_custom_call" | custom-call | bytes 3145728 | tf_op jit(solution)/shard_map/pallas_call | solution.py:558
  53.5 0.0 collective-permute-done.1.late
  53.5 0.0 all-to-all-done.1
  53.5 0.1 collective-permute-start.7
  53.6 1.9 %collective-permute-done.7.pair_late = bf16[1,384,512]{2,1,0:T(8,128)(2,1)S(1)} collective-permute-done((bf16[1,384,512]{2,1,0:T(8,128)(2,1)}, bf16[1,384,512]{2,1,0:T(8,128)(2,1)S(1)}, u32[]{:S(2)}, u32[]{:S(2)}) %collective-permute-start.7) | collective-permute-done | bytes 393248 | tf_op jit(solution)/shard_map/ppermute | solution.py:484
  55.5 0.0 copy-start.1
  55.5 1.9 %copy-done.1 = bf16[8,384,512]{2,1,0:T(8,128)(2,1)S(1)} copy-done((bf16[8,384,512]{2,1,0:T(8,128)(2,1)S(1)}, bf16[8,384,512]{2,1,0:T(8,128)(2,1)}, u32[]{:S(2)}) %copy-start.1) | copy-done | bytes 3145752
  57.4 4.0 %shard_map.68 = (bf16[384,256]{1,0:T(8,128)(2,1)S(1)}, bf16[8,384,512]{2,1,0:T(8,128)(2,1)S(1)}, f32[384,128]{1,0:T(8,128)S(1)}) custom-call(s32[8,128]{1,0:T(8,128)S(1)} %get-tuple-element.46.labels, bf16[384,256]{1,0:T(8,128)(2,1)S(1)} %bitcast.19, bf16[8,384,512]{2,1,0:T(8,128)(2,1)S(1)} %copy-done.1, bf16[1,384,512]{2,1,0:T(8,128)(2,1)} %collective-permute-done.1.late, ...), custom_call_target="tpu_custom_call" | custom-call | flops 1610612736 | bytes 10485760 | tf_op jit(solution)/shard_map/pallas_call | solution.py:589
  61.4 13.9 %all_to_all.45.got = bf16[8,48,256]{2,1,0:T(8,128)(2,1)S(1)} all-to-all(bf16[8,48,256]{2,1,0:T(8,128)(2,1)S(1)} %bitcast.20), channel_id=1, replica_groups={{0,2,4,6,8,10,12,14},{1,3,5,7,9,11,13,15},{16,18,20,22,24,26,28,30},{17..., dimensions={0} | all-to-all | bytes 393216 | tf_op jit(solution)/shard_map/all_to_all | solution.py:487
  75.3 0.2 shard_map.69
  75.5 10.7 %all_to_all.46 = bf16[8,48,256]{2,1,0:T(8,128)(2,1)S(1)} all-to-all(bf16[8,48,256]{2,1,0:T(8,128)(2,1)S(1)} %get-tuple-element.53), channel_id=1, replica_groups={{0,2,4,6,8,10,12,14},{1,3,5,7,9,11,13,15},{16,18,20,22,24,26,28,30},{17..., dimensions={0} | all-to-all | bytes 393216 | tf_op jit(solution)/shard_map/all_to_all | solution.py:487
  86.2 1.9 %shard_map.70 = bf16[384,256]{1,0:T(8,128)(2,1)S(1)} custom-call(bf16[384,256]{1,0:T(8,128)(2,1)S(1)} %bitcast.21, f32[384,128]{1,0:T(8,128)S(1)} %get-tuple-element.54.reg, bf16[8,384,512]{2,1,0:T(8,128)(2,1)S(1)} %get-tuple-element.55.plays, bf16[4096,256]{1,0:T(8,128)(2,1)S(1)} %get-tuple-element.50.factors), custom_call_target="tpu_custom_call" | custom-call | flops 1610612736 | bytes 5242880 | tf_op jit(solution)/shard_map/pallas_call | solution.py:604
  88.2 10.7 %all_to_all.47.got = bf16[8,48,256]{2,1,0:T(8,128)(2,1)S(1)} all-to-all(bf16[8,48,256]{2,1,0:T(8,128)(2,1)S(1)} %bitcast.22), channel_id=1, replica_groups={{0,2,4,6,8,10,12,14},{1,3,5,7,9,11,13,15},{16,18,20,22,24,26,28,30},{17..., dimensions={0} | all-to-all | bytes 393216 | tf_op jit(solution)/shard_map/all_to_all | solution.py:487
  98.8 0.2 shard_map.71
  99.0 10.5 %all_to_all.48 = bf16[8,48,256]{2,1,0:T(8,128)(2,1)S(1)} all-to-all(bf16[8,48,256]{2,1,0:T(8,128)(2,1)S(1)} %get-tuple-element.59), channel_id=1, replica_groups={{0,2,4,6,8,10,12,14},{1,3,5,7,9,11,13,15},{16,18,20,22,24,26,28,30},{17..., dimensions={0} | all-to-all | bytes 393216 | tf_op jit(solution)/shard_map/all_to_all | solution.py:487
  109.5 1.9 %shard_map.72 = bf16[384,256]{1,0:T(8,128)(2,1)S(1)} custom-call(bf16[384,256]{1,0:T(8,128)(2,1)S(1)} %bitcast.23, f32[384,128]{1,0:T(8,128)S(1)} %get-tuple-element.54.reg, bf16[8,384,512]{2,1,0:T(8,128)(2,1)S(1)} %get-tuple-element.55.plays, bf16[4096,256]{1,0:T(8,128)(2,1)S(1)} %get-tuple-element.50.factors), custom_call_target="tpu_custom_call" | custom-call | flops 1610612736 | bytes 5242880 | tf_op jit(solution)/shard_map/pallas_call | solution.py:604
  111.5 10.4 %all_to_all.49.got = bf16[8,48,256]{2,1,0:T(8,128)(2,1)S(1)} all-to-all(bf16[8,48,256]{2,1,0:T(8,128)(2,1)S(1)} %bitcast.24), channel_id=1, replica_groups={{0,2,4,6,8,10,12,14},{1,3,5,7,9,11,13,15},{16,18,20,22,24,26,28,30},{17..., dimensions={0} | all-to-all | bytes 393216 | tf_op jit(solution)/shard_map/all_to_all | solution.py:487
  121.8 0.4 shard_map.73
  122.2 10.2 %all_to_all.50 = bf16[8,48,256]{2,1,0:T(8,128)(2,1)S(1)} all-to-all(bf16[8,48,256]{2,1,0:T(8,128)(2,1)S(1)} %get-tuple-element.63), channel_id=1, replica_groups={{0,2,4,6,8,10,12,14},{1,3,5,7,9,11,13,15},{16,18,20,22,24,26,28,30},{17..., dimensions={0} | all-to-all | bytes 393216 | tf_op jit(solution)/shard_map/all_to_all | solution.py:487
  132.4 1.7 %shard_map.74 = f32[16,16,128]{2,1,0:T(8,128)S(1)} custom-call(bf16[384,256]{1,0:T(8,128)(2,1)S(1)} %bitcast.18, f32[384,128]{1,0:T(8,128)S(1)} %get-tuple-element.54.reg, f32[16,16,128]{2,1,0:T(8,128)S(1)} %get-tuple-element.64.base, bf16[8,384,512]{2,1,0:T(8,128)(2,1)S(1)} %get-tuple-element.55.plays, bf16[4096,256]{1,0:T(8,128)(2,1)S(1)} %get-tuple-element.50.factors), custom_call_target="tpu_custom_call" | custom-call | flops 805306368 | bytes 5242880 | tf_op jit(solution)/shard_map/pallas_call | solution.py:628
  134.1 10.5 %all_to_all.51.got = f32[16,16,128]{2,1,0:T(8,128)S(1)} all-to-all(f32[16,16,128]{2,1,0:T(8,128)S(1)} %shard_map.74), channel_id=1, replica_groups=mesh['user'=2,'item'=16] {'item'}, dimensions={0} | all-to-all | bytes 262144 | tf_op jit(solution)/shard_map/all_to_all | solution.py:637
  144.7 1.0 shard_map.75
  (1 shorter events, 0.0 us)
Async XLA Ops:
  4.4 29.7 %collective-permute-start.4 = (bf16[1,1168,512]{2,1,0:T(8,128)(2,1)}, bf16[1,1168,512]{2,1,0:T(8,128)(2,1)}, u32[]{:S(2)}, u32[]{:S(2)}) collective-permute-start(bf16[1,1168,512]{2,1,0:T(8,128)(2,1)} %get-tuple-element.37.refs_0_), channel_id=1, source_target_pairs={{0,16},{16,0},{1,17},{17,1},{2,18},{18,2},{3,19},{19,3},{4,20},{20... | collective-permute-start | bytes 3588104 | tf_op jit(solution)/shard_map/ppermute | solution.py:477
  16.3 17.7 %copy-start = (bf16[2048,256]{1,0:T(8,128)(2,1)S(1)}, bf16[2048,256]{1,0:T(8,128)(2,1)}, u32[]{:S(2)}) copy-start(bf16[2048,256]{1,0:T(8,128)(2,1)} %refs_2_.3) | copy-start | bytes 3145732
  16.4 1.8 %collective-permute-start = (bf16[8,96,256]{2,1,0:T(8,128)(2,1)S(1)}, bf16[8,96,256]{2,1,0:T(8,128)(2,1)S(1)}, u32[]{:S(2)}, u32[]{:S(2)}) collective-permute-start(bf16[8,96,256]{2,1,0:T(8,128)(2,1)S(1)} %get-tuple-element.39), channel_id=1, source_target_pairs={{0,1},{1,0},{2,3},{3,2},{4,5},{5,4},{6,7},{7,6},{8,9},{9,8},{10,11... | collective-permute-start | bytes 1179656 | tf_op jit(solution)/shard_map/ppermute | solution.py:484
  16.4 29.3 %collective-permute-start.3 = (bf16[1552,512]{1,0:T(8,128)(2,1)}, bf16[1552,512]{1,0:T(8,128)(2,1)S(1)}, u32[]{:S(2)}, u32[]{:S(2)}) collective-permute-start(bf16[1552,512]{1,0:T(8,128)(2,1)} %get-tuple-element.44.tiles), channel_id=1, source_target_pairs={{0,1},{1,0},{2,3},{3,2},{4,5},{5,4},{6,7},{7,6},{8,9},{9,8},{10,11... | collective-permute-start | bytes 4767752 | tf_op jit(solution)/shard_map/ppermute | solution.py:484
  18.1 28.8 %copy-start.2 = (s32[16]{0:T(128)S(1)}, s32[16]{0:T(128)}, u32[]{:S(2)}) copy-start(s32[16]{0:T(128)} %get-tuple-element.43.own_label) | copy-start | bytes 196
  19.0 17.9 %all-to-all-start = ((bf16[8,96,256]{2,1,0:T(8,128)(2,1)}), bf16[8,96,256]{2,1,0:T(8,128)(2,1)S(1)}, u32[]{:S(2)}, u32[]{:S(2)}) async-start(bf16[8,96,256]{2,1,0:T(8,128)(2,1)} %add_convert_fusion), calls=%async_computation | async-start | bytes 786432 | tf_op jit(solution)/shard_map/all_to_all | solution.py:487
  34.1 11.7 %collective-permute-start.5 = (bf16[1,1168,512]{2,1,0:T(8,128)(2,1)}, bf16[1,1168,512]{2,1,0:T(8,128)(2,1)}, u32[]{:S(2)}, u32[]{:S(2)}) collective-permute-start(bf16[1,1168,512]{2,1,0:T(8,128)(2,1)} %collective-permute-done.4.refs_0_), channel_id=1, source_target_pairs={{0,1},{1,0},{2,3},{3,2},{4,5},{5,4},{6,7},{7,6},{8,9},{9,8},{10,11... | collective-permute-start | bytes 3588104 | tf_op jit(solution)/shard_map/ppermute | solution.py:484
  34.1 11.7 %collective-permute-start.6 = (bf16[2048,256]{1,0:T(8,128)(2,1)S(1)}, bf16[2048,256]{1,0:T(8,128)(2,1)}, u32[]{:S(2)}, u32[]{:S(2)}) collective-permute-start(bf16[2048,256]{1,0:T(8,128)(2,1)S(1)} %copy-done), channel_id=1, source_target_pairs={{0,1},{1,0},{2,3},{3,2},{4,5},{5,4},{6,7},{7,6},{8,9},{9,8},{10,11... | collective-permute-start | bytes 3145736 | tf_op jit(solution)/shard_map/ppermute | solution.py:484
  36.9 4.7 %collective-permute-start.2 = (f32[48,256]{1,0:T(8,128)S(1)}, f32[48,256]{1,0:T(8,128)S(1)}, u32[]{:S(2)}, u32[]{:S(2)}) collective-permute-start(f32[48,256]{1,0:T(8,128)S(1)} %get-tuple-element.65), channel_id=1, source_target_pairs={{0,16},{16,0},{1,17},{17,1},{2,18},{18,2},{3,19},{19,3},{4,20},{20... | collective-permute-start | bytes 147464 | tf_op jit(solution)/shard_map/ppermute | solution.py:477
  37.5 15.9 %collective-permute-start.1 = (bf16[1,384,512]{2,1,0:T(8,128)(2,1)}, bf16[1,384,512]{2,1,0:T(8,128)(2,1)}, u32[]{:S(2)}, u32[]{:S(2)}) collective-permute-start(bf16[1,384,512]{2,1,0:T(8,128)(2,1)} %get-tuple-element.40.refs_1_), channel_id=1, source_target_pairs={{0,16},{16,0},{1,17},{17,1},{2,18},{18,2},{3,19},{19,3},{4,20},{20... | collective-permute-start | bytes 1179656 | tf_op jit(solution)/shard_map/ppermute | solution.py:477
  42.4 11.1 %all-to-all-start.1 = ((bf16[8,48,256]{2,1,0:T(8,128)(2,1)}), bf16[8,48,256]{2,1,0:T(8,128)(2,1)S(1)}, u32[]{:S(2)}, u32[]{:S(2)}) async-start(bf16[8,48,256]{2,1,0:T(8,128)(2,1)} %get-tuple-element.42), calls=%async_computation.1 | async-start | bytes 393216 | tf_op jit(solution)/shard_map/all_to_all | solution.py:487
  45.8 1.2 copy-start.3
  53.5 2.0 %collective-permute-start.7 = (bf16[1,384,512]{2,1,0:T(8,128)(2,1)}, bf16[1,384,512]{2,1,0:T(8,128)(2,1)S(1)}, u32[]{:S(2)}, u32[]{:S(2)}) collective-permute-start(bf16[1,384,512]{2,1,0:T(8,128)(2,1)} %collective-permute-done.1.late), channel_id=1, source_target_pairs={{0,1},{1,0},{2,3},{3,2},{4,5},{5,4},{6,7},{7,6},{8,9},{9,8},{10,11... | collective-permute-start | bytes 1179656 | tf_op jit(solution)/shard_map/ppermute | solution.py:484
  55.5 1.9 %copy-start.1 = (bf16[8,384,512]{2,1,0:T(8,128)(2,1)S(1)}, bf16[8,384,512]{2,1,0:T(8,128)(2,1)}, u32[]{:S(2)}) copy-start(bf16[8,384,512]{2,1,0:T(8,128)(2,1)} %get-tuple-element.48.placed) | copy-start | bytes 9437188

commit v4 on v3

--- a/solution.py
+++ b/solution.py
@@ -120,7 +120,7 @@
 def rhs_kernel(n_user, cap, sizes, owner, cell, rows, cols, out_label, counts, *refs):
     n = len(sizes)
     parts, (factors, keep, send, tiles, label), bufs = refs[:n], refs[n : n + 5], refs[n + 5 : n + 5 + n]
-    slots, fill, buf, logs, dense, sems, out_sems, part_sems = refs[n + 5 + n :]
+    slots, fill, buf, logs, dense, items, sems, out_sems, part_sems, item_sem = refs[n + 5 + n :]
     start_tiles(n_user, cap, True, owner, cell, counts, label, slots, fill, buf, sems)
     height, width = counts.shape[1], counts.shape[2]
     half = HG * height
@@ -131,6 +131,8 @@
     ]
     for move in moves:
         move.start()
+    item_copy = pltpu.make_async_copy(factors, items, item_sem)
+    item_copy.start()
     dense[...] = jnp.zeros_like(dense)
 
     def put(tile, shift, where):
@@ -189,13 +191,14 @@
         return carry
 
     lax.fori_loop(0, cap, work_own, 0)
+    item_copy.wait()
     n_chunk = keep.shape[0]
     chunk = half // n_chunk
     for side, target in ((1, send), (0, keep)):
 
         def dots(s, carry, side=side, target=target):
             row = pl.multiple_of((side * n_user + s) * half, 16)
-            part = jnp.dot(dense[pl.ds(row, half), :], factors[...], preferred_element_type=F32)
+            part = jnp.dot(dense[pl.ds(row, half), :], items[...], preferred_element_type=F32)
             at = pl.ds(pl.multiple_of(s * chunk, 8), chunk)
             for k in range(n_chunk):
                 target[k, at, :] = part[k * chunk : (k + 1) * chunk, :].astype(target.dtype)
@@ -206,7 +209,7 @@
     tail_copy.wait()
 
 
-def place_tiles(act, source, label_of, count, plays, first_block, sems, base):
+def place_tiles(act, source, label_of, count, plays, sems, base):
     height = plays.shape[1] // HG
     core = this_half()
 
@@ -216,9 +219,7 @@
         @pl.when((where >= core * (HG * CBLK)) & (where < (core + 1) * (HG * CBLK)))
         def _():
             local = where - core * (HG * CBLK)
-            target = plays.at[
-                first_block + lax.rem(local, CBLK), pl.ds(pl.multiple_of(local // CBLK * height, 16), height), :
-            ]
+            target = plays.at[lax.rem(local, CBLK), pl.ds(pl.multiple_of(local // CBLK * height, 16), height), :]
             tile = source.at[pl.ds(pl.multiple_of(k * height, 16), height), :]
             act(pltpu.make_async_copy(tile, target, sems.at[base + k]))
 
@@ -230,7 +231,7 @@
 def place_kernel(cap, sizes, own_label, tiles, pair_tiles, *refs):
     n = len(sizes) - 1
     parts, pair_parts = refs[:n], refs[n : 2 * n]
-    factors, pair_factors, plays, stacked, labels, raw, whole, raw_sems, label_sem, sems = refs[2 * n :]
+    factors, pair_factors, plays, pair_plays, stacked, labels, raw, whole, raw_sems, label_sem, sems = refs[2 * n :]
     height = plays.shape[1] // HG
     senders = parts[0].shape[0]
     tails = [pair_tiles.at[pl.ds(cap * height, 16), pl.ds(0, 128)]]
@@ -241,12 +242,13 @@
     for read in reads:
         read.start()
     plays[...] = jnp.zeros_like(plays)
+    pair_plays[...] = jnp.zeros_like(pair_plays)
 
     def own(act):
-        place_tiles(act, tiles, lambda k: own_label[k], cap, plays, 0, sems, 0)
+        place_tiles(act, tiles, lambda k: own_label[k], cap, plays, sems, 0)
 
     def others(act):
-        place_tiles(act, pair_tiles, lambda k: labels[0, k], cap, plays, CBLK, sems, cap)
+        place_tiles(act, pair_tiles, lambda k: labels[0, k], cap, pair_plays, sems, cap)
         base = 2 * cap
         for side, group in enumerate((parts, pair_parts)):
             for s in range(senders):
@@ -254,7 +256,7 @@
                 low = 0
                 for part, size in zip(group, sizes):
                     label_of = lambda k, row=row, low=low: labels[row, low + k]
-                    place_tiles(act, part.at[s], label_of, size, plays, side * CBLK, sems, base)
+                    place_tiles(act, part.at[s], label_of, size, (plays, pair_plays)[side], sems, base)
                     low += size
                     base += size
 
@@ -292,56 +294,57 @@
     return sum(x[:, k * 128 : (k + 1) * 128] for k in range(x.shape[1] // 128))
 
 
-def first_kernel(
-    n_items, offset, labels, direction, placed, late, pair_late, factors, image, plays, reg, seen, acc, buf, sems
-):
+def first_kernel(n_items, offset, side, labels, direction, placed, late, factors, *refs):
+    before, after = refs[: 2 * side], refs[2 * side :]
+    if side:
+        image, plays, reg, acc, seen, buf, sem = after
+    else:
+        plays, acc, seen, buf, sem = after
+    blocks, _, width = plays.shape
     senders, height = late.shape[0], plays.shape[1] // HG
     size = late.shape[1] // height
-    moves = [pltpu.make_async_copy(part, buf.at[i], sems.at[i]) for i, part in enumerate((late, pair_late))]
-    for move in moves:
-        move.start()
+    move = pltpu.make_async_copy(late, buf, sem)
+    move.start()
     plays[...] = placed[...]
     core = this_half()
-    for side, move in enumerate(moves):
-        move.wait()
-
-        def visit(i, carry, side=side):
-            s, k = i // size, lax.rem(i, size)
-            where = labels[1 + side * senders + s, offset + k]
-
-            @pl.when((where >= core * (HG * CBLK)) & (where < (core + 1) * (HG * CBLK)))
-            def _():
-                local = where - core * (HG * CBLK)
-                row = pl.ds(pl.multiple_of(local // CBLK * height, 16), height)
-                tile = buf[side, s, pl.ds(pl.multiple_of(k * height, 16), height), :]
-                plays[side * CBLK + lax.rem(local, CBLK), row, :] = tile
-
-            return carry
-
-        lax.fori_loop(0, senders * size, visit, 0)
-    blocks, _, width = plays.shape
+    move.wait()
+
+    def visit(i, carry):
+        s, k = i // size, lax.rem(i, size)
+        local = labels[1 + side * senders + s, offset + k] - core * (HG * CBLK)
+
+        @pl.when((local >= 0) & (local < HG * CBLK))
+        def _():
+            row = pl.ds(pl.multiple_of(local // CBLK * height, 16), height)
+            plays[lax.rem(local, CBLK), row, :] = buf[s, pl.ds(pl.multiple_of(k * height, 16), height), :]
+
+        return carry
+
+    lax.fori_loop(0, senders * size, visit, 0)
     for j in range(blocks):
-        block = factors[j * width : (j + 1) * width, :]
+        at = (side * blocks + j) * width
+        block = factors[at : at + width, :]
         value = plays[j].astype(F32)
         _, scaled = scaled_block(direction[...], block, value)
         part = jnp.dot(scaled, block, preferred_element_type=F32)
         count = lanes(jnp.where(value > 0, 1.0, 0.0))
         if j == 0:
-            acc[...] = part
-            seen[...] = count
+            acc[...] = before[0][...] + part if side else part
+            seen[...] = before[1][...] + count if side else count
         else:
             acc[...] += part
             seen[...] += count
-    share = jnp.sum(seen[...], axis=1, keepdims=True) / n_items
-    reg[...] = jnp.broadcast_to(share, reg.shape)
-    image[...] = (acc[...] + share * direction[...].astype(F32)).astype(BF16)
-
-
-def mid_kernel(direction, reg, plays, factors, image, acc):
-    blocks, _, width = plays.shape
-    for j in range(blocks):
+    if side:
+        share = jnp.sum(seen[...], axis=1, keepdims=True) / n_items
+        reg[...] = jnp.broadcast_to(share, reg.shape)
+        image[...] = (acc[...] + share * direction[...].astype(F32)).astype(BF16)
+
+
+def mid_kernel(direction, reg, plays, pair_plays, factors, image, acc):
+    width = plays.shape[2]
+    for j in range(2 * CBLK):
         block = factors[j * width : (j + 1) * width, :]
-        _, scaled = scaled_block(direction[...], block, plays[j].astype(F32))
+        _, scaled = scaled_block(direction[...], block, (plays, pair_plays)[j // CBLK][j % CBLK].astype(F32))
         part = jnp.dot(scaled, block, preferred_element_type=F32)
         if j == 0:
             acc[...] = part
@@ -350,11 +353,11 @@
     image[...] = (acc[...] + reg[:, :1] * direction[...].astype(F32)).astype(BF16)
 
 
-def last_kernel(direction, reg, base, plays, factors, payload, acc, laid):
-    blocks, _, width = plays.shape
-    for j in range(blocks):
+def last_kernel(direction, reg, base, plays, pair_plays, factors, payload, acc, laid):
+    width = plays.shape[2]
+    for j in range(2 * CBLK):
         block = factors[j * width : (j + 1) * width, :]
-        projected, scaled = scaled_block(direction[...], block, plays[j].astype(F32))
+        projected, scaled = scaled_block(direction[...], block, (plays, pair_plays)[j // CBLK][j % CBLK].astype(F32))
         part = lanes(scaled.astype(F32) * projected)
         if j == 0:
             acc[...] = part
@@ -514,7 +517,7 @@
     state = (n_chunk, n_user * chunk, rank)
     keep, send, own, own_label = call(
         functools.partial(rhs_kernel, n_user, cap, sizes),
-        [SMEM] * 5 + [HBM] * (1 + len(sizes)) + [VMEM],
+        [SMEM] * 5 + [HBM] * (2 + len(sizes)),
         [
             (pltpu.VMEM(state, F32), VMEM),
             (pltpu.VMEM(state, BF16), VMEM),
@@ -528,9 +531,11 @@
             pltpu.VMEM((cap, height, width), jnp.int32),
             pltpu.VMEM((cap * height + 16, width), BF16),
             pltpu.VMEM((HALVES * n_user * half, shard_items), BF16),
+            pltpu.VMEM((shard_items, rank), BF16),
             dma((cap,)),
             dma((cap + 1,)),
             dma((len(sizes),)),
+            dma(()),
         ],
         56,
         flops=2 * HALVES * n_user * half * shard_items * rank,
@@ -552,13 +557,14 @@
     residual = folded = direction
     late = from_users(last_part)
     pair_parts = [to_pair(part) for part in far]
-    plays_shape = (blocks, half, width)
+    plays_shape = (CBLK, half, width)
     n_labels = 2 * (n_user - 1) + 1
     label_shape = (-(-n_labels // 8) * 8, 128)
-    placed, factors, labels = call(
+    placed, pair_placed, factors, labels = call(
         functools.partial(place_kernel, cap, sizes),
         [SMEM] + [HBM] * (2 + 2 * len(far)) + [VMEM] * 2,
         [
+            (shape(plays_shape, BF16), VMEM),
             (shape(plays_shape, BF16), VMEM),
             (pltpu.VMEM((HALVES * shard_items, rank), BF16), VMEM),
             (shape(label_shape, jnp.int32), SMEM),
@@ -586,30 +592,37 @@
         if number == 0:
             late, whole, labels = lax.optimization_barrier((late, whole, labels))
             pair_late = to_pair(late)
-            image, plays, reg = call(
-                functools.partial(first_kernel, n_items, cap - sizes[-1]),
-                [SMEM] + [VMEM] * 2 + [HBM] * 2 + [VMEM],
-                [image_out, (pltpu.VMEM(plays_shape, BF16), VMEM), (shape((half, 128), F32), VMEM)],
-                [
-                    pltpu.VMEM((half, 128), F32),
-                    pltpu.VMEM((half, rank), F32),
-                    pltpu.VMEM((2, *part_shapes[-1]), BF16),
-                    dma((2,)),
-                ],
+            acc_out, seen_out = shape((half, rank), F32), shape((half, 128), F32)
+            plays_out = (pltpu.VMEM(plays_shape, BF16), VMEM)
+            buffers = [pltpu.VMEM(part_shapes[-1], BF16), dma(())]
+            plays, acc, seen = call(
+                functools.partial(first_kernel, n_items, cap - sizes[-1], 0),
+                [SMEM, VMEM, VMEM, HBM, VMEM],
+                [plays_out, (acc_out, VMEM), (seen_out, VMEM)],
+                buffers,
                 20,
-                flops=block_flops,
-                nbytes=2 * block_bytes,
-            )(labels, whole, placed, late, pair_late, factors)
+                flops=block_flops // 2,
+                nbytes=block_bytes,
+            )(labels, whole, placed, late, factors)
+            image, pair_plays, reg = call(
+                functools.partial(first_kernel, n_items, cap - sizes[-1], 1),
+                [SMEM, VMEM, VMEM, HBM, VMEM, VMEM, VMEM],
+                [image_out, plays_out, (seen_out, VMEM)],
+                [pltpu.VMEM((half, rank), F32), pltpu.VMEM((half, 128), F32)] + buffers,
+                20,
+                flops=block_flops // 2,
+                nbytes=block_bytes,
+            )(labels, whole, pair_placed, pair_late, factors, acc, seen)
         else:
             (image,) = call(
                 mid_kernel,
-                [VMEM] * 4,
+                [VMEM] * 5,
                 [image_out],
                 [pltpu.VMEM((half, rank), F32)],
                 12,
                 flops=block_flops,
                 nbytes=block_bytes,
-            )(whole, reg, plays, factors)
+            )(whole, reg, plays, pair_plays, factors)
         got = exchange(image.reshape(n_chunk, chunk, rank))
         ends = number == ITERS - 2
         outs = [(payload_shape, VMEM)] if ends else [(shape((chunk, rank), F32), VMEM)] * 3
@@ -627,13 +640,13 @@
 
     (payload,) = call(
         last_kernel,
-        [VMEM] * 5,
+        [VMEM] * 6,
         [(payload_shape, VMEM)],
         [pltpu.VMEM((half, 128), F32), pltpu.VMEM((share, 128), F32)],
         12,
         flops=block_flops // 2,
         nbytes=block_bytes,
-    )(whole, reg, base, plays, factors)
+    )(whole, reg, base, plays, pair_plays, factors)
     got = lax.all_to_all(payload, "item", 0, 0, tiled=True)
     (out,) = call(final_kernel, [VMEM], [(shape((share, HALVES * half), F32), VMEM)], [], 4)(got)
     return out.T

time: 147 us -> 146 us (level)
  waiting for transfers between devices: 17.3 us -> 15.4 us
    ppermute x5, waiting for transfers between devices: 3.14 us -> 1.22 us  [to_pair(): return lax.ppermute(x, 'item', pair)]
    pallas_call x4 -> x5, Pallas kernels: 9.58 us -> 10.8 us  [the longest x2 3.88 us: shards(): call(mid_kernel, [VMEM] * 5, [image_out], [pltpu.VMEM((half, rank), F32)]...]
    unnamed x8 -> x10, local copies, waits for them, and re-layouts: 3.06 us -> 2.55 us
  transfers between devices with their start and end apart: 10 -> 10, of which waited for: 5 -> 5; matrix products, arithmetic and copies ran while one was open for 1% -> 1% of each run, Pallas kernels for 11% -> 13%
where the time goes in v4:
time: 146 us
  blocking collectives  77.9 us (53%)
  Pallas kernels  32.5 us (22%)
  starting transfers between devices  16.1 us (11%)
  waiting for transfers between devices  15.4 us (11%)
  local copies, waits for them, and re-layouts  2.56 us (2%)
    all_to_all x6, blocking collectives, exchange(): return lax.all_to_all(x, 'item', 0, 0, axis_index_groups=groups, tiled=True)  67.3 us
    ppermute x3, waiting for transfers between devices, over_users(): lax.ppermute(x, 'user', [(u, (u + shift) % n_user) for u in range(n_user)])  12.1 us
    all_to_all x1, blocking collectives, shards(): got = lax.all_to_all(payload, 'item', 0, 0, tiled=True)  10.5 us
    all_to_all x2, starting transfers between devices, exchange(): return lax.all_to_all(x, 'item', 0, 0, axis_index_groups=groups, tiled=True)  9.84 us
    pallas_call x1, Pallas kernels, shards(): call(functools.partial(rhs_kernel, n_user, cap, sizes), [SMEM] * 5 + [HBM...  8.47 us
    pallas_call x1, Pallas kernels, shards(): call(functools.partial(place_kernel, cap, sizes), [SMEM] + [HBM] * (2 + 2...  6.5 us
    ppermute x3, starting transfers between devices, over_users(): lax.ppermute(x, 'user', [(u, (u + shift) % n_user) for u in range(n_user)])  5.15 us
    pallas_call x1, Pallas kernels, shards(): call(functools.partial(pack_kernel, n_user, cap, sizes), [SMEM] * 4 + [HB...  4.37 us
  transfers between devices with their start and end apart: 10, of which 5 were waited for; matrix products, arithmetic and copies ran while one was open for 1% of the time, Pallas kernels for 13%

profile of v4, /device:TPU:0, one launch (start us, length us, event | category | flops | bytes accessed | tf_op | source)
XLA Modules:
  0.0 145.5 jit_solution(10055765820097616766)
XLA Ops:
  0.0 4.4 %shard_map.64 = (bf16[1,1168,512]{2,1,0:T(8,128)(2,1)}, bf16[1,384,512]{2,1,0:T(8,128)(2,1)}, s32[16]{0:T(128)}) custom-call(s32[31]{0:T(128)} %bitcast.29, s32[31]{0:T(128)} %bitcast.31, s32[31]{0:T(128)} %bitcast.33, s32[31]{0:T(128)} %bitcast.35, s32[31,96,512]{2,1,0:T(8,128)} %bitcast.26), custom_call_target="tpu_custom_call" | custom-call | bytes 4718592 | tf_op jit(solution)/shard_map/pallas_call | solution.py:497
  4.4 3.1 %collective-permute-start.4 = (bf16[1,1168,512]{2,1,0:T(8,128)(2,1)}, bf16[1,1168,512]{2,1,0:T(8,128)(2,1)}, u32[]{:S(2)}, u32[]{:S(2)}) collective-permute-start(bf16[1,1168,512]{2,1,0:T(8,128)(2,1)} %get-tuple-element.41.refs_0_), channel_id=1, source_target_pairs={{0,16},{16,0},{1,17},{17,1},{2,18},{18,2},{3,19},{19,3},{4,20},{20... | collective-permute-start | bytes 3588104 | tf_op jit(solution)/shard_map/ppermute | solution.py:480
  7.4 8.5 %shard_map.65 = (f32[8,96,256]{2,1,0:T(8,128)S(1)}, bf16[8,96,256]{2,1,0:T(8,128)(2,1)S(1)}, bf16[1552,512]{1,0:T(8,128)(2,1)}, s32[16]{0:T(128)}) custom-call(s32[31]{0:T(128)} %bitcast.30, s32[31]{0:T(128)} %bitcast.32, s32[31]{0:T(128)} %bitcast.34, s32[31]{0:T(128)} %bitcast.36, s32[16]{0:T(128)} %get-tuple-element.40.out_label, ...), custom_call_target="tpu_custom_call" | custom-call | flops 1610612736 | bytes 12189696 | tf_op jit(solution)/shard_map/pallas_call | solution.py:518
  15.9 0.0 copy-start
  15.9 0.1 collective-permute-start
  16.0 0.5 collective-permute-start.3
  16.5 1.2 collective-permute-done
  17.7 0.0 copy-start.3
  17.7 0.8 add_convert_fusion
  18.6 5.9 %all-to-all-start = ((bf16[8,96,256]{2,1,0:T(8,128)(2,1)}), bf16[8,96,256]{2,1,0:T(8,128)(2,1)S(1)}, u32[]{:S(2)}, u32[]{:S(2)}) async-start(bf16[8,96,256]{2,1,0:T(8,128)(2,1)} %add_convert_fusion), calls=%async_computation | async-start | bytes 786432 | tf_op jit(solution)/shard_map/all_to_all | solution.py:490
  24.5 9.5 %collective-permute-done.4.refs_0_ = bf16[1,1168,512]{2,1,0:T(8,128)(2,1)} collective-permute-done((bf16[1,1168,512]{2,1,0:T(8,128)(2,1)}, bf16[1,1168,512]{2,1,0:T(8,128)(2,1)}, u32[]{:S(2)}, u32[]{:S(2)}) %collective-permute-start.4) | collective-permute-done | bytes 1196064 | tf_op jit(solution)/shard_map/ppermute | solution.py:480
  34.0 0.0 collective-permute-start.5
  34.0 0.0 copy-done
  34.0 0.5 collective-permute-start.6
  34.5 2.0 %all-to-all-done = bf16[8,96,256]{2,1,0:T(8,128)(2,1)S(1)} async-done(((bf16[8,96,256]{2,1,0:T(8,128)(2,1)}), bf16[8,96,256]{2,1,0:T(8,128)(2,1)S(1)}, u32[]{:S(2)}, u32[]{:S(2)}) %all-to-all-start) | async-done | bytes 393248 | tf_op jit(solution)/shard_map/all_to_all | solution.py:490
  36.5 0.1 convert_reduce_fusion
  36.5 0.3 collective-permute-start.2
  36.9 1.8 %collective-permute-start.1 = (bf16[1,384,512]{2,1,0:T(8,128)(2,1)}, bf16[1,384,512]{2,1,0:T(8,128)(2,1)}, u32[]{:S(2)}, u32[]{:S(2)}) collective-permute-start(bf16[1,384,512]{2,1,0:T(8,128)(2,1)} %get-tuple-element.44.refs_1_), channel_id=1, source_target_pairs={{0,16},{16,0},{1,17},{17,1},{2,18},{18,2},{3,19},{19,3},{4,20},{20... | collective-permute-start | bytes 1179656 | tf_op jit(solution)/shard_map/ppermute | solution.py:480
  38.6 2.6 %collective-permute-done.2.refs_1_ = f32[48,256]{1,0:T(8,128)S(1)} collective-permute-done((f32[48,256]{1,0:T(8,128)S(1)}, f32[48,256]{1,0:T(8,128)S(1)}, u32[]{:S(2)}, u32[]{:S(2)}) %collective-permute-start.2) | collective-permute-done | bytes 49184 | tf_op jit(solution)/shard_map/ppermute | solution.py:480
  41.2 0.7 shard_map.66
  41.9 3.9 %all-to-all-start.1 = ((bf16[8,48,256]{2,1,0:T(8,128)(2,1)}), bf16[8,48,256]{2,1,0:T(8,128)(2,1)S(1)}, u32[]{:S(2)}, u32[]{:S(2)}) async-start(bf16[8,48,256]{2,1,0:T(8,128)(2,1)} %get-tuple-element.46), calls=%async_computation.1 | async-start | bytes 393216 | tf_op jit(solution)/shard_map/all_to_all | solution.py:490
  45.9 0.0 collective-permute-done.6.refs_3_
  45.9 0.0 collective-permute-done.3.pair_tiles
  45.9 0.0 copy-start.4
  45.9 0.0 collective-permute-done.5.refs_1_
  45.9 1.1 copy-done.4
  47.0 0.0 copy-done.3
  47.0 6.5 %shard_map.67 = (bf16[4,384,512]{2,1,0:T(8,128)(2,1)}, bf16[4,384,512]{2,1,0:T(8,128)(2,1)}, bf16[4096,256]{1,0:T(8,128)(2,1)S(1)}, s32[8,128]{1,0:T(8,128)S(1)}) custom-call(s32[16]{0:T(128)S(1)} %copy-done.3, bf16[1552,512]{1,0:T(8,128)(2,1)} %get-tuple-element.48.tiles, bf16[1552,512]{1,0:T(8,128)(2,1)} %copy-done.4, ...), custom_call_target="tpu_custom_call" | custom-call | bytes 3145728 | tf_op jit(solution)/shard_map/pallas_call | solution.py:563
  53.5 0.0 collective-permute-done.1.late
  53.5 0.1 all-to-all-done.1
  53.6 0.0 collective-permute-start.7
  53.6 0.0 copy-start.1
  53.6 1.4 copy-done.1
  55.0 0.0 copy-start.2
  55.1 2.8 %shard_map.68 = (bf16[4,384,512]{2,1,0:T(8,128)(2,1)S(1)}, f32[384,256]{1,0:T(8,128)S(1)}, f32[384,128]{1,0:T(8,128)S(1)}) custom-call(s32[8,128]{1,0:T(8,128)S(1)} %get-tuple-element.50.labels, bf16[384,256]{1,0:T(8,128)(2,1)S(1)} %bitcast.18, bf16[4,384,512]{2,1,0:T(8,128)(2,1)S(1)} %copy-done.1, bf16[1,384,512]{2,1,0:T(8,128)(2,1)} %collective-permute-done.1.late, ...), custom_call_target="tpu_custom_call" | custom-call | flops 805306368 | bytes 5242880 | tf_op jit(solution)/shard_map/pallas_call | solution.py:598
  57.9 0.0 collective-permute-done.7.late
  57.9 0.0 copy-done.2
  57.9 2.3 %shard_map.69 = (bf16[384,256]{1,0:T(8,128)(2,1)S(1)}, bf16[4,384,512]{2,1,0:T(8,128)(2,1)S(1)}, f32[384,128]{1,0:T(8,128)S(1)}) custom-call(s32[8,128]{1,0:T(8,128)S(1)} %get-tuple-element.50.labels, bf16[384,256]{1,0:T(8,128)(2,1)S(1)} %bitcast.19, bf16[4,384,512]{2,1,0:T(8,128)(2,1)S(1)} %copy-done.2, ...), custom_call_target="tpu_custom_call" | custom-call | flops 805306368 | bytes 5242880 | tf_op jit(solution)/shard_map/pallas_call | solution.py:607
  60.2 14.3 %all_to_all.45.got = bf16[8,48,256]{2,1,0:T(8,128)(2,1)S(1)} all-to-all(bf16[8,48,256]{2,1,0:T(8,128)(2,1)S(1)} %bitcast.21), channel_id=1, replica_groups={{0,2,4,6,8,10,12,14},{1,3,5,7,9,11,13,15},{16,18,20,22,24,26,28,30},{17..., dimensions={0} | all-to-all | bytes 393216 | tf_op jit(solution)/shard_map/all_to_all | solution.py:490
  74.6 0.2 shard_map.70
  74.8 11.0 %all_to_all.46 = bf16[8,48,256]{2,1,0:T(8,128)(2,1)S(1)} all-to-all(bf16[8,48,256]{2,1,0:T(8,128)(2,1)S(1)} %get-tuple-element.60), channel_id=1, replica_groups={{0,2,4,6,8,10,12,14},{1,3,5,7,9,11,13,15},{16,18,20,22,24,26,28,30},{17..., dimensions={0} | all-to-all | bytes 393216 | tf_op jit(solution)/shard_map/all_to_all | solution.py:490
  85.8 1.9 %shard_map.71 = bf16[384,256]{1,0:T(8,128)(2,1)S(1)} custom-call(bf16[384,256]{1,0:T(8,128)(2,1)S(1)} %bitcast.22, f32[384,128]{1,0:T(8,128)S(1)} %get-tuple-element.61.reg, bf16[4,384,512]{2,1,0:T(8,128)(2,1)S(1)} %get-tuple-element.62.plays, bf16[4,384,512]{2,1,0:T(8,128)(2,1)S(1)} %get-tuple-element.63.pair_plays, ...), custom_call_target="tpu_custom_call" | custom-call | flops 1610612736 | bytes 5242880 | tf_op jit(solution)/shard_map/pallas_call | solution.py:617
  87.7 10.7 %all_to_all.47.got = bf16[8,48,256]{2,1,0:T(8,128)(2,1)S(1)} all-to-all(bf16[8,48,256]{2,1,0:T(8,128)(2,1)S(1)} %bitcast.23), channel_id=1, replica_groups={{0,2,4,6,8,10,12,14},{1,3,5,7,9,11,13,15},{16,18,20,22,24,26,28,30},{17..., dimensions={0} | all-to-all | bytes 393216 | tf_op jit(solution)/shard_map/all_to_all | solution.py:490
  98.4 0.2 shard_map.72
  98.6 10.6 %all_to_all.48 = bf16[8,48,256]{2,1,0:T(8,128)(2,1)S(1)} all-to-all(bf16[8,48,256]{2,1,0:T(8,128)(2,1)S(1)} %get-tuple-element.67), channel_id=1, replica_groups={{0,2,4,6,8,10,12,14},{1,3,5,7,9,11,13,15},{16,18,20,22,24,26,28,30},{17..., dimensions={0} | all-to-all | bytes 393216 | tf_op jit(solution)/shard_map/all_to_all | solution.py:490
  109.3 1.9 %shard_map.73 = bf16[384,256]{1,0:T(8,128)(2,1)S(1)} custom-call(bf16[384,256]{1,0:T(8,128)(2,1)S(1)} %bitcast.24, f32[384,128]{1,0:T(8,128)S(1)} %get-tuple-element.61.reg, bf16[4,384,512]{2,1,0:T(8,128)(2,1)S(1)} %get-tuple-element.62.plays, bf16[4,384,512]{2,1,0:T(8,128)(2,1)S(1)} %get-tuple-element.63.pair_plays, ...), custom_call_target="tpu_custom_call" | custom-call | flops 1610612736 | bytes 5242880 | tf_op jit(solution)/shard_map/pallas_call | solution.py:617
  111.2 10.5 %all_to_all.49.got = bf16[8,48,256]{2,1,0:T(8,128)(2,1)S(1)} all-to-all(bf16[8,48,256]{2,1,0:T(8,128)(2,1)S(1)} %bitcast.25), channel_id=1, replica_groups={{0,2,4,6,8,10,12,14},{1,3,5,7,9,11,13,15},{16,18,20,22,24,26,28,30},{17..., dimensions={0} | all-to-all | bytes 393216 | tf_op jit(solution)/shard_map/all_to_all | solution.py:490
  121.7 0.4 shard_map.74
  122.1 10.2 %all_to_all.50 = bf16[8,48,256]{2,1,0:T(8,128)(2,1)S(1)} all-to-all(bf16[8,48,256]{2,1,0:T(8,128)(2,1)S(1)} %get-tuple-element.71), channel_id=1, replica_groups={{0,2,4,6,8,10,12,14},{1,3,5,7,9,11,13,15},{16,18,20,22,24,26,28,30},{17..., dimensions={0} | all-to-all | bytes 393216 | tf_op jit(solution)/shard_map/all_to_all | solution.py:490
  132.3 1.7 %shard_map.75 = f32[16,16,128]{2,1,0:T(8,128)S(1)} custom-call(bf16[384,256]{1,0:T(8,128)(2,1)S(1)} %bitcast.20, f32[384,128]{1,0:T(8,128)S(1)} %get-tuple-element.61.reg, f32[16,16,128]{2,1,0:T(8,128)S(1)} %get-tuple-element.72.base, bf16[4,384,512]{2,1,0:T(8,128)(2,1)S(1)} %get-tuple-element.62.plays, ...), custom_call_target="tpu_custom_call" | custom-call | flops 805306368 | bytes 5242880 | tf_op jit(solution)/shard_map/pallas_call | solution.py:641
  134.0 10.5 %all_to_all.51.got = f32[16,16,128]{2,1,0:T(8,128)S(1)} all-to-all(f32[16,16,128]{2,1,0:T(8,128)S(1)} %shard_map.75), channel_id=1, replica_groups=mesh['user'=2,'item'=16] {'item'}, dimensions={0} | all-to-all | bytes 262144 | tf_op jit(solution)/shard_map/all_to_all | solution.py:650
  144.5 1.0 shard_map.76
  (1 shorter events, 0.0 us)
Async XLA Ops:
  4.4 29.6 %collective-permute-start.4 = (bf16[1,1168,512]{2,1,0:T(8,128)(2,1)}, bf16[1,1168,512]{2,1,0:T(8,128)(2,1)}, u32[]{:S(2)}, u32[]{:S(2)}) collective-permute-start(bf16[1,1168,512]{2,1,0:T(8,128)(2,1)} %get-tuple-element.41.refs_0_), channel_id=1, source_target_pairs={{0,16},{16,0},{1,17},{17,1},{2,18},{18,2},{3,19},{19,3},{4,20},{20... | collective-permute-start | bytes 3588104 | tf_op jit(solution)/shard_map/ppermute | solution.py:480
  15.9 18.1 %copy-start = (bf16[2048,256]{1,0:T(8,128)(2,1)S(1)}, bf16[2048,256]{1,0:T(8,128)(2,1)}, u32[]{:S(2)}) copy-start(bf16[2048,256]{1,0:T(8,128)(2,1)} %refs_2_.3) | copy-start | bytes 3145732
  15.9 1.8 %collective-permute-start = (bf16[8,96,256]{2,1,0:T(8,128)(2,1)S(1)}, bf16[8,96,256]{2,1,0:T(8,128)(2,1)S(1)}, u32[]{:S(2)}, u32[]{:S(2)}) collective-permute-start(bf16[8,96,256]{2,1,0:T(8,128)(2,1)S(1)} %get-tuple-element.43), channel_id=1, source_target_pairs={{0,1},{1,0},{2,3},{3,2},{4,5},{5,4},{6,7},{7,6},{8,9},{9,8},{10,11... | collective-permute-start | bytes 1179656 | tf_op jit(solution)/shard_map/ppermute | solution.py:487
  16.0 29.9 %collective-permute-start.3 = (bf16[1552,512]{1,0:T(8,128)(2,1)}, bf16[1552,512]{1,0:T(8,128)(2,1)S(1)}, u32[]{:S(2)}, u32[]{:S(2)}) collective-permute-start(bf16[1552,512]{1,0:T(8,128)(2,1)} %get-tuple-element.48.tiles), channel_id=1, source_target_pairs={{0,1},{1,0},{2,3},{3,2},{4,5},{5,4},{6,7},{7,6},{8,9},{9,8},{10,11... | collective-permute-start | bytes 4767752 | tf_op jit(solution)/shard_map/ppermute | solution.py:487
  17.7 29.3 %copy-start.3 = (s32[16]{0:T(128)S(1)}, s32[16]{0:T(128)}, u32[]{:S(2)}) copy-start(s32[16]{0:T(128)} %get-tuple-element.47.own_label) | copy-start | bytes 196
  18.6 17.9 %all-to-all-start = ((bf16[8,96,256]{2,1,0:T(8,128)(2,1)}), bf16[8,96,256]{2,1,0:T(8,128)(2,1)S(1)}, u32[]{:S(2)}, u32[]{:S(2)}) async-start(bf16[8,96,256]{2,1,0:T(8,128)(2,1)} %add_convert_fusion), calls=%async_computation | async-start | bytes 786432 | tf_op jit(solution)/shard_map/all_to_all | solution.py:490
  34.0 11.9 %collective-permute-start.5 = (bf16[1,1168,512]{2,1,0:T(8,128)(2,1)}, bf16[1,1168,512]{2,1,0:T(8,128)(2,1)}, u32[]{:S(2)}, u32[]{:S(2)}) collective-permute-start(bf16[1,1168,512]{2,1,0:T(8,128)(2,1)} %collective-permute-done.4.refs_0_), channel_id=1, source_target_pairs={{0,1},{1,0},{2,3},{3,2},{4,5},{5,4},{6,7},{7,6},{8,9},{9,8},{10,11... | collective-permute-start | bytes 3588104 | tf_op jit(solution)/shard_map/ppermute | solution.py:487
  34.0 11.9 %collective-permute-start.6 = (bf16[2048,256]{1,0:T(8,128)(2,1)S(1)}, bf16[2048,256]{1,0:T(8,128)(2,1)}, u32[]{:S(2)}, u32[]{:S(2)}) collective-permute-start(bf16[2048,256]{1,0:T(8,128)(2,1)S(1)} %copy-done), channel_id=1, source_target_pairs={{0,1},{1,0},{2,3},{3,2},{4,5},{5,4},{6,7},{7,6},{8,9},{9,8},{10,11... | collective-permute-start | bytes 3145736 | tf_op jit(solution)/shard_map/ppermute | solution.py:487
  36.5 4.7 %collective-permute-start.2 = (f32[48,256]{1,0:T(8,128)S(1)}, f32[48,256]{1,0:T(8,128)S(1)}, u32[]{:S(2)}, u32[]{:S(2)}) collective-permute-start(f32[48,256]{1,0:T(8,128)S(1)} %get-tuple-element.73), channel_id=1, source_target_pairs={{0,16},{16,0},{1,17},{17,1},{2,18},{18,2},{3,19},{19,3},{4,20},{20... | collective-permute-start | bytes 147464 | tf_op jit(solution)/shard_map/ppermute | solution.py:480
  36.9 16.7 %collective-permute-start.1 = (bf16[1,384,512]{2,1,0:T(8,128)(2,1)}, bf16[1,384,512]{2,1,0:T(8,128)(2,1)}, u32[]{:S(2)}, u32[]{:S(2)}) collective-permute-start(bf16[1,384,512]{2,1,0:T(8,128)(2,1)} %get-tuple-element.44.refs_1_), channel_id=1, source_target_pairs={{0,16},{16,0},{1,17},{17,1},{2,18},{18,2},{3,19},{19,3},{4,20},{20... | collective-permute-start | bytes 1179656 | tf_op jit(solution)/shard_map/ppermute | solution.py:480
  41.9 11.7 %all-to-all-start.1 = ((bf16[8,48,256]{2,1,0:T(8,128)(2,1)}), bf16[8,48,256]{2,1,0:T(8,128)(2,1)S(1)}, u32[]{:S(2)}, u32[]{:S(2)}) async-start(bf16[8,48,256]{2,1,0:T(8,128)(2,1)} %get-tuple-element.46), calls=%async_computation.1 | async-start | bytes 393216 | tf_op jit(solution)/shard_map/all_to_all | solution.py:490
  45.9 1.1 copy-start.4
  53.6 4.3 %collective-permute-start.7 = (bf16[1,384,512]{2,1,0:T(8,128)(2,1)}, bf16[1,384,512]{2,1,0:T(8,128)(2,1)S(1)}, u32[]{:S(2)}, u32[]{:S(2)}) collective-permute-start(bf16[1,384,512]{2,1,0:T(8,128)(2,1)} %collective-permute-done.1.late), channel_id=1, source_target_pairs={{0,1},{1,0},{2,3},{3,2},{4,5},{5,4},{6,7},{7,6},{8,9},{9,8},{10,11... | collective-permute-start | bytes 1179656 | tf_op jit(solution)/shard_map/ppermute | solution.py:487
  53.6 1.4 copy-start.1
  55.0 2.9 %copy-start.2 = (bf16[4,384,512]{2,1,0:T(8,128)(2,1)S(1)}, bf16[4,384,512]{2,1,0:T(8,128)(2,1)}, u32[]{:S(2)}) copy-start(bf16[4,384,512]{2,1,0:T(8,128)(2,1)} %get-tuple-element.52.placed) | copy-start | bytes 4718596

commit v5 on v4

--- a/solution.py
+++ b/solution.py
@@ -564,7 +564,7 @@
         functools.partial(place_kernel, cap, sizes),
         [SMEM] + [HBM] * (2 + 2 * len(far)) + [VMEM] * 2,
         [
-            (shape(plays_shape, BF16), VMEM),
+            (pltpu.VMEM(plays_shape, BF16), VMEM),
             (shape(plays_shape, BF16), VMEM),
             (pltpu.VMEM((HALVES * shard_items, rank), BF16), VMEM),
             (shape(label_shape, jnp.int32), SMEM),

time: 146 us -> 146 us (level)
  transfers between devices with their start and end apart: 10 -> 10, of which waited for: 5 -> 5; matrix products, arithmetic and copies ran while one was open for 1% -> 1% of each run, Pallas kernels for 13% -> 12%
where the time goes in v5:
time: 146 us; the launch traced here: 145 us
  blocking collectives  77.9 us (53%)
  Pallas kernels  31.8 us (22%)
  starting transfers between devices  16 us (11%)
  waiting for transfers between devices  15.5 us (11%)
  local copies, waits for them, and re-layouts  2.6 us (2%)
    all_to_all x6, blocking collectives, exchange(): return lax.all_to_all(x, 'item', 0, 0, axis_index_groups=groups, tiled=True)  67.4 us
    ppermute x3, waiting for transfers between devices, over_users(): lax.ppermute(x, 'user', [(u, (u + shift) % n_user) for u in range(n_user)])  12.3 us
    all_to_all x1, blocking collectives, shards(): got = lax.all_to_all(payload, 'item', 0, 0, tiled=True)  10.5 us
    all_to_all x2, starting transfers between devices, exchange(): return lax.all_to_all(x, 'item', 0, 0, axis_index_groups=groups, tiled=True)  9.87 us
    pallas_call x1, Pallas kernels, shards(): call(functools.partial(rhs_kernel, n_user, cap, sizes), [SMEM] * 5 + [HBM...  8.36 us
    pallas_call x1, Pallas kernels, shards(): call(functools.partial(place_kernel, cap, sizes), [SMEM] + [HBM] * (2 + 2...  6.38 us
    ppermute x3, starting transfers between devices, over_users(): lax.ppermute(x, 'user', [(u, (u + shift) % n_user) for u in range(n_user)])  5.07 us
    pallas_call x1, Pallas kernels, shards(): call(functools.partial(pack_kernel, n_user, cap, sizes), [SMEM] * 4 + [HB...  4.42 us
  transfers between devices with their start and end apart: 10, of which 5 were waited for; matrix products, arithmetic and copies ran while one was open for 1% of the time, Pallas kernels for 12%

profile of v5, /device:TPU:0, one launch (start us, length us, event | category | flops | bytes accessed | tf_op | source)
XLA Modules:
  0.0 144.9 jit_solution(2580407957388144291)
XLA Ops:
  0.0 4.4 %shard_map.64 = (bf16[1,1168,512]{2,1,0:T(8,128)(2,1)}, bf16[1,384,512]{2,1,0:T(8,128)(2,1)}, s32[16]{0:T(128)}) custom-call(s32[31]{0:T(128)} %bitcast.29, s32[31]{0:T(128)} %bitcast.31, s32[31]{0:T(128)} %bitcast.33, s32[31]{0:T(128)} %bitcast.35, s32[31,96,512]{2,1,0:T(8,128)} %bitcast.26), custom_call_target="tpu_custom_call" | custom-call | bytes 4718592 | tf_op jit(solution)/shard_map/pallas_call | solution.py:497
  4.4 3.0 %collective-permute-start.4 = (bf16[1,1168,512]{2,1,0:T(8,128)(2,1)}, bf16[1,1168,512]{2,1,0:T(8,128)(2,1)}, u32[]{:S(2)}, u32[]{:S(2)}) collective-permute-start(bf16[1,1168,512]{2,1,0:T(8,128)(2,1)} %get-tuple-element.41.refs_0_), channel_id=1, source_target_pairs={{0,16},{16,0},{1,17},{17,1},{2,18},{18,2},{3,19},{19,3},{4,20},{20... | collective-permute-start | bytes 3588104 | tf_op jit(solution)/shard_map/ppermute | solution.py:480
  7.4 8.4 %shard_map.65 = (f32[8,96,256]{2,1,0:T(8,128)S(1)}, bf16[8,96,256]{2,1,0:T(8,128)(2,1)S(1)}, bf16[1552,512]{1,0:T(8,128)(2,1)}, s32[16]{0:T(128)}) custom-call(s32[31]{0:T(128)} %bitcast.30, s32[31]{0:T(128)} %bitcast.32, s32[31]{0:T(128)} %bitcast.34, s32[31]{0:T(128)} %bitcast.36, s32[16]{0:T(128)} %get-tuple-element.40.out_label, ...), custom_call_target="tpu_custom_call" | custom-call | flops 1610612736 | bytes 12189696 | tf_op jit(solution)/shard_map/pallas_call | solution.py:518
  15.8 0.0 copy-start.4
  15.8 0.0 copy-start.5
  15.8 0.1 collective-permute-start
  15.9 0.5 collective-permute-start.3
  16.4 1.2 collective-permute-done
  17.6 0.0 copy-start.3
  17.6 0.8 add_convert_fusion
  18.4 5.9 %all-to-all-start = ((bf16[8,96,256]{2,1,0:T(8,128)(2,1)}), bf16[8,96,256]{2,1,0:T(8,128)(2,1)S(1)}, u32[]{:S(2)}, u32[]{:S(2)}) async-start(bf16[8,96,256]{2,1,0:T(8,128)(2,1)} %add_convert_fusion), calls=%async_computation | async-start | bytes 786432 | tf_op jit(solution)/shard_map/all_to_all | solution.py:490
  24.3 9.7 %collective-permute-done.4.refs_0_ = bf16[1,1168,512]{2,1,0:T(8,128)(2,1)} collective-permute-done((bf16[1,1168,512]{2,1,0:T(8,128)(2,1)}, bf16[1,1168,512]{2,1,0:T(8,128)(2,1)}, u32[]{:S(2)}, u32[]{:S(2)}) %collective-permute-start.4) | collective-permute-done | bytes 1196064 | tf_op jit(solution)/shard_map/ppermute | solution.py:480
  34.0 0.0 collective-permute-start.5
  34.0 0.0 copy-done.4
  34.0 0.5 collective-permute-start.6
  34.5 1.8 %all-to-all-done = bf16[8,96,256]{2,1,0:T(8,128)(2,1)S(1)} async-done(((bf16[8,96,256]{2,1,0:T(8,128)(2,1)}), bf16[8,96,256]{2,1,0:T(8,128)(2,1)S(1)}, u32[]{:S(2)}, u32[]{:S(2)}) %all-to-all-start) | async-done | bytes 393248 | tf_op jit(solution)/shard_map/all_to_all | solution.py:490
  36.3 0.1 convert_reduce_fusion
  36.4 0.7 collective-permute-start.2
  37.0 0.0 copy-done.5
  37.0 1.4 collective-permute-start.1
  38.5 2.6 %collective-permute-done.2.refs_1_ = f32[48,256]{1,0:T(8,128)S(1)} collective-permute-done((f32[48,256]{1,0:T(8,128)S(1)}, f32[48,256]{1,0:T(8,128)S(1)}, u32[]{:S(2)}, u32[]{:S(2)}) %collective-permute-start.2) | collective-permute-done | bytes 49184 | tf_op jit(solution)/shard_map/ppermute | solution.py:480
  41.1 0.7 shard_map.66
  41.8 4.0 %all-to-all-start.1 = ((bf16[8,48,256]{2,1,0:T(8,128)(2,1)}), bf16[8,48,256]{2,1,0:T(8,128)(2,1)S(1)}, u32[]{:S(2)}, u32[]{:S(2)}) async-start(bf16[8,48,256]{2,1,0:T(8,128)(2,1)} %get-tuple-element.46), calls=%async_computation.1 | async-start | bytes 393216 | tf_op jit(solution)/shard_map/all_to_all | solution.py:490
  45.8 0.0 collective-permute-done.6.refs_3_
  45.8 0.0 collective-permute-done.3.pair_tiles
  45.8 0.0 collective-permute-done.5.refs_1_
  45.8 0.0 copy-done.3
  45.8 6.4 %shard_map.67 = (bf16[4,384,512]{2,1,0:T(8,128)(2,1)S(1)}, bf16[4,384,512]{2,1,0:T(8,128)(2,1)}, bf16[4096,256]{1,0:T(8,128)(2,1)S(1)}, s32[8,128]{1,0:T(8,128)S(1)}) custom-call(s32[16]{0:T(128)S(1)} %copy-done.3, bf16[1552,512]{1,0:T(8,128)(2,1)} %get-tuple-element.48.tiles, bf16[1552,512]{1,0:T(8,128)(2,1)} %collective-permute-done.3.pair_tiles, ...), custom_call_target="tpu_custom_call" | custom-call | bytes 3145728 | tf_op jit(solution)/shard_map/pallas_call | solution.py:563
  52.2 0.0 copy-start
  52.2 1.2 copy-done
  53.4 0.0 collective-permute-done.1.late
  53.4 0.2 all-to-all-done.1
  53.6 0.0 collective-permute-start.7
  53.6 0.0 copy-start.1
  53.6 1.4 copy-done.1
  55.0 0.0 copy-start.2
  55.0 2.2 %shard_map.68 = (bf16[4,384,512]{2,1,0:T(8,128)(2,1)S(1)}, f32[384,256]{1,0:T(8,128)S(1)}, f32[384,128]{1,0:T(8,128)S(1)}) custom-call(s32[8,128]{1,0:T(8,128)S(1)} %get-tuple-element.50.labels, bf16[384,256]{1,0:T(8,128)(2,1)S(1)} %bitcast.18, bf16[4,384,512]{2,1,0:T(8,128)(2,1)S(1)} %copy-done.1, bf16[1,384,512]{2,1,0:T(8,128)(2,1)S(1)} %collective-permute-done.1.late, ...), custom_call_target="tpu_custom_call" | custom-call | flops 805306368 | bytes 5242880 | tf_op jit(solution)/shard_map/pallas_call | solution.py:598
  57.2 0.0 collective-permute-done.7.late
  57.2 0.0 copy-done.2
  57.2 2.3 %shard_map.69 = (bf16[384,256]{1,0:T(8,128)(2,1)S(1)}, bf16[4,384,512]{2,1,0:T(8,128)(2,1)S(1)}, f32[384,128]{1,0:T(8,128)S(1)}) custom-call(s32[8,128]{1,0:T(8,128)S(1)} %get-tuple-element.50.labels, bf16[384,256]{1,0:T(8,128)(2,1)S(1)} %bitcast.19, bf16[4,384,512]{2,1,0:T(8,128)(2,1)S(1)} %copy-done.2, ...), custom_call_target="tpu_custom_call" | custom-call | flops 805306368 | bytes 5242880 | tf_op jit(solution)/shard_map/pallas_call | solution.py:607
  59.5 14.3 %all_to_all.45.got = bf16[8,48,256]{2,1,0:T(8,128)(2,1)S(1)} all-to-all(bf16[8,48,256]{2,1,0:T(8,128)(2,1)S(1)} %bitcast.21), channel_id=1, replica_groups={{0,2,4,6,8,10,12,14},{1,3,5,7,9,11,13,15},{16,18,20,22,24,26,28,30},{17..., dimensions={0} | all-to-all | bytes 393216 | tf_op jit(solution)/shard_map/all_to_all | solution.py:490
  73.9 0.2 shard_map.70
  74.1 11.0 %all_to_all.46 = bf16[8,48,256]{2,1,0:T(8,128)(2,1)S(1)} all-to-all(bf16[8,48,256]{2,1,0:T(8,128)(2,1)S(1)} %get-tuple-element.60), channel_id=1, replica_groups={{0,2,4,6,8,10,12,14},{1,3,5,7,9,11,13,15},{16,18,20,22,24,26,28,30},{17..., dimensions={0} | all-to-all | bytes 393216 | tf_op jit(solution)/shard_map/all_to_all | solution.py:490
  85.0 2.0 %shard_map.71 = bf16[384,256]{1,0:T(8,128)(2,1)S(1)} custom-call(bf16[384,256]{1,0:T(8,128)(2,1)S(1)} %bitcast.22, f32[384,128]{1,0:T(8,128)S(1)} %get-tuple-element.61.reg, bf16[4,384,512]{2,1,0:T(8,128)(2,1)S(1)} %get-tuple-element.62.plays, bf16[4,384,512]{2,1,0:T(8,128)(2,1)S(1)} %get-tuple-element.63.pair_plays, ...), custom_call_target="tpu_custom_call" | custom-call | flops 1610612736 | bytes 5242880 | tf_op jit(solution)/shard_map/pallas_call | solution.py:617
  87.0 10.7 %all_to_all.47.got = bf16[8,48,256]{2,1,0:T(8,128)(2,1)S(1)} all-to-all(bf16[8,48,256]{2,1,0:T(8,128)(2,1)S(1)} %bitcast.23), channel_id=1, replica_groups={{0,2,4,6,8,10,12,14},{1,3,5,7,9,11,13,15},{16,18,20,22,24,26,28,30},{17..., dimensions={0} | all-to-all | bytes 393216 | tf_op jit(solution)/shard_map/all_to_all | solution.py:490
  97.7 0.2 shard_map.72
  97.9 10.6 %all_to_all.48 = bf16[8,48,256]{2,1,0:T(8,128)(2,1)S(1)} all-to-all(bf16[8,48,256]{2,1,0:T(8,128)(2,1)S(1)} %get-tuple-element.67), channel_id=1, replica_groups={{0,2,4,6,8,10,12,14},{1,3,5,7,9,11,13,15},{16,18,20,22,24,26,28,30},{17..., dimensions={0} | all-to-all | bytes 393216 | tf_op jit(solution)/shard_map/all_to_all | solution.py:490
  108.6 2.0 %shard_map.73 = bf16[384,256]{1,0:T(8,128)(2,1)S(1)} custom-call(bf16[384,256]{1,0:T(8,128)(2,1)S(1)} %bitcast.24, f32[384,128]{1,0:T(8,128)S(1)} %get-tuple-element.61.reg, bf16[4,384,512]{2,1,0:T(8,128)(2,1)S(1)} %get-tuple-element.62.plays, bf16[4,384,512]{2,1,0:T(8,128)(2,1)S(1)} %get-tuple-element.63.pair_plays, ...), custom_call_target="tpu_custom_call" | custom-call | flops 1610612736 | bytes 5242880 | tf_op jit(solution)/shard_map/pallas_call | solution.py:617
  110.5 10.5 %all_to_all.49.got = bf16[8,48,256]{2,1,0:T(8,128)(2,1)S(1)} all-to-all(bf16[8,48,256]{2,1,0:T(8,128)(2,1)S(1)} %bitcast.25), channel_id=1, replica_groups={{0,2,4,6,8,10,12,14},{1,3,5,7,9,11,13,15},{16,18,20,22,24,26,28,30},{17..., dimensions={0} | all-to-all | bytes 393216 | tf_op jit(solution)/shard_map/all_to_all | solution.py:490
  121.0 0.4 shard_map.74
  121.4 10.2 %all_to_all.50 = bf16[8,48,256]{2,1,0:T(8,128)(2,1)S(1)} all-to-all(bf16[8,48,256]{2,1,0:T(8,128)(2,1)S(1)} %get-tuple-element.71), channel_id=1, replica_groups={{0,2,4,6,8,10,12,14},{1,3,5,7,9,11,13,15},{16,18,20,22,24,26,28,30},{17..., dimensions={0} | all-to-all | bytes 393216 | tf_op jit(solution)/shard_map/all_to_all | solution.py:490
  131.6 1.8 %shard_map.75 = f32[16,16,128]{2,1,0:T(8,128)S(1)} custom-call(bf16[384,256]{1,0:T(8,128)(2,1)S(1)} %bitcast.20, f32[384,128]{1,0:T(8,128)S(1)} %get-tuple-element.61.reg, f32[16,16,128]{2,1,0:T(8,128)S(1)} %get-tuple-element.72.base, bf16[4,384,512]{2,1,0:T(8,128)(2,1)S(1)} %get-tuple-element.62.plays, ...), custom_call_target="tpu_custom_call" | custom-call | flops 805306368 | bytes 5242880 | tf_op jit(solution)/shard_map/pallas_call | solution.py:641
  133.4 10.5 %all_to_all.51.got = f32[16,16,128]{2,1,0:T(8,128)S(1)} all-to-all(f32[16,16,128]{2,1,0:T(8,128)S(1)} %shard_map.75), channel_id=1, replica_groups=mesh['user'=2,'item'=16] {'item'}, dimensions={0} | all-to-all | bytes 262144 | tf_op jit(solution)/shard_map/all_to_all | solution.py:650
  143.9 1.0 shard_map.76
  (1 shorter events, 0.0 us)
Async XLA Ops:
  4.4 29.6 %collective-permute-start.4 = (bf16[1,1168,512]{2,1,0:T(8,128)(2,1)}, bf16[1,1168,512]{2,1,0:T(8,128)(2,1)}, u32[]{:S(2)}, u32[]{:S(2)}) collective-permute-start(bf16[1,1168,512]{2,1,0:T(8,128)(2,1)} %get-tuple-element.41.refs_0_), channel_id=1, source_target_pairs={{0,16},{16,0},{1,17},{17,1},{2,18},{18,2},{3,19},{19,3},{4,20},{20... | collective-permute-start | bytes 3588104 | tf_op jit(solution)/shard_map/ppermute | solution.py:480
  15.8 18.2 %copy-start.4 = (bf16[2048,256]{1,0:T(8,128)(2,1)S(1)}, bf16[2048,256]{1,0:T(8,128)(2,1)}, u32[]{:S(2)}) copy-start(bf16[2048,256]{1,0:T(8,128)(2,1)} %refs_2_.3) | copy-start | bytes 3145732
  15.8 21.2 %copy-start.5 = (bf16[1,384,512]{2,1,0:T(8,128)(2,1)S(1)}, bf16[1,384,512]{2,1,0:T(8,128)(2,1)}, u32[]{:S(2)}) copy-start(bf16[1,384,512]{2,1,0:T(8,128)(2,1)} %get-tuple-element.44.refs_1_) | copy-start | bytes 1179652
  15.8 1.8 %collective-permute-start = (bf16[8,96,256]{2,1,0:T(8,128)(2,1)S(1)}, bf16[8,96,256]{2,1,0:T(8,128)(2,1)S(1)}, u32[]{:S(2)}, u32[]{:S(2)}) collective-permute-start(bf16[8,96,256]{2,1,0:T(8,128)(2,1)S(1)} %get-tuple-element.43), channel_id=1, source_target_pairs={{0,1},{1,0},{2,3},{3,2},{4,5},{5,4},{6,7},{7,6},{8,9},{9,8},{10,11... | collective-permute-start | bytes 1179656 | tf_op jit(solution)/shard_map/ppermute | solution.py:487
  15.9 29.9 %collective-permute-start.3 = (bf16[1552,512]{1,0:T(8,128)(2,1)}, bf16[1552,512]{1,0:T(8,128)(2,1)}, u32[]{:S(2)}, u32[]{:S(2)}) collective-permute-start(bf16[1552,512]{1,0:T(8,128)(2,1)} %get-tuple-element.48.tiles), channel_id=1, source_target_pairs={{0,1},{1,0},{2,3},{3,2},{4,5},{5,4},{6,7},{7,6},{8,9},{9,8},{10,11... | collective-permute-start | bytes 4767752 | tf_op jit(solution)/shard_map/ppermute | solution.py:487
  17.6 28.2 %copy-start.3 = (s32[16]{0:T(128)S(1)}, s32[16]{0:T(128)}, u32[]{:S(2)}) copy-start(s32[16]{0:T(128)} %get-tuple-element.47.own_label) | copy-start | bytes 196
  18.4 17.9 %all-to-all-start = ((bf16[8,96,256]{2,1,0:T(8,128)(2,1)}), bf16[8,96,256]{2,1,0:T(8,128)(2,1)S(1)}, u32[]{:S(2)}, u32[]{:S(2)}) async-start(bf16[8,96,256]{2,1,0:T(8,128)(2,1)} %add_convert_fusion), calls=%async_computation | async-start | bytes 786432 | tf_op jit(solution)/shard_map/all_to_all | solution.py:490
  34.0 11.8 %collective-permute-start.5 = (bf16[1,1168,512]{2,1,0:T(8,128)(2,1)}, bf16[1,1168,512]{2,1,0:T(8,128)(2,1)}, u32[]{:S(2)}, u32[]{:S(2)}) collective-permute-start(bf16[1,1168,512]{2,1,0:T(8,128)(2,1)} %collective-permute-done.4.refs_0_), channel_id=1, source_target_pairs={{0,1},{1,0},{2,3},{3,2},{4,5},{5,4},{6,7},{7,6},{8,9},{9,8},{10,11... | collective-permute-start | bytes 3588104 | tf_op jit(solution)/shard_map/ppermute | solution.py:487
  34.0 11.8 %collective-permute-start.6 = (bf16[2048,256]{1,0:T(8,128)(2,1)S(1)}, bf16[2048,256]{1,0:T(8,128)(2,1)}, u32[]{:S(2)}, u32[]{:S(2)}) collective-permute-start(bf16[2048,256]{1,0:T(8,128)(2,1)S(1)} %copy-done.4), channel_id=1, source_target_pairs={{0,1},{1,0},{2,3},{3,2},{4,5},{5,4},{6,7},{7,6},{8,9},{9,8},{10,11... | collective-permute-start | bytes 3145736 | tf_op jit(solution)/shard_map/ppermute | solution.py:487
  36.4 4.7 %collective-permute-start.2 = (f32[48,256]{1,0:T(8,128)S(1)}, f32[48,256]{1,0:T(8,128)S(1)}, u32[]{:S(2)}, u32[]{:S(2)}) collective-permute-start(f32[48,256]{1,0:T(8,128)S(1)} %get-tuple-element.73), channel_id=1, source_target_pairs={{0,16},{16,0},{1,17},{17,1},{2,18},{18,2},{3,19},{19,3},{4,20},{20... | collective-permute-start | bytes 147464 | tf_op jit(solution)/shard_map/ppermute | solution.py:480
  37.0 16.3 %collective-permute-start.1 = (bf16[1,384,512]{2,1,0:T(8,128)(2,1)S(1)}, bf16[1,384,512]{2,1,0:T(8,128)(2,1)S(1)}, u32[]{:S(2)}, u32[]{:S(2)}) collective-permute-start(bf16[1,384,512]{2,1,0:T(8,128)(2,1)S(1)} %copy-done.5), channel_id=1, source_target_pairs={{0,16},{16,0},{1,17},{17,1},{2,18},{18,2},{3,19},{19,3},{4,20},{20... | collective-permute-start | bytes 1179656 | tf_op jit(solution)/shard_map/ppermute | solution.py:480
  41.8 11.8 %all-to-all-start.1 = ((bf16[8,48,256]{2,1,0:T(8,128)(2,1)}), bf16[8,48,256]{2,1,0:T(8,128)(2,1)S(1)}, u32[]{:S(2)}, u32[]{:S(2)}) async-start(bf16[8,48,256]{2,1,0:T(8,128)(2,1)} %get-tuple-element.46), calls=%async_computation.1 | async-start | bytes 393216 | tf_op jit(solution)/shard_map/all_to_all | solution.py:490
  52.2 1.2 copy-start
  53.6 3.6 %collective-permute-start.7 = (bf16[1,384,512]{2,1,0:T(8,128)(2,1)S(1)}, bf16[1,384,512]{2,1,0:T(8,128)(2,1)S(1)}, u32[]{:S(2)}, u32[]{:S(2)}) collective-permute-start(bf16[1,384,512]{2,1,0:T(8,128)(2,1)S(1)} %collective-permute-done.1.late), channel_id=1, source_target_pairs={{0,1},{1,0},{2,3},{3,2},{4,5},{5,4},{6,7},{7,6},{8,9},{9,8},{10,11... | collective-permute-start | bytes 1179656 | tf_op jit(solution)/shard_map/ppermute | solution.py:487
  53.6 1.4 copy-start.1
  55.0 2.2 %copy-start.2 = (bf16[4,384,512]{2,1,0:T(8,128)(2,1)S(1)}, bf16[4,384,512]{2,1,0:T(8,128)(2,1)}, u32[]{:S(2)}) copy-start(bf16[4,384,512]{2,1,0:T(8,128)(2,1)} %get-tuple-element.52.placed) | copy-start | bytes 4718596

commit v6 on v5

--- a/solution.py
+++ b/solution.py
@@ -121,7 +121,6 @@
     n = len(sizes)
     parts, (factors, keep, send, tiles, label), bufs = refs[:n], refs[n : n + 5], refs[n + 5 : n + 5 + n]
     slots, fill, buf, logs, dense, items, sems, out_sems, part_sems, item_sem = refs[n + 5 + n :]
-    start_tiles(n_user, cap, True, owner, cell, counts, label, slots, fill, buf, sems)
     height, width = counts.shape[1], counts.shape[2]
     half = HG * height
     core = this_half()
@@ -131,6 +130,7 @@
     ]
     for move in moves:
         move.start()
+    start_tiles(n_user, cap, True, owner, cell, counts, label, slots, fill, buf, sems)
     item_copy = pltpu.make_async_copy(factors, items, item_sem)
     item_copy.start()
     dense[...] = jnp.zeros_like(dense)

time: 146 us -> 145 us (level)
  transfers between devices with their start and end apart: 10 -> 10, of which waited for: 5 -> 5; matrix products, arithmetic and copies ran while one was open for 1% -> 1% of each run, Pallas kernels for 12% -> 11%
where the time goes in v6:
time: 145 us
  blocking collectives  77.8 us (54%)
  Pallas kernels  30.7 us (21%)
  starting transfers between devices  17.2 us (12%)
  waiting for transfers between devices  15.4 us (11%)
  local copies, waits for them, and re-layouts  2.6 us (2%)
    all_to_all x6, blocking collectives, exchange(): return lax.all_to_all(x, 'item', 0, 0, axis_index_groups=groups, tiled=True)  67.3 us
    ppermute x3, waiting for transfers between devices, over_users(): lax.ppermute(x, 'user', [(u, (u + shift) % n_user) for u in range(n_user)])  13.4 us
    all_to_all x2, starting transfers between devices, exchange(): return lax.all_to_all(x, 'item', 0, 0, axis_index_groups=groups, tiled=True)  11 us
    all_to_all x1, blocking collectives, shards(): got = lax.all_to_all(payload, 'item', 0, 0, tiled=True)  10.5 us
    pallas_call x1, Pallas kernels, shards(): call(functools.partial(rhs_kernel, n_user, cap, sizes), [SMEM] * 5 + [HBM...  7.27 us
    pallas_call x1, Pallas kernels, shards(): call(functools.partial(place_kernel, cap, sizes), [SMEM] + [HBM] * (2 + 2...  6.41 us
    ppermute x3, starting transfers between devices, over_users(): lax.ppermute(x, 'user', [(u, (u + shift) % n_user) for u in range(n_user)])  5.06 us
    pallas_call x1, Pallas kernels, shards(): call(functools.partial(pack_kernel, n_user, cap, sizes), [SMEM] * 4 + [HB...  4.39 us
  transfers between devices with their start and end apart: 10, of which 5 were waited for; matrix products, arithmetic and copies ran while one was open for 1% of the time, Pallas kernels for 11%

profile of v6, /device:TPU:0, one launch (start us, length us, event | category | flops | bytes accessed | tf_op | source)
XLA Modules:
  0.0 144.8 jit_solution(12334089212074208799)
XLA Ops:
  0.0 4.4 %shard_map.64 = (bf16[1,1168,512]{2,1,0:T(8,128)(2,1)}, bf16[1,384,512]{2,1,0:T(8,128)(2,1)}, s32[16]{0:T(128)}) custom-call(s32[31]{0:T(128)} %bitcast.29, s32[31]{0:T(128)} %bitcast.31, s32[31]{0:T(128)} %bitcast.33, s32[31]{0:T(128)} %bitcast.35, s32[31,96,512]{2,1,0:T(8,128)} %bitcast.26), custom_call_target="tpu_custom_call" | custom-call | bytes 4718592 | tf_op jit(solution)/shard_map/pallas_call | solution.py:497
  4.4 3.0 %collective-permute-start.4 = (bf16[1,1168,512]{2,1,0:T(8,128)(2,1)}, bf16[1,1168,512]{2,1,0:T(8,128)(2,1)}, u32[]{:S(2)}, u32[]{:S(2)}) collective-permute-start(bf16[1,1168,512]{2,1,0:T(8,128)(2,1)} %get-tuple-element.41.refs_0_), channel_id=1, source_target_pairs={{0,16},{16,0},{1,17},{17,1},{2,18},{18,2},{3,19},{19,3},{4,20},{20... | collective-permute-start | bytes 3588104 | tf_op jit(solution)/shard_map/ppermute | solution.py:480
  7.4 7.3 %shard_map.65 = (f32[8,96,256]{2,1,0:T(8,128)S(1)}, bf16[8,96,256]{2,1,0:T(8,128)(2,1)S(1)}, bf16[1552,512]{1,0:T(8,128)(2,1)}, s32[16]{0:T(128)}) custom-call(s32[31]{0:T(128)} %bitcast.30, s32[31]{0:T(128)} %bitcast.32, s32[31]{0:T(128)} %bitcast.34, s32[31]{0:T(128)} %bitcast.36, s32[16]{0:T(128)} %get-tuple-element.40.out_label, ...), custom_call_target="tpu_custom_call" | custom-call | flops 1610612736 | bytes 12189696 | tf_op jit(solution)/shard_map/pallas_call | solution.py:518
  14.6 0.0 copy-start.4
  14.7 0.0 copy-start.5
  14.7 0.1 collective-permute-start
  14.7 0.5 collective-permute-start.3
  15.2 1.2 collective-permute-done
  16.5 0.0 copy-start.3
  16.5 0.8 add_convert_fusion
  17.3 5.9 %all-to-all-start = ((bf16[8,96,256]{2,1,0:T(8,128)(2,1)}), bf16[8,96,256]{2,1,0:T(8,128)(2,1)S(1)}, u32[]{:S(2)}, u32[]{:S(2)}) async-start(bf16[8,96,256]{2,1,0:T(8,128)(2,1)} %add_convert_fusion), calls=%async_computation | async-start | bytes 786432 | tf_op jit(solution)/shard_map/all_to_all | solution.py:490
  23.2 10.8 %collective-permute-done.4.refs_0_ = bf16[1,1168,512]{2,1,0:T(8,128)(2,1)} collective-permute-done((bf16[1,1168,512]{2,1,0:T(8,128)(2,1)}, bf16[1,1168,512]{2,1,0:T(8,128)(2,1)}, u32[]{:S(2)}, u32[]{:S(2)}) %collective-permute-start.4) | collective-permute-done | bytes 1196064 | tf_op jit(solution)/shard_map/ppermute | solution.py:480
  34.1 0.0 collective-permute-start.5
  34.1 0.0 copy-done.4
  34.1 0.5 collective-permute-start.6
  34.6 0.7 all-to-all-done
  35.2 0.1 convert_reduce_fusion
  35.3 1.1 collective-permute-start.2
  36.4 0.0 copy-done.5
  36.5 0.9 collective-permute-start.1
  37.4 2.6 %collective-permute-done.2.refs_1_ = f32[48,256]{1,0:T(8,128)S(1)} collective-permute-done((f32[48,256]{1,0:T(8,128)S(1)}, f32[48,256]{1,0:T(8,128)S(1)}, u32[]{:S(2)}, u32[]{:S(2)}) %collective-permute-start.2) | collective-permute-done | bytes 49184 | tf_op jit(solution)/shard_map/ppermute | solution.py:480
  40.0 0.7 shard_map.66
  40.7 5.1 %all-to-all-start.1 = ((bf16[8,48,256]{2,1,0:T(8,128)(2,1)}), bf16[8,48,256]{2,1,0:T(8,128)(2,1)S(1)}, u32[]{:S(2)}, u32[]{:S(2)}) async-start(bf16[8,48,256]{2,1,0:T(8,128)(2,1)} %get-tuple-element.46), calls=%async_computation.1 | async-start | bytes 393216 | tf_op jit(solution)/shard_map/all_to_all | solution.py:490
  45.8 0.0 collective-permute-done.6.refs_3_
  45.8 0.0 collective-permute-done.3.pair_tiles
  45.8 0.0 collective-permute-done.5.refs_1_
  45.8 0.0 copy-done.3
  45.8 6.4 %shard_map.67 = (bf16[4,384,512]{2,1,0:T(8,128)(2,1)S(1)}, bf16[4,384,512]{2,1,0:T(8,128)(2,1)}, bf16[4096,256]{1,0:T(8,128)(2,1)S(1)}, s32[8,128]{1,0:T(8,128)S(1)}) custom-call(s32[16]{0:T(128)S(1)} %copy-done.3, bf16[1552,512]{1,0:T(8,128)(2,1)} %get-tuple-element.48.tiles, bf16[1552,512]{1,0:T(8,128)(2,1)} %collective-permute-done.3.pair_tiles, ...), custom_call_target="tpu_custom_call" | custom-call | bytes 3145728 | tf_op jit(solution)/shard_map/pallas_call | solution.py:563
  52.2 0.0 copy-start
  52.2 1.2 copy-done
  53.4 0.0 collective-permute-done.1.late
  53.4 0.1 all-to-all-done.1
  53.6 0.0 collective-permute-start.7
  53.6 0.0 copy-start.1
  53.6 1.4 copy-done.1
  55.0 0.0 copy-start.2
  55.0 2.2 %shard_map.68 = (bf16[4,384,512]{2,1,0:T(8,128)(2,1)S(1)}, f32[384,256]{1,0:T(8,128)S(1)}, f32[384,128]{1,0:T(8,128)S(1)}) custom-call(s32[8,128]{1,0:T(8,128)S(1)} %get-tuple-element.50.labels, bf16[384,256]{1,0:T(8,128)(2,1)S(1)} %bitcast.18, bf16[4,384,512]{2,1,0:T(8,128)(2,1)S(1)} %copy-done.1, bf16[1,384,512]{2,1,0:T(8,128)(2,1)S(1)} %collective-permute-done.1.late, ...), custom_call_target="tpu_custom_call" | custom-call | flops 805306368 | bytes 5242880 | tf_op jit(solution)/shard_map/pallas_call | solution.py:598
  57.1 0.0 collective-permute-done.7.late
  57.2 0.0 copy-done.2
  57.2 2.3 %shard_map.69 = (bf16[384,256]{1,0:T(8,128)(2,1)S(1)}, bf16[4,384,512]{2,1,0:T(8,128)(2,1)S(1)}, f32[384,128]{1,0:T(8,128)S(1)}) custom-call(s32[8,128]{1,0:T(8,128)S(1)} %get-tuple-element.50.labels, bf16[384,256]{1,0:T(8,128)(2,1)S(1)} %bitcast.19, bf16[4,384,512]{2,1,0:T(8,128)(2,1)S(1)} %copy-done.2, ...), custom_call_target="tpu_custom_call" | custom-call | flops 805306368 | bytes 5242880 | tf_op jit(solution)/shard_map/pallas_call | solution.py:607
  59.5 14.3 %all_to_all.45.got = bf16[8,48,256]{2,1,0:T(8,128)(2,1)S(1)} all-to-all(bf16[8,48,256]{2,1,0:T(8,128)(2,1)S(1)} %bitcast.21), channel_id=1, replica_groups={{0,2,4,6,8,10,12,14},{1,3,5,7,9,11,13,15},{16,18,20,22,24,26,28,30},{17..., dimensions={0} | all-to-all | bytes 393216 | tf_op jit(solution)/shard_map/all_to_all | solution.py:490
  73.8 0.2 shard_map.70
  74.0 11.0 %all_to_all.46 = bf16[8,48,256]{2,1,0:T(8,128)(2,1)S(1)} all-to-all(bf16[8,48,256]{2,1,0:T(8,128)(2,1)S(1)} %get-tuple-element.60), channel_id=1, replica_groups={{0,2,4,6,8,10,12,14},{1,3,5,7,9,11,13,15},{16,18,20,22,24,26,28,30},{17..., dimensions={0} | all-to-all | bytes 393216 | tf_op jit(solution)/shard_map/all_to_all | solution.py:490
  84.9 2.0 %shard_map.71 = bf16[384,256]{1,0:T(8,128)(2,1)S(1)} custom-call(bf16[384,256]{1,0:T(8,128)(2,1)S(1)} %bitcast.22, f32[384,128]{1,0:T(8,128)S(1)} %get-tuple-element.61.reg, bf16[4,384,512]{2,1,0:T(8,128)(2,1)S(1)} %get-tuple-element.62.plays, bf16[4,384,512]{2,1,0:T(8,128)(2,1)S(1)} %get-tuple-element.63.pair_plays, ...), custom_call_target="tpu_custom_call" | custom-call | flops 1610612736 | bytes 5242880 | tf_op jit(solution)/shard_map/pallas_call | solution.py:617
  86.9 10.7 %all_to_all.47.got = bf16[8,48,256]{2,1,0:T(8,128)(2,1)S(1)} all-to-all(bf16[8,48,256]{2,1,0:T(8,128)(2,1)S(1)} %bitcast.23), channel_id=1, replica_groups={{0,2,4,6,8,10,12,14},{1,3,5,7,9,11,13,15},{16,18,20,22,24,26,28,30},{17..., dimensions={0} | all-to-all | bytes 393216 | tf_op jit(solution)/shard_map/all_to_all | solution.py:490
  97.6 0.2 shard_map.72
  97.8 10.6 %all_to_all.48 = bf16[8,48,256]{2,1,0:T(8,128)(2,1)S(1)} all-to-all(bf16[8,48,256]{2,1,0:T(8,128)(2,1)S(1)} %get-tuple-element.67), channel_id=1, replica_groups={{0,2,4,6,8,10,12,14},{1,3,5,7,9,11,13,15},{16,18,20,22,24,26,28,30},{17..., dimensions={0} | all-to-all | bytes 393216 | tf_op jit(solution)/shard_map/all_to_all | solution.py:490
  108.5 2.0 %shard_map.73 = bf16[384,256]{1,0:T(8,128)(2,1)S(1)} custom-call(bf16[384,256]{1,0:T(8,128)(2,1)S(1)} %bitcast.24, f32[384,128]{1,0:T(8,128)S(1)} %get-tuple-element.61.reg, bf16[4,384,512]{2,1,0:T(8,128)(2,1)S(1)} %get-tuple-element.62.plays, bf16[4,384,512]{2,1,0:T(8,128)(2,1)S(1)} %get-tuple-element.63.pair_plays, ...), custom_call_target="tpu_custom_call" | custom-call | flops 1610612736 | bytes 5242880 | tf_op jit(solution)/shard_map/pallas_call | solution.py:617
  110.4 10.5 %all_to_all.49.got = bf16[8,48,256]{2,1,0:T(8,128)(2,1)S(1)} all-to-all(bf16[8,48,256]{2,1,0:T(8,128)(2,1)S(1)} %bitcast.25), channel_id=1, replica_groups={{0,2,4,6,8,10,12,14},{1,3,5,7,9,11,13,15},{16,18,20,22,24,26,28,30},{17..., dimensions={0} | all-to-all | bytes 393216 | tf_op jit(solution)/shard_map/all_to_all | solution.py:490
  120.9 0.4 shard_map.74
  121.3 10.2 %all_to_all.50 = bf16[8,48,256]{2,1,0:T(8,128)(2,1)S(1)} all-to-all(bf16[8,48,256]{2,1,0:T(8,128)(2,1)S(1)} %get-tuple-element.71), channel_id=1, replica_groups={{0,2,4,6,8,10,12,14},{1,3,5,7,9,11,13,15},{16,18,20,22,24,26,28,30},{17..., dimensions={0} | all-to-all | bytes 393216 | tf_op jit(solution)/shard_map/all_to_all | solution.py:490
  131.5 1.8 %shard_map.75 = f32[16,16,128]{2,1,0:T(8,128)S(1)} custom-call(bf16[384,256]{1,0:T(8,128)(2,1)S(1)} %bitcast.20, f32[384,128]{1,0:T(8,128)S(1)} %get-tuple-element.61.reg, f32[16,16,128]{2,1,0:T(8,128)S(1)} %get-tuple-element.72.base, bf16[4,384,512]{2,1,0:T(8,128)(2,1)S(1)} %get-tuple-element.62.plays, ...), custom_call_target="tpu_custom_call" | custom-call | flops 805306368 | bytes 5242880 | tf_op jit(solution)/shard_map/pallas_call | solution.py:641
  133.3 10.5 %all_to_all.51.got = f32[16,16,128]{2,1,0:T(8,128)S(1)} all-to-all(f32[16,16,128]{2,1,0:T(8,128)S(1)} %shard_map.75), channel_id=1, replica_groups=mesh['user'=2,'item'=16] {'item'}, dimensions={0} | all-to-all | bytes 262144 | tf_op jit(solution)/shard_map/all_to_all | solution.py:650
  143.8 1.0 shard_map.76
  (1 shorter events, 0.0 us)
Async XLA Ops:
  4.4 29.7 %collective-permute-start.4 = (bf16[1,1168,512]{2,1,0:T(8,128)(2,1)}, bf16[1,1168,512]{2,1,0:T(8,128)(2,1)}, u32[]{:S(2)}, u32[]{:S(2)}) collective-permute-start(bf16[1,1168,512]{2,1,0:T(8,128)(2,1)} %get-tuple-element.41.refs_0_), channel_id=1, source_target_pairs={{0,16},{16,0},{1,17},{17,1},{2,18},{18,2},{3,19},{19,3},{4,20},{20... | collective-permute-start | bytes 3588104 | tf_op jit(solution)/shard_map/ppermute | solution.py:480
  14.6 19.4 %copy-start.4 = (bf16[2048,256]{1,0:T(8,128)(2,1)S(1)}, bf16[2048,256]{1,0:T(8,128)(2,1)}, u32[]{:S(2)}) copy-start(bf16[2048,256]{1,0:T(8,128)(2,1)} %refs_2_.3) | copy-start | bytes 3145732
  14.7 21.8 %copy-start.5 = (bf16[1,384,512]{2,1,0:T(8,128)(2,1)S(1)}, bf16[1,384,512]{2,1,0:T(8,128)(2,1)}, u32[]{:S(2)}) copy-start(bf16[1,384,512]{2,1,0:T(8,128)(2,1)} %get-tuple-element.44.refs_1_) | copy-start | bytes 1179652
  14.7 1.8 %collective-permute-start = (bf16[8,96,256]{2,1,0:T(8,128)(2,1)S(1)}, bf16[8,96,256]{2,1,0:T(8,128)(2,1)S(1)}, u32[]{:S(2)}, u32[]{:S(2)}) collective-permute-start(bf16[8,96,256]{2,1,0:T(8,128)(2,1)S(1)} %get-tuple-element.43), channel_id=1, source_target_pairs={{0,1},{1,0},{2,3},{3,2},{4,5},{5,4},{6,7},{7,6},{8,9},{9,8},{10,11... | collective-permute-start | bytes 1179656 | tf_op jit(solution)/shard_map/ppermute | solution.py:487
  14.7 31.0 %collective-permute-start.3 = (bf16[1552,512]{1,0:T(8,128)(2,1)}, bf16[1552,512]{1,0:T(8,128)(2,1)}, u32[]{:S(2)}, u32[]{:S(2)}) collective-permute-start(bf16[1552,512]{1,0:T(8,128)(2,1)} %get-tuple-element.48.tiles), channel_id=1, source_target_pairs={{0,1},{1,0},{2,3},{3,2},{4,5},{5,4},{6,7},{7,6},{8,9},{9,8},{10,11... | collective-permute-start | bytes 4767752 | tf_op jit(solution)/shard_map/ppermute | solution.py:487
  16.5 29.3 %copy-start.3 = (s32[16]{0:T(128)S(1)}, s32[16]{0:T(128)}, u32[]{:S(2)}) copy-start(s32[16]{0:T(128)} %get-tuple-element.47.own_label) | copy-start | bytes 196
  17.3 17.9 %all-to-all-start = ((bf16[8,96,256]{2,1,0:T(8,128)(2,1)}), bf16[8,96,256]{2,1,0:T(8,128)(2,1)S(1)}, u32[]{:S(2)}, u32[]{:S(2)}) async-start(bf16[8,96,256]{2,1,0:T(8,128)(2,1)} %add_convert_fusion), calls=%async_computation | async-start | bytes 786432 | tf_op jit(solution)/shard_map/all_to_all | solution.py:490
  34.1 11.7 %collective-permute-start.5 = (bf16[1,1168,512]{2,1,0:T(8,128)(2,1)}, bf16[1,1168,512]{2,1,0:T(8,128)(2,1)}, u32[]{:S(2)}, u32[]{:S(2)}) collective-permute-start(bf16[1,1168,512]{2,1,0:T(8,128)(2,1)} %collective-permute-done.4.refs_0_), channel_id=1, source_target_pairs={{0,1},{1,0},{2,3},{3,2},{4,5},{5,4},{6,7},{7,6},{8,9},{9,8},{10,11... | collective-permute-start | bytes 3588104 | tf_op jit(solution)/shard_map/ppermute | solution.py:487
  34.1 11.7 %collective-permute-start.6 = (bf16[2048,256]{1,0:T(8,128)(2,1)S(1)}, bf16[2048,256]{1,0:T(8,128)(2,1)}, u32[]{:S(2)}, u32[]{:S(2)}) collective-permute-start(bf16[2048,256]{1,0:T(8,128)(2,1)S(1)} %copy-done.4), channel_id=1, source_target_pairs={{0,1},{1,0},{2,3},{3,2},{4,5},{5,4},{6,7},{7,6},{8,9},{9,8},{10,11... | collective-permute-start | bytes 3145736 | tf_op jit(solution)/shard_map/ppermute | solution.py:487
  35.3 4.7 %collective-permute-start.2 = (f32[48,256]{1,0:T(8,128)S(1)}, f32[48,256]{1,0:T(8,128)S(1)}, u32[]{:S(2)}, u32[]{:S(2)}) collective-permute-start(f32[48,256]{1,0:T(8,128)S(1)} %get-tuple-element.73), channel_id=1, source_target_pairs={{0,16},{16,0},{1,17},{17,1},{2,18},{18,2},{3,19},{19,3},{4,20},{20... | collective-permute-start | bytes 147464 | tf_op jit(solution)/shard_map/ppermute | solution.py:480
  36.5 17.0 %collective-permute-start.1 = (bf16[1,384,512]{2,1,0:T(8,128)(2,1)S(1)}, bf16[1,384,512]{2,1,0:T(8,128)(2,1)S(1)}, u32[]{:S(2)}, u32[]{:S(2)}) collective-permute-start(bf16[1,384,512]{2,1,0:T(8,128)(2,1)S(1)} %copy-done.5), channel_id=1, source_target_pairs={{0,16},{16,0},{1,17},{17,1},{2,18},{18,2},{3,19},{19,3},{4,20},{20... | collective-permute-start | bytes 1179656 | tf_op jit(solution)/shard_map/ppermute | solution.py:480
  40.7 12.9 %all-to-all-start.1 = ((bf16[8,48,256]{2,1,0:T(8,128)(2,1)}), bf16[8,48,256]{2,1,0:T(8,128)(2,1)S(1)}, u32[]{:S(2)}, u32[]{:S(2)}) async-start(bf16[8,48,256]{2,1,0:T(8,128)(2,1)} %get-tuple-element.46), calls=%async_computation.1 | async-start | bytes 393216 | tf_op jit(solution)/shard_map/all_to_all | solution.py:490
  52.2 1.2 copy-start
  53.6 3.6 %collective-permute-start.7 = (bf16[1,384,512]{2,1,0:T(8,128)(2,1)S(1)}, bf16[1,384,512]{2,1,0:T(8,128)(2,1)S(1)}, u32[]{:S(2)}, u32[]{:S(2)}) collective-permute-start(bf16[1,384,512]{2,1,0:T(8,128)(2,1)S(1)} %collective-permute-done.1.late), channel_id=1, source_target_pairs={{0,1},{1,0},{2,3},{3,2},{4,5},{5,4},{6,7},{7,6},{8,9},{9,8},{10,11... | collective-permute-start | bytes 1179656 | tf_op jit(solution)/shard_map/ppermute | solution.py:487
  53.6 1.4 copy-start.1
  55.0 2.2 %copy-start.2 = (bf16[4,384,512]{2,1,0:T(8,128)(2,1)S(1)}, bf16[4,384,512]{2,1,0:T(8,128)(2,1)}, u32[]{:S(2)}) copy-start(bf16[4,384,512]{2,1,0:T(8,128)(2,1)} %get-tuple-element.52.placed) | copy-start | bytes 4718596
